TPU v7x, 32 devices: a whole 2x2x4 slice. The times are simulated.
32 devices in a mesh: seq: 4 (over y, x), chan: 8 (over z, core).
Axes of the slice: x: 2, y: 2, z: 4, core: 2. Of those that a mesh axis runs over, the one named last changes fastest.
Arguments:
- x_rows: bfloat16 [4096, 8192], P('seq'), may hold values from -6 to 6
- norm_gain: float32 [8192], replicated, may hold values from 0.1 to 1.9
- in_weight: bfloat16 [8192, 3, 8192], P('seq', None, 'chan'), may hold values from -0.0625 to 0.0625
- feat_filter: float32 [3, 3, 8192], P(None, None, 'chan'), may hold values from -3 to 3
- inner_filter: float32 [7, 8192], P(None, 'chan'), may hold values from -2.5 to 2.5
- out_weight: bfloat16 [8192, 8192], P('seq', 'chan'), may hold values from -0.0625 to 0.0625
Outputs:
- mixer_output: bfloat16 [4096, 8192], P(('seq', 'chan'))
All inputs are finite; a program needn't handle non-finite values.
Results may differ from a plain program's by a relative error of at most 0.0086.
Values may be sent and summed in bfloat16 or wider, within the bound.
No kernel may reach another device: no remote copies, remote signals or barrier semaphores. Data moves between devices by JAX's collectives and lax.ppermute only.
A program may use at most 192 MiB of HBM per device.

v0:
```python
import jax
import jax.numpy as jnp
from jax import lax
from jax.sharding import PartitionSpec as P

FEAT = 3
FILT = 7


def passed_along(block, axis, distance):
    devices = range(lax.axis_size(axis))
    route = [(i - distance, i) for i in devices if i - distance in devices]
    return lax.ppermute(block, axis, route)


def short_mix(extended, feat_filter, inner_filter, length):
    feat_taps = feat_filter.shape[0]
    inner_taps = inner_filter.shape[0]
    extent = length + inner_taps - 1
    offset = extended.shape[0] - extent
    featured = feat_filter[0] * extended[offset : offset + extent]
    for back_step in range(1, feat_taps):
        featured = (
            featured
            + feat_filter[back_step] * extended[offset - back_step : offset - back_step + extent]
        )
    product = featured[:, 1] * featured[:, 2]
    filtered = inner_filter[0] * product[inner_taps - 1 :]
    for back_step in range(1, inner_taps):
        filtered = (
            filtered
            + inner_filter[back_step]
            * product[inner_taps - 1 - back_step : inner_taps - 1 - back_step + length]
        )
    return (featured[inner_taps - 1 :, 0] * filtered).astype(jnp.bfloat16)


def per_device(x_rows, norm_gain, in_weight, feat_filter, inner_filter, out_weight):
    tokens_here = x_rows.shape[0]
    values = x_rows.astype(jnp.float32)
    squares = jnp.mean(values * values, axis=1, keepdims=True)
    normed = (values * lax.rsqrt(squares + 1e-06) * norm_gain).astype(jnp.bfloat16)
    local_cols = in_weight.shape[1] * in_weight.shape[2]
    panel = lax.all_gather(in_weight, "seq", axis=0, tiled=True)
    operand = normed
    flat_panel = panel.reshape(panel.shape[0], local_cols)
    accumulated = jnp.dot(operand, flat_panel, preferred_element_type=jnp.float32)
    projected = accumulated.astype(jnp.bfloat16).reshape(tokens_here, 3, in_weight.shape[2])
    history_rows = FEAT + FILT - 2
    last_rows = projected[tokens_here - history_rows :]
    previous = passed_along(last_rows, "seq", 1)
    extended = jnp.concatenate([previous, projected], axis=0).astype(jnp.float32)
    gated_values = short_mix(extended, feat_filter, inner_filter, tokens_here)
    gated_full = lax.all_gather(gated_values, "chan", axis=1, tiled=True)
    operand = gated_full
    out_cols = jnp.dot(
        operand,
        lax.all_gather(out_weight, "seq", axis=0, tiled=True),
        preferred_element_type=jnp.float32,
    )
    return lax.all_to_all(
        out_cols.astype(jnp.bfloat16), "chan", split_axis=0, concat_axis=1, tiled=True
    )


def solution(mesh):
    return jax.shard_map(
        per_device,
        mesh=mesh,
        in_specs=(
            P("seq", None),
            P(),
            P("seq", None, "chan"),
            P(None, None, "chan"),
            P(None, "chan"),
            P("seq", "chan"),
        ),
        out_specs=P(("seq", "chan"), None),
        check_vma=False,
    )
```

profile of v0, /device:TPU:0, one launch (start us, length us, event | category | flops | bytes accessed | tf_op | source)
XLA Modules:
  0.0 857.6 jit_solution(8396171314442653330)
XLA Ops:
  6.5 0.0 all-gather.4.cloned.1.call-start
  6.5 16.9 %copy.20 = bf16[2048,3,1024]{0,2,1:T(8,128)(2,1)} copy(bf16[2048,3,1024]{2,0,1:T(8,128)(2,1)} %param.8) | data formatting | bytes 25165824 | tf_op args[2]
  23.5 0.0 all-gather.4.cloned.1.call-update
  23.5 0.0 copy-start
  23.5 0.0 copy-start.2
  23.5 0.0 all-gather.8.cloned.1.call-start
  23.6 0.7 all-gather.8.cloned.1.call-update
  24.3 0.0 all-gather.6.cloned.1.call-start
  24.3 7.2 fusion
  31.5 0.0 copy-done
  31.6 431.8 %all-gather.4.cloned.1.call-done = bf16[8192,3,1024]{0,2,1:T(8,128)(2,1)} async-done(((bf16[2048,3,1024]{0,2,1:T(8,128)(2,1)}), bf16[8192,3,1024]{0,2,1:T(8,128)(2,1)}) %all-gather.4.cloned.1.call-update) | async-done | bytes 50331664 | tf_op jit(solution)/shard_map/all_gather | solution.py:44
  463.4 0.0 copy-done.2
  463.4 0.0 copy-start.1
  463.4 62.9 %fusion.9 = bf16[1024,3072]{1,0:T(8,128)(2,1)} fusion(bf16[8192,3072]{0,1:T(8,128)(2,1)} %bitcast.95, bf16[1024,8192]{1,0:T(8,128)(2,1)} %param.6, f32[8192]{0:T(1024)S(1)} %copy-done.2, f32[1024]{0:T(1024)S(1)} %add_rsqrt_fusion), kind=kOutput, calls=%fused_computation.14 | convolution fusion | flops 51576307712 | bytes 73437184 | tf_op jit(solution)/shard_map/dot_general | solution.py:47
  526.3 0.8 slice.128
  527.1 3.5 collective-permute-start
  530.7 0.0 copy-done.1
  530.7 9.0 %copy.21 = bf16[1024,3072]{0,1:T(8,128)(2,1)} copy(bf16[1024,3072]{1,0:T(8,128)(2,1)} %fusion.9) | data formatting | bytes 12582912 | tf_op jit(solution)/shard_map/convert_element_type | solution.py:48
  539.7 0.0 collective-permute-done
  539.7 0.4 copy.22
  540.1 11.0 %maximum_convert_fusion = f32[1032,3,1024]{0,2,1:T(8,128)} fusion(bf16[1024,3,1024]{0,2,1:T(8,128)(2,1)} %bitcast.84, bf16[8,3,1024]{0,2,1:T(8,128)(2,1)S(1)} %copy.22), kind=kLoop, calls=%fused_computation.13 | loop fusion | flops 12681216 | bytes 19021824 | tf_op jit(solution)/shard_map/convert_element_type | solution.py:52
  551.1 17.1 %fusion.7 = f32[1030,3,1024]{0,2,1:T(8,128)S(1)} fusion(f32[1032,3,1024]{0,2,1:T(8,128)} %maximum_convert_fusion, f32[3,1024]{1,0:T(4,128)S(1)} %get-tuple-element.6, f32[3,1024]{1,0:T(4,128)S(1)} %get-tuple-element.7, f32[3,1024]{1,0:T(4,128)S(1)} %get-tuple-element.5), kind=kLoop, calls=%fused_computation.9 | loop fusion | flops 15820800 | bytes 50663424 | tf_op jit(solution)/shard_map/add | solution.py:24
  568.2 0.5 slice_multiply_fusion.3
  568.7 10.4 %fusion.15 = bf16[1024,1024]{0,1:T(8,128)(2,1)} fusion(f32[1030,1,1024]{0,2,1:T(8,128)S(1)} %slice_multiply_fusion.3, f32[1030,3,1024]{0,2,1:T(8,128)S(1)} %fusion.7, f32[1024]{0:T(1024)S(1)} %bitcast.93, f32[1024]{0:T(1024)S(1)} %bitcast.94, f32[1024]{0:T(1024)S(1)} %bitcast.89, f32[1024]{0:T(1024)S(1)} %bitcast.90, f32[1024]{0:T(1024)S(1)} %bitcast.91, ...), kind=kLoop, calls=%fused_computation.20 | loop fusion | flops 15728640 | bytes 35680256 | tf_op jit(solution)/shard_map/convert_element_type | solution.py:35
  579.1 0.0 all-gather.6.cloned.1.call-update
  579.1 44.5 %all-gather.8.cloned.1.call-done = bf16[8192,1024]{1,0:T(8,128)(2,1)} async-done(((bf16[2048,1024]{1,0:T(8,128)(2,1)}), bf16[8192,1024]{1,0:T(8,128)(2,1)}) %all-gather.8.cloned.1.call-update) | async-done | bytes 16777232 | tf_op jit(solution)/shard_map/all_gather | solution.py:58
  623.6 152.3 %all-gather.6.cloned.1.call-done = bf16[1024,8192]{0,1:T(8,128)(2,1)} async-done(((bf16[1024,1024]{0,1:T(8,128)(2,1)}), bf16[1024,8192]{0,1:T(8,128)(2,1)}) %all-gather.6.cloned.1.call-update) | async-done | bytes 16777232 | tf_op jit(solution)/shard_map/all_gather | solution.py:54
  775.9 22.1 %convolution_convert_fusion = bf16[1024,1024]{1,0:T(8,128)(2,1)S(1)} fusion(bf16[1024,8192]{0,1:T(8,128)(2,1)} %all-gather.6.cloned.1.call-done, bf16[8192,1024]{1,0:T(8,128)(2,1)} %all-gather.8.cloned.1.call-done), kind=kOutput, calls=%fused_computation.39 | convolution fusion | flops 17180917760 | bytes 35651584 | tf_op jit(solution)/shard_map/dot_general | solution.py:56
  798.0 51.5 %all_to_all.19 = bf16[8,128,1024]{2,1,0:T(8,128)(2,1)S(1)} all-to-all(bf16[8,128,1024]{2,1,0:T(8,128)(2,1)S(1)} %bitcast.86), channel_id=1, replica_groups=mesh['seq'=4,'chan'=8] {'chan'}, dimensions={0} | all-to-all | bytes 4194304 | tf_op jit(solution)/shard_map/all_to_all | solution.py:61
  849.5 1.5 copy.24
  (3 shorter events, 0.0 us)
Async XLA Ops:
  6.5 456.8 %all-gather.4.cloned.1.call-start = ((), (), s32[]{:S(2)}) async-start(), calls=%async_computation.1 | async-start | bytes 62914560 | tf_op jit(solution)/shard_map/all_gather | solution.py:44
  23.5 8.0 copy-start
  23.5 439.9 %copy-start.2 = (f32[8192]{0:T(1024)S(1)}, f32[8192]{0:T(1024)}, u32[]{:S(2)}) copy-start(f32[8192]{0:T(1024)} %param.7) | copy-start | bytes 98308
  23.5 600.1 %all-gather.8.cloned.1.call-start = ((), (), s32[]{:S(2)}) async-start(), calls=%async_computation.3 | async-start | bytes 20971520 | tf_op jit(solution)/shard_map/all_gather | solution.py:58
  24.3 751.6 %all-gather.6.cloned.1.call-start = ((), (), s32[]{:S(2)}) async-start(), calls=%async_computation.2 | async-start | bytes 18874368 | tf_op jit(solution)/shard_map/all_gather | solution.py:54
  463.4 67.3 %copy-start.1 = (f32[7,1024]{1,0:T(8,128)S(1)}, f32[7,1024]{1,0:T(8,128)}, u32[]{:S(2)}) copy-start(f32[7,1024]{1,0:T(8,128)} %param.10) | copy-start | bytes 86020
  527.1 12.6 %collective-permute-start = (bf16[8,3,1024]{2,0,1:T(8,128)(2,1)S(1)}, bf16[8,3,1024]{2,0,1:T(8,128)(2,1)S(1)}, u32[]{:S(2)}, u32[]{:S(2)}) collective-permute-start(bf16[8,3,1024]{2,0,1:T(8,128)(2,1)S(1)} %bitcast.87), channel_id=1, source_target_pairs={{0,8},{8,16},{16,24},{1,9},{9,17},{17,25},{2,10},{10,18},{18,26},{... | collective-permute-start | bytes 147464 | tf_op jit(solution)/shard_map/ppermute | solution.py:13
Sparse Core Ops, SparseCore 0:
  23.6 439.6 all-gather.3
  465.2 158.3 all-gather.7
  625.2 150.6 all-gather.5
where the time goes:
time: 858 us
  waiting for transfers between devices  629 us (73%)
  matrix products  85.1 us (10%)
  blocking collectives  51.5 us (6%)
  other arithmetic  46.2 us (5%)
  local copies, waits for them, and re-layouts  28.7 us (3%)
  between operations  13.2 us (2%)
    all_gather x1, waiting for transfers between devices, per_device(): panel = lax.all_gather(in_weight, 'seq', axis=0, tiled=True)  432 us
    all_gather x1, waiting for transfers between devices, per_device(): gated_full = lax.all_gather(gated_values, 'chan', axis=1, tiled=True)  152 us
    dot_general x1, matrix products, per_device(): jnp.dot(operand, flat_panel, preferred_element_type=jnp.float32)  62.9 us
    all_to_all x1, blocking collectives, per_device(): lax.all_to_all(out_cols.astype(jnp.bfloat16), 'chan', split_axis=0, conca...  51.5 us
    all_gather x1, waiting for transfers between devices, per_device(): lax.all_gather(out_weight, 'seq', axis=0, tiled=True)  44.5 us
    dot_general x1, matrix products, per_device(): jnp.dot(operand, lax.all_gather(out_weight, 'seq', axis=0, tiled=True), p...  22.1 us
  transfers between devices with their start and end apart: 4, of which 3 were waited for; matrix products, arithmetic and copies ran while one was open for 14% of the time, Pallas kernels for 0%

commit v1 on v0

v1 whole, which is shorter than its diff:
```python
import functools

import jax
import jax.numpy as jnp
from jax import lax
from jax.experimental import pallas as pl
from jax.experimental.pallas import tpu as pltpu
from jax.sharding import PartitionSpec as P

HALO = 16
CHUNKS = 4
OUT_CHUNKS = 2
VMEM = 56 * 2**20


def project_kernel(count, extra, *refs):
    x_ref = refs[0]
    weights = refs[1 : 1 + count]
    received = refs[1 + count : 1 + count + extra]
    out_ref = refs[-1]
    depth = weights[0].shape[0]
    total = jnp.dot(x_ref[:, :depth], weights[0][...], preferred_element_type=jnp.float32)
    for i in range(1, count):
        total += jnp.dot(
            x_ref[:, i * depth : (i + 1) * depth],
            weights[i][...],
            preferred_element_type=jnp.float32,
        )
    for ref in received:
        total += ref[...].astype(jnp.float32)
    out_ref[...] = total.astype(out_ref.dtype)


def project(x, weights, received=()):
    rows, depth = x.shape
    columns = weights[0].shape[1]
    tile = min(rows, 256)
    whole = pl.BlockSpec(weights[0].shape, lambda i: (0, 0), pipeline_mode=pl.Buffered(1))
    return pl.pallas_call(
        functools.partial(project_kernel, len(weights), len(received)),
        grid=(rows // tile,),
        in_specs=[pl.BlockSpec((tile, depth), lambda i: (i, 0))]
        + [whole] * len(weights)
        + [pl.BlockSpec((tile, columns), lambda i: (i, 0))] * len(received),
        out_specs=pl.BlockSpec((tile, columns), lambda i: (i, 0)),
        out_shape=jax.ShapeDtypeStruct((rows, columns), jnp.bfloat16),
        compiler_params=pltpu.CompilerParams(vmem_limit_bytes=VMEM),
        cost_estimate=pl.CostEstimate(
            flops=2 * rows * depth * columns,
            bytes_accessed=2 * (rows * depth + depth * columns + (1 + len(received)) * rows * columns),
            transcendentals=0,
        ),
        name="project",
    )(x, *weights, *received)


def mix_kernel(feat, filt, qh, kh, vh, q, k, v, taps, out_ref, ext, prod):
    rows = q.shape[0]
    for i, (h, b) in enumerate(((qh, q), (kh, k), (vh, v))):
        ext[i, :HALO, :] = h[...].astype(jnp.float32)
        ext[i, HALO:, :] = b[...].astype(jnp.float32)
    tile = min(rows, 128)

    def featured(i, start, size):
        total = taps[i : i + 1, :] * ext[i, pl.ds(start, size), :]
        for j in range(1, feat):
            total += taps[3 * j + i : 3 * j + i + 1, :] * ext[i, pl.ds(start - j, size), :]
        return total

    for t in range(rows // tile):
        base = HALO + t * tile
        prod[...] = featured(1, base - 8, tile + 8) * featured(2, base - 8, tile + 8)
        total = taps[3 * feat : 3 * feat + 1, :] * prod[pl.ds(8, tile), :]
        for j in range(1, filt):
            total += taps[3 * feat + j : 3 * feat + j + 1, :] * prod[pl.ds(8 - j, tile), :]
        out_ref[t * tile : (t + 1) * tile, :] = (featured(0, base, tile) * total).astype(out_ref.dtype)


def short_mix(halo, projected, taps, feat, filt):
    rows, width = projected.shape[0], projected.shape[1] // 3
    lanes = 128
    steps = width // lanes

    def part(i, size):
        return pl.BlockSpec((size, lanes), lambda b: (0, i * steps + b))

    tile = min(rows, 128)
    return pl.pallas_call(
        functools.partial(mix_kernel, feat, filt),
        grid=(steps,),
        in_specs=[part(i, HALO) for i in range(3)]
        + [part(i, rows) for i in range(3)]
        + [pl.BlockSpec((taps.shape[0], lanes), lambda b: (0, b))],
        out_specs=pl.BlockSpec((rows, lanes), lambda b: (0, b)),
        out_shape=jax.ShapeDtypeStruct((rows, width), jnp.bfloat16),
        scratch_shapes=[
            pltpu.VMEM((3, HALO + rows, lanes), jnp.float32),
            pltpu.VMEM((tile + 8, lanes), jnp.float32),
        ],
        compiler_params=pltpu.CompilerParams(vmem_limit_bytes=VMEM),
        cost_estimate=pl.CostEstimate(
            flops=40 * rows * width, bytes_accessed=8 * rows * width, transcendentals=0
        ),
        name="short_mix",
    )(halo, halo, halo, projected, projected, projected, taps)


def out_kernel(blocks, parts, order, *refs):
    gated = refs[:parts]
    weights = refs[parts : parts + blocks]
    out_ref = refs[-1]
    width = gated[0].shape[2]
    per_block = weights[0].shape[0] // (width * parts)
    total = jnp.zeros(out_ref.shape, jnp.float32)
    for b in range(blocks):
        for i in range(per_block):
            for j in range(parts):
                row = (i * parts + j) * width
                total += jnp.dot(
                    gated[j][order[b] * per_block + i],
                    weights[b][row : row + width, :],
                    preferred_element_type=jnp.float32,
                )
    out_ref[...] = total.astype(out_ref.dtype)


def out_project(order, gated, weights):
    chans, rows, width = gated[0].shape
    depth, columns = weights[0].shape
    tile = min(rows, 256)
    spec = pltpu.PrefetchScalarGridSpec(
        num_scalar_prefetch=1,
        grid=(rows // tile,),
        in_specs=[pl.BlockSpec((chans, tile, width), lambda i, o: (0, i, 0))] * len(gated)
        + [pl.BlockSpec((depth, columns), lambda i, o: (0, 0), pipeline_mode=pl.Buffered(1))] * len(weights),
        out_specs=pl.BlockSpec((tile, columns), lambda i, o: (i, 0)),
    )
    total = depth * len(weights)
    return pl.pallas_call(
        functools.partial(out_kernel, len(weights), len(gated)),
        grid_spec=spec,
        out_shape=jax.ShapeDtypeStruct((rows, columns), jnp.bfloat16),
        compiler_params=pltpu.CompilerParams(vmem_limit_bytes=VMEM),
        cost_estimate=pl.CostEstimate(
            flops=2 * rows * total * columns,
            bytes_accessed=2 * (rows * total + total * columns + rows * columns),
            transcendentals=0,
        ),
        name="out_project",
    )(order, *gated, *weights)


def normalised(x, gain):
    values = x.astype(jnp.float32)
    squares = jnp.mean(values * values, axis=1, keepdims=True)
    return (values * lax.rsqrt(squares + 1e-06) * gain).astype(jnp.bfloat16)


def per_device(x_rows, norm_gain, in_weight, feat_filter, inner_filter, out_weight):
    tokens, model = x_rows.shape
    depth, _, chans_here = in_weight.shape
    seqs, chans = lax.axis_size("seq"), lax.axis_size("chan")
    near = 2 if seqs % 2 == 0 else 1
    far = seqs // near
    seq, chan = lax.axis_index("seq"), lax.axis_index("chan")
    e, g = seq // near, seq % near
    feat, filt = feat_filter.shape[0], inner_filter.shape[0]

    def from_near(block, k):
        pairs = [(a * near + (b + k) % near, a * near + b) for a in range(far) for b in range(near)]
        return lax.ppermute(block, "seq", pairs)

    def from_far(block, k):
        pairs = [((a + k) % far * near + b, a * near + b) for a in range(far) for b in range(near)]
        return lax.ppermute(block, "seq", pairs)

    def columns_of(rows, group):
        return jnp.concatenate(
            [
                lax.dynamic_slice_in_dim(rows, (group * near + (g + i) % near) * depth, depth, 1)
                for i in range(near)
            ],
            axis=1,
        )

    share = tokens // chans
    part = normalised(lax.dynamic_slice_in_dim(x_rows, chan * share, share, 0), norm_gain)
    theirs = []
    for k in range(1, far):
        piece = from_far(columns_of(part, (e - k) % far), k)
        full = lax.all_gather(piece, "chan", axis=0, tiled=True)
        theirs.append(full)
    mine = columns_of(normalised(x_rows, norm_gain), e)

    step = chans_here // CHUNKS
    taps = jnp.concatenate([feat_filter.reshape(feat * 3, chans_here), inner_filter], axis=0)
    gated = []
    for j in range(CHUNKS):
        cut = slice(j * step, (j + 1) * step)
        own = in_weight[:, :, cut].reshape(depth, 3 * step)
        weights = [own] + [from_near(own, k) for k in range(1, near)]
        sums = [
            from_far(project(theirs[k - 1], weights), far - k) for k in range(1, far)
        ]
        projected = project(mine, weights, sums)
        halo = lax.ppermute(
            projected[tokens - HALO :], "seq", [(i, i + 1) for i in range(seqs - 1)]
        )
        mixed = short_mix(halo, projected, taps[:, cut], feat, filt)
        gated.append(lax.all_gather(mixed, "chan", axis=0))

    order = jnp.stack(
        [(e + a) % far * near + (g + b) % near for a in range(far) for b in range(near)]
    ).astype(jnp.int32)
    width = out_weight.shape[1] // OUT_CHUNKS
    pieces = []
    for m in range(OUT_CHUNKS):
        own = out_weight[:, m * width : (m + 1) * width]
        row = [own] + [from_near(own, k) for k in range(1, near)]
        rows = row + [from_far(block, a) for a in range(1, far) for block in row]
        out = out_project(order, gated, rows)
        got = lax.all_to_all(
            out.reshape(chans, share, width), "chan", split_axis=0, concat_axis=0, tiled=True
        )
        pieces.append(got)
    return jnp.stack(pieces, axis=1).transpose(2, 0, 1, 3).reshape(share, -1)


def solution(mesh):
    return jax.shard_map(
        per_device,
        mesh=mesh,
        in_specs=(
            P("seq", None),
            P(),
            P("seq", None, "chan"),
            P(None, None, "chan"),
            P(None, "chan"),
            P("seq", "chan"),
        ),
        out_specs=P(("seq", "chan"), None),
        check_vma=False,
    )
```

time: 858 us -> 840 us (0.979)
  Pallas kernels: 0 us -> 136 us
  waiting for transfers between devices: 629 us -> 493 us
  matrix products: 85.1 us -> 0 us
  starting transfers between devices: 3.63 us -> 52.6 us
  local copies, waits for them, and re-layouts: 28.7 us -> 75.1 us
  blocking collectives: 51.5 us -> 32 us
  other arithmetic: 46.2 us -> 36.2 us
    all_gather x3 -> x5, waiting for transfers between devices: 629 us -> 0.02 us  [the longest x4 0.02 us: per_device(): gated.append(lax.all_gather(mixed, 'chan', axis=0))]
    ppermute x1 -> x19, waiting for transfers between devices: 0.01 us -> 492 us  [the longest x6 314 us: from_near(): return lax.ppermute(block, 'seq', pairs)]
    pallas_call x0 -> x14, Pallas kernels: none -> 136 us  [the longest x8 92 us: project(): pl.pallas_call(functools.partial(project_kernel, len(weights), len(receiv...]
    dot_general x2 -> x0, matrix products: 85.1 us -> none  [the longest x1 62.9 us: per_device(): jnp.dot(operand, flat_panel, preferred_element_type=jnp.float32)]
    ppermute x1 -> x19, starting transfers between devices: 3.54 us -> 46.8 us  [the longest x9 24.3 us: from_far(): return lax.ppermute(block, 'seq', pairs)]
    reshape x0 -> x6, local copies, waits for them, and re-layouts: none -> 19.9 us  [the longest x4 17.1 us: per_device(): own = in_weight[:, :, cut].reshape(depth, 3 * step)]
    all_to_all x1, blocking collectives: 51.5 us -> 32 us  [per_device(): lax.all_to_all(out.reshape(chans, share, width), 'chan', split_axis=0, co...]
    add x1 -> x0, other arithmetic: 17.1 us -> none  [short_mix(): featured + feat_filter[back_step] * extended[offset - back_step:offset -...]
  transfers between devices with their start and end apart: 4 -> 25, of which waited for: 3 -> 18; matrix products, arithmetic and copies ran while one was open for 14% -> 11% of each run, Pallas kernels for 0% -> 13%
where the time goes in v1:
time: 840 us; the launch traced here: 838 us
  waiting for transfers between devices  493 us (59%)
  Pallas kernels  136 us (16%)
  local copies, waits for them, and re-layouts  75.1 us (9%)
  starting transfers between devices  52.6 us (6%)
  other arithmetic  36.2 us (4%)
  blocking collectives  32 us (4%)
  between operations  13.3 us (2%)
    ppermute x6, waiting for transfers between devices, from_near(): return lax.ppermute(block, 'seq', pairs)  314 us
    ppermute x9, waiting for transfers between devices, from_far(): return lax.ppermute(block, 'seq', pairs)  173 us
    pallas_call x8, Pallas kernels, project(): pl.pallas_call(functools.partial(project_kernel, len(weights), len(receiv...  92 us
    all_to_all x1, blocking collectives, per_device(): lax.all_to_all(out.reshape(chans, share, width), 'chan', split_axis=0, co...  32 us
    pallas_call x2, Pallas kernels, out_project(): pl.pallas_call(functools.partial(out_kernel, len(weights), len(gated)), g...  31 us
    unnamed x36, local copies, waits for them, and re-layouts  29.4 us
    ppermute x9, starting transfers between devices, from_far(): return lax.ppermute(block, 'seq', pairs)  24.3 us
    convert_element_type x2, other arithmetic, normalised(): return (values * lax.rsqrt(squares + 1e-06) * gain).astype(jnp.bfloat16)  17.4 us
  transfers between devices with their start and end apart: 25, of which 18 were waited for; matrix products, arithmetic and copies ran while one was open for 11% of the time, Pallas kernels for 13%

profile of v1, /device:TPU:0, one launch (start us, length us, event | category | flops | bytes accessed | tf_op | source)
XLA Modules:
  0.0 838.0 jit_solution(17546738421212648124)
XLA Ops:
  14.1 23.2 %collective-permute-done.1 = bf16[128,4096]{1,0:T(8,128)(2,1)S(1)} collective-permute-done((bf16[128,4096]{1,0:T(8,128)(2,1)S(1)}, bf16[128,4096]{1,0:T(8,128)(2,1)S(1)}, u32[]{:S(2)}, u32[]{:S(2)}) %collective-permute-start.1) | collective-permute-done | bytes 1048608 | tf_op jit(solution)/shard_map/ppermute | solution.py:175
  38.3 8.4 %fusion.9 = (bf16[2048,3,256]{2,0,1:T(8,128)(2,1)S(1)}, bf16[2048,3,256]{2,0,1:T(8,128)(2,1)}, bf16[2048,3,256]{2,0,1:T(8,128)(2,1)}, bf16[2048,3,256]{2,0,1:T(8,128)(2,1)}) fusion(bf16[2048,3,1024]{2,0,1:T(8,128)(2,1)} %param.8), kind=kLoop, calls=%fused_computation.30 | loop fusion | bytes 25165824 | tf_op jit(solution)/shard_map/slice | solution.py:200
  46.6 5.0 copy.29
  58.0 7.3 fusion
  65.3 60.4 %collective-permute-done.refs_2_ = bf16[2048,768]{1,0:T(8,128)(2,1)} collective-permute-done((bf16[2048,768]{1,0:T(8,128)(2,1)}, bf16[2048,768]{1,0:T(8,128)(2,1)}, u32[]{:S(2)}, u32[]{:S(2)}) %collective-permute-start) | collective-permute-done | bytes 3145760 | tf_op jit(solution)/shard_map/ppermute | solution.py:171
  125.7 11.4 %project.8 = bf16[1024,768]{1,0:T(8,128)(2,1)} custom-call(bf16[1024,4096]{1,0:T(8,128)(2,1)} %all-gather.10.cloned.1.call-done.refs_0_, bf16[2048,768]{1,0:T(8,128)(2,1)} %copy.15.refs_1_, bf16[2048,768]{1,0:T(8,128)(2,1)} %collective-permute-done.refs_2_), custom_call_target="tpu_custom_call" | custom-call | flops 6442450944 | bytes 16252928 | tf_op jit(solution)/shard_map/project/pallas_call | solution.py:39
  138.5 15.2 %fusion.2 = bf16[1024,8192]{1,0:T(8,128)(2,1)} fusion(bf16[1024,8192]{1,0:T(8,128)(2,1)} %param.6, f32[8192]{0:T(1024)S(1)} %copy-done.7, f32[1024]{0:T(1024)S(1)} %add_rsqrt_fusion), kind=kLoop, calls=%fused_computation.4 | loop fusion | flops 33554432 | bytes 33591296 | tf_op jit(solution)/shard_map/convert_element_type | solution.py:156
  153.7 8.4 %constant_dynamic-slice_fusion.3 = (bf16[1024,2048]{1,0:T(8,128)(2,1)}, bf16[1024,2048]{1,0:T(8,128)(2,1)}) fusion(bf16[1024,8192]{1,0:T(8,128)(2,1)} %fusion.2, s32[]{:T(128)S(6)} %select_n.68, s32[]{:T(128)S(6)} %select_n.69), kind=kLoop, calls=%fused_computation.27 | loop fusion | bytes 16777224 | tf_op jit(solution)/shard_map/dynamic_slice | solution.py:180
  162.1 7.9 pad_maximum_fusion.refs_0_
  171.9 11.6 %project.9.q.k.v = bf16[1024,768]{1,0:T(8,128)(2,1)} custom-call(bf16[1024,4096]{1,0:T(8,128)(2,1)} %pad_maximum_fusion.refs_0_, bf16[2048,768]{1,0:T(8,128)(2,1)} %copy.15.refs_1_, bf16[2048,768]{1,0:T(8,128)(2,1)} %collective-permute-done.refs_2_, bf16[1024,768]{1,0:T(8,128)(2,1)} %collective-permute-done.2.refs_3_), custom_call_target="tpu_custom_call" | custom-call | flops 6442450944 | bytes 17825792 | tf_op jit(solution)/shard_map/project/pallas_call | solution.py:39
  192.8 4.7 copy.30
  204.5 64.2 %collective-permute-done.4.refs_2_ = bf16[2048,768]{1,0:T(8,128)(2,1)S(1)} collective-permute-done((bf16[2048,768]{1,0:T(8,128)(2,1)}, bf16[2048,768]{1,0:T(8,128)(2,1)S(1)}, u32[]{:S(2)}, u32[]{:S(2)}) %collective-permute-start.4) | collective-permute-done | bytes 3145760 | tf_op jit(solution)/shard_map/ppermute | solution.py:171
  270.3 11.4 %project.10 = bf16[1024,768]{1,0:T(8,128)(2,1)} custom-call(bf16[1024,4096]{1,0:T(8,128)(2,1)} %all-gather.10.cloned.1.call-done.refs_0_, bf16[2048,768]{1,0:T(8,128)(2,1)} %copy.19.refs_1_, bf16[2048,768]{1,0:T(8,128)(2,1)} %copy-done.11), custom_call_target="tpu_custom_call" | custom-call | flops 6442450944 | bytes 16252928 | tf_op jit(solution)/shard_map/project/pallas_call | solution.py:39
  284.4 29.5 %collective-permute-done.5.refs_3_ = bf16[1024,768]{1,0:T(8,128)(2,1)S(1)} collective-permute-done((bf16[1024,768]{1,0:T(8,128)(2,1)}, bf16[1024,768]{1,0:T(8,128)(2,1)S(1)}, u32[]{:S(2)}, u32[]{:S(2)}) %collective-permute-start.5) | collective-permute-done | bytes 1572896 | tf_op jit(solution)/shard_map/ppermute | solution.py:175
  315.1 11.6 %project.11.q.k.v = bf16[1024,768]{1,0:T(8,128)(2,1)} custom-call(bf16[1024,4096]{1,0:T(8,128)(2,1)} %pad_maximum_fusion.refs_0_, bf16[2048,768]{1,0:T(8,128)(2,1)} %copy.19.refs_1_, bf16[2048,768]{1,0:T(8,128)(2,1)} %copy-done.11, bf16[1024,768]{1,0:T(8,128)(2,1)} %copy-done.14), custom_call_target="tpu_custom_call" | custom-call | flops 6442450944 | bytes 17825792 | tf_op jit(solution)/shard_map/project/pallas_call | solution.py:39
  347.3 61.5 %collective-permute-done.7.refs_2_ = bf16[2048,768]{1,0:T(8,128)(2,1)S(1)} collective-permute-done((bf16[2048,768]{1,0:T(8,128)(2,1)}, bf16[2048,768]{1,0:T(8,128)(2,1)S(1)}, u32[]{:S(2)}, u32[]{:S(2)}) %collective-permute-start.7) | collective-permute-done | bytes 3145760 | tf_op jit(solution)/shard_map/ppermute | solution.py:171
  410.5 11.4 %project.12 = bf16[1024,768]{1,0:T(8,128)(2,1)} custom-call(bf16[1024,4096]{1,0:T(8,128)(2,1)} %all-gather.10.cloned.1.call-done.refs_0_, bf16[2048,768]{1,0:T(8,128)(2,1)} %copy.23.refs_1_, bf16[2048,768]{1,0:T(8,128)(2,1)} %copy-done.12), custom_call_target="tpu_custom_call" | custom-call | flops 6442450944 | bytes 16252928 | tf_op jit(solution)/shard_map/project/pallas_call | solution.py:39
  425.1 26.5 %collective-permute-done.8.refs_3_ = bf16[1024,768]{1,0:T(8,128)(2,1)S(1)} collective-permute-done((bf16[1024,768]{1,0:T(8,128)(2,1)}, bf16[1024,768]{1,0:T(8,128)(2,1)S(1)}, u32[]{:S(2)}, u32[]{:S(2)}) %collective-permute-start.8) | collective-permute-done | bytes 1572896 | tf_op jit(solution)/shard_map/ppermute | solution.py:175
  452.7 11.6 %project.13.q.k.v = bf16[1024,768]{1,0:T(8,128)(2,1)} custom-call(bf16[1024,4096]{1,0:T(8,128)(2,1)} %pad_maximum_fusion.refs_0_, bf16[2048,768]{1,0:T(8,128)(2,1)} %copy.23.refs_1_, bf16[2048,768]{1,0:T(8,128)(2,1)} %copy-done.12, bf16[1024,768]{1,0:T(8,128)(2,1)} %copy-done.15), custom_call_target="tpu_custom_call" | custom-call | flops 6442450944 | bytes 17825792 | tf_op jit(solution)/shard_map/project/pallas_call | solution.py:39
  482.1 58.2 %collective-permute-done.10.refs_2_ = bf16[2048,768]{1,0:T(8,128)(2,1)S(1)} collective-permute-done((bf16[2048,768]{1,0:T(8,128)(2,1)S(1)}, bf16[2048,768]{1,0:T(8,128)(2,1)S(1)}, u32[]{:S(2)}, u32[]{:S(2)}) %collective-permute-start.10) | collective-permute-done | bytes 3145760 | tf_op jit(solution)/shard_map/ppermute | solution.py:171
  542.0 11.4 %project.14 = bf16[1024,768]{1,0:T(8,128)(2,1)} custom-call(bf16[1024,4096]{1,0:T(8,128)(2,1)} %all-gather.10.cloned.1.call-done.refs_0_, bf16[2048,768]{1,0:T(8,128)(2,1)} %copy-done, bf16[2048,768]{1,0:T(8,128)(2,1)} %copy-done.10), custom_call_target="tpu_custom_call" | custom-call | flops 6442450944 | bytes 16252928 | tf_op jit(solution)/shard_map/project/pallas_call | solution.py:39
  556.6 23.5 %collective-permute-done.11.refs_3_ = bf16[1024,768]{1,0:T(8,128)(2,1)S(1)} collective-permute-done((bf16[1024,768]{1,0:T(8,128)(2,1)}, bf16[1024,768]{1,0:T(8,128)(2,1)S(1)}, u32[]{:S(2)}, u32[]{:S(2)}) %collective-permute-start.11) | collective-permute-done | bytes 1572896 | tf_op jit(solution)/shard_map/ppermute | solution.py:175
  581.2 11.6 %project.15.q.k.v = bf16[1024,768]{1,0:T(8,128)(2,1)} custom-call(bf16[1024,4096]{1,0:T(8,128)(2,1)} %pad_maximum_fusion.refs_0_, bf16[2048,768]{1,0:T(8,128)(2,1)} %copy-done, bf16[2048,768]{1,0:T(8,128)(2,1)} %copy-done.10, bf16[1024,768]{1,0:T(8,128)(2,1)} %copy-done.13), custom_call_target="tpu_custom_call" | custom-call | flops 6442450944 | bytes 17825792 | tf_op jit(solution)/shard_map/project/pallas_call | solution.py:39
  612.0 42.9 %collective-permute-done.16.refs_5_ = bf16[2048,512]{1,0:T(8,128)(2,1)} collective-permute-done((bf16[2048,512]{1,0:T(8,128)(2,1)}, bf16[2048,512]{1,0:T(8,128)(2,1)}, u32[]{:S(2)}, u32[]{:S(2)}) %collective-permute-start.16) | collective-permute-done | bytes 2097184 | tf_op jit(solution)/shard_map/ppermute | solution.py:171
  658.9 27.3 %collective-permute-done.13.refs_5_ = bf16[2048,512]{1,0:T(8,128)(2,1)} collective-permute-done((bf16[2048,512]{1,0:T(8,128)(2,1)S(1)}, bf16[2048,512]{1,0:T(8,128)(2,1)}, u32[]{:S(2)}, u32[]{:S(2)}) %collective-permute-start.13) | collective-permute-done | bytes 2097184 | tf_op jit(solution)/shard_map/ppermute | solution.py:171
  689.8 15.9 %collective-permute-done.18.refs_7_ = bf16[2048,512]{1,0:T(8,128)(2,1)} collective-permute-done((bf16[2048,512]{1,0:T(8,128)(2,1)}, bf16[2048,512]{1,0:T(8,128)(2,1)}, u32[]{:S(2)}, u32[]{:S(2)}) %collective-permute-start.18) | collective-permute-done | bytes 2097184 | tf_op jit(solution)/shard_map/ppermute | solution.py:175
  705.8 15.5 %out_project.3 = bf16[1024,512]{1,0:T(8,128)(2,1)} custom-call(s32[4]{0:T(128)} %pad_add_fusion.order, bf16[8,1024,256]{2,1,0:T(8,128)(2,1)} %bitcast.26, bf16[8,1024,256]{2,1,0:T(8,128)(2,1)} %bitcast.28, bf16[8,1024,256]{2,1,0:T(8,128)(2,1)} %bitcast.30, bf16[8,1024,256]{2,1,0:T(8,128)(2,1)} %bitcast.32, bf16[2048,512]{1,0:T(8,128)(2,1)} %get-tuple-element.12.refs_4_, ...), custom_call_target="tpu_custom_call" | custom-call | flops 8589934592 | bytes 26214400 | tf_op jit(solution)/shard_map/out_project/pallas_call | solution.py:139
  721.3 5.4 all-to-all-start.1
  726.7 24.0 %collective-permute-done.14.refs_6_ = bf16[2048,512]{1,0:T(8,128)(2,1)} collective-permute-done((bf16[2048,512]{1,0:T(8,128)(2,1)S(1)}, bf16[2048,512]{1,0:T(8,128)(2,1)}, u32[]{:S(2)}, u32[]{:S(2)}) %collective-permute-start.14) | collective-permute-done | bytes 2097184 | tf_op jit(solution)/shard_map/ppermute | solution.py:175
  750.7 28.0 %collective-permute-done.15.refs_7_ = bf16[2048,512]{1,0:T(8,128)(2,1)} collective-permute-done((bf16[2048,512]{1,0:T(8,128)(2,1)}, bf16[2048,512]{1,0:T(8,128)(2,1)}, u32[]{:S(2)}, u32[]{:S(2)}) %collective-permute-start.15) | collective-permute-done | bytes 2097184 | tf_op jit(solution)/shard_map/ppermute | solution.py:175
  778.7 15.5 %out_project.2 = bf16[1024,512]{1,0:T(8,128)(2,1)} custom-call(s32[4]{0:T(128)} %pad_add_fusion.order, bf16[8,1024,256]{2,1,0:T(8,128)(2,1)} %bitcast.27, bf16[8,1024,256]{2,1,0:T(8,128)(2,1)} %bitcast.29, bf16[8,1024,256]{2,1,0:T(8,128)(2,1)} %bitcast.31, bf16[8,1024,256]{2,1,0:T(8,128)(2,1)} %bitcast.33, bf16[2048,512]{1,0:T(8,128)(2,1)} %copy-done.1, ...), custom_call_target="tpu_custom_call" | custom-call | flops 8589934592 | bytes 26214400 | tf_op jit(solution)/shard_map/out_project/pallas_call | solution.py:139
  794.2 32.0 %all_to_all.10 = bf16[8,128,512]{2,1,0:T(8,128)(2,1)S(1)} all-to-all(bf16[8,128,512]{2,1,0:T(8,128)(2,1)} %bitcast.25), channel_id=1, replica_groups=mesh['seq'=4,'chan'=8] {'chan'}, dimensions={0} | all-to-all | bytes 2097152 | tf_op jit(solution)/shard_map/all_to_all | solution.py:222
  (100 shorter events, 122.2 us)
Async XLA Ops:
  6.5 119.2 %all-gather.10.cloned.1.call-start = ((), (), s32[]{:S(2)}) async-start(), calls=%async_computation.2 | async-start | bytes 9437184 | tf_op jit(solution)/shard_map/all_gather | solution.py:191
  11.0 26.2 %collective-permute-start.1 = (bf16[128,4096]{1,0:T(8,128)(2,1)S(1)}, bf16[128,4096]{1,0:T(8,128)(2,1)S(1)}, u32[]{:S(2)}, u32[]{:S(2)}) collective-permute-start(bf16[128,4096]{1,0:T(8,128)(2,1)S(1)} %pad_maximum_fusion.1), channel_id=1, source_target_pairs={{16,0},{24,8},{0,16},{8,24},{17,1},{25,9},{1,17},{9,25},{18,2},{26... | collective-permute-start | bytes 3145736 | tf_op jit(solution)/shard_map/ppermute | solution.py:175
  38.2 667.5 %all-gather.12.cloned.1.call-start = ((), (), s32[]{:S(2)}) async-start(), calls=%async_computation.3 | async-start | bytes 4718592 | tf_op jit(solution)/shard_map/all_gather | solution.py:210
  56.3 69.4 %collective-permute-start = (bf16[2048,768]{1,0:T(8,128)(2,1)}, bf16[2048,768]{1,0:T(8,128)(2,1)}, u32[]{:S(2)}, u32[]{:S(2)}) collective-permute-start(bf16[2048,768]{1,0:T(8,128)(2,1)} %copy.15.refs_1_), channel_id=1, source_target_pairs={{8,0},{0,8},{24,16},{16,24},{9,1},{1,9},{25,17},{17,25},{10,2},{2,... | collective-permute-start | bytes 9437192 | tf_op jit(solution)/shard_map/ppermute | solution.py:171
  65.3 73.2 %copy-start.7 = (f32[8192]{0:T(1024)S(1)}, f32[8192]{0:T(1024)}, u32[]{:S(2)}) copy-start(f32[8192]{0:T(1024)} %param.7) | copy-start | bytes 98308
  137.1 16.5 %copy-start.8 = (f32[3,3,1024]{2,1,0:T(4,128)S(1)}, f32[3,3,1024]{2,1,0:T(4,128)}, u32[]{:S(2)}) copy-start(f32[3,3,1024]{2,1,0:T(4,128)} %param.9) | copy-start | bytes 110596
  137.1 34.8 %collective-permute-start.2 = (bf16[1024,768]{1,0:T(8,128)(2,1)}, bf16[1024,768]{1,0:T(8,128)(2,1)}, u32[]{:S(2)}, u32[]{:S(2)}) collective-permute-start(bf16[1024,768]{1,0:T(8,128)(2,1)} %project.8), channel_id=1, source_target_pairs={{16,0},{24,8},{0,16},{8,24},{17,1},{25,9},{1,17},{9,25},{18,2},{26... | collective-permute-start | bytes 4718600 | tf_op jit(solution)/shard_map/ppermute | solution.py:175
  170.0 17.1 %copy-start.9 = (f32[7,1024]{1,0:T(8,128)S(1)}, f32[7,1024]{1,0:T(8,128)}, u32[]{:S(2)}) copy-start(f32[7,1024]{1,0:T(8,128)} %param.10) | copy-start | bytes 86020
  184.2 4.4 collective-permute-start.3
  192.5 513.2 %all-gather.14.cloned.1.call-start = ((), (), s32[]{:S(2)}) async-start(), calls=%async_computation.4 | async-start | bytes 4718592 | tf_op jit(solution)/shard_map/all_gather | solution.py:210
  202.2 66.5 %collective-permute-start.4 = (bf16[2048,768]{1,0:T(8,128)(2,1)}, bf16[2048,768]{1,0:T(8,128)(2,1)S(1)}, u32[]{:S(2)}, u32[]{:S(2)}) collective-permute-start(bf16[2048,768]{1,0:T(8,128)(2,1)} %copy.19.refs_1_), channel_id=1, source_target_pairs={{8,0},{0,8},{24,16},{16,24},{9,1},{1,9},{25,17},{17,25},{10,2},{2,... | collective-permute-start | bytes 9437192 | tf_op jit(solution)/shard_map/ppermute | solution.py:171
  281.7 32.2 %collective-permute-start.5 = (bf16[1024,768]{1,0:T(8,128)(2,1)}, bf16[1024,768]{1,0:T(8,128)(2,1)S(1)}, u32[]{:S(2)}, u32[]{:S(2)}) collective-permute-start(bf16[1024,768]{1,0:T(8,128)(2,1)} %project.10), channel_id=1, source_target_pairs={{16,0},{24,8},{0,16},{8,24},{17,1},{25,9},{1,17},{9,25},{18,2},{26... | collective-permute-start | bytes 4718600 | tf_op jit(solution)/shard_map/ppermute | solution.py:175
  327.4 4.2 collective-permute-start.6
  335.6 370.2 %all-gather.16.cloned.1.call-start = ((), (), s32[]{:S(2)}) async-start(), calls=%async_computation.5 | async-start | bytes 4718592 | tf_op jit(solution)/shard_map/all_gather | solution.py:210
  344.9 63.8 %collective-permute-start.7 = (bf16[2048,768]{1,0:T(8,128)(2,1)}, bf16[2048,768]{1,0:T(8,128)(2,1)S(1)}, u32[]{:S(2)}, u32[]{:S(2)}) collective-permute-start(bf16[2048,768]{1,0:T(8,128)(2,1)} %copy.23.refs_1_), channel_id=1, source_target_pairs={{8,0},{0,8},{24,16},{16,24},{9,1},{1,9},{25,17},{17,25},{10,2},{2,... | collective-permute-start | bytes 9437192 | tf_op jit(solution)/shard_map/ppermute | solution.py:171
  408.8 1.7 copy-start.12
  421.9 29.7 %collective-permute-start.8 = (bf16[1024,768]{1,0:T(8,128)(2,1)}, bf16[1024,768]{1,0:T(8,128)(2,1)S(1)}, u32[]{:S(2)}, u32[]{:S(2)}) collective-permute-start(bf16[1024,768]{1,0:T(8,128)(2,1)} %project.12), channel_id=1, source_target_pairs={{16,0},{24,8},{0,16},{8,24},{17,1},{25,9},{1,17},{9,25},{18,2},{26... | collective-permute-start | bytes 4718600 | tf_op jit(solution)/shard_map/ppermute | solution.py:175
  465.0 4.0 collective-permute-start.9
  473.0 232.7 %all-gather.18.cloned.1.call-start = ((), (), s32[]{:S(2)}) async-start(), calls=%async_computation.6 | async-start | bytes 4718592 | tf_op jit(solution)/shard_map/all_gather | solution.py:210
  479.4 60.9 %copy-start = (bf16[2048,768]{1,0:T(8,128)(2,1)}, bf16[2048,768]{1,0:T(8,128)(2,1)S(1)}, u32[]{:S(2)}) copy-start(bf16[2048,768]{1,0:T(8,128)(2,1)S(1)} %copy.27.refs_1_) | copy-start | bytes 9437188
  479.5 60.9 %collective-permute-start.10 = (bf16[2048,768]{1,0:T(8,128)(2,1)S(1)}, bf16[2048,768]{1,0:T(8,128)(2,1)S(1)}, u32[]{:S(2)}, u32[]{:S(2)}) collective-permute-start(bf16[2048,768]{1,0:T(8,128)(2,1)S(1)} %copy.27.refs_1_), channel_id=1, source_target_pairs={{8,0},{0,8},{24,16},{16,24},{9,1},{1,9},{25,17},{17,25},{10,2},{2,... | collective-permute-start | bytes 9437192 | tf_op jit(solution)/shard_map/ppermute | solution.py:171
  540.3 1.6 copy-start.10
  553.4 26.7 %collective-permute-start.11 = (bf16[1024,768]{1,0:T(8,128)(2,1)}, bf16[1024,768]{1,0:T(8,128)(2,1)S(1)}, u32[]{:S(2)}, u32[]{:S(2)}) collective-permute-start(bf16[1024,768]{1,0:T(8,128)(2,1)} %project.14), channel_id=1, source_target_pairs={{16,0},{24,8},{0,16},{8,24},{17,1},{25,9},{1,17},{9,25},{18,2},{26... | collective-permute-start | bytes 4718600 | tf_op jit(solution)/shard_map/ppermute | solution.py:175
  593.6 4.1 collective-permute-start.12
  605.5 115.8 %copy-start.1 = (bf16[2048,512]{1,0:T(8,128)(2,1)}, bf16[2048,512]{1,0:T(8,128)(2,1)S(1)}, u32[]{:S(2)}) copy-start(bf16[2048,512]{1,0:T(8,128)(2,1)S(1)} %get-tuple-element.11.refs_4_) | copy-start | bytes 6291460
  605.5 49.5 %collective-permute-start.16 = (bf16[2048,512]{1,0:T(8,128)(2,1)}, bf16[2048,512]{1,0:T(8,128)(2,1)}, u32[]{:S(2)}, u32[]{:S(2)}) collective-permute-start(bf16[2048,512]{1,0:T(8,128)(2,1)} %get-tuple-element.12.refs_4_), channel_id=1, source_target_pairs={{8,0},{0,8},{24,16},{16,24},{9,1},{1,9},{25,17},{17,25},{10,2},{2,... | collective-permute-start | bytes 6291464 | tf_op jit(solution)/shard_map/ppermute | solution.py:171
  608.1 78.1 %collective-permute-start.13 = (bf16[2048,512]{1,0:T(8,128)(2,1)S(1)}, bf16[2048,512]{1,0:T(8,128)(2,1)}, u32[]{:S(2)}, u32[]{:S(2)}) collective-permute-start(bf16[2048,512]{1,0:T(8,128)(2,1)S(1)} %get-tuple-element.11.refs_4_), channel_id=1, source_target_pairs={{8,0},{0,8},{24,16},{16,24},{9,1},{1,9},{25,17},{17,25},{10,2},{2,... | collective-permute-start | bytes 6291464 | tf_op jit(solution)/shard_map/ppermute | solution.py:171
  608.1 81.7 %collective-permute-start.17 = (bf16[2048,512]{1,0:T(8,128)(2,1)}, bf16[2048,512]{1,0:T(8,128)(2,1)}, u32[]{:S(2)}, u32[]{:S(2)}) collective-permute-start(bf16[2048,512]{1,0:T(8,128)(2,1)} %get-tuple-element.12.refs_4_), channel_id=1, source_target_pairs={{16,0},{24,8},{0,16},{8,24},{17,1},{25,9},{1,17},{9,25},{18,2},{26... | collective-permute-start | bytes 6291464 | tf_op jit(solution)/shard_map/ppermute | solution.py:175
  654.9 50.8 %collective-permute-start.18 = (bf16[2048,512]{1,0:T(8,128)(2,1)}, bf16[2048,512]{1,0:T(8,128)(2,1)}, u32[]{:S(2)}, u32[]{:S(2)}) collective-permute-start(bf16[2048,512]{1,0:T(8,128)(2,1)} %collective-permute-done.16.refs_5_), channel_id=1, source_target_pairs={{16,0},{24,8},{0,16},{8,24},{17,1},{25,9},{1,17},{9,25},{18,2},{26... | collective-permute-start | bytes 6291464 | tf_op jit(solution)/shard_map/ppermute | solution.py:175
  658.9 91.8 %collective-permute-start.14 = (bf16[2048,512]{1,0:T(8,128)(2,1)S(1)}, bf16[2048,512]{1,0:T(8,128)(2,1)}, u32[]{:S(2)}, u32[]{:S(2)}) collective-permute-start(bf16[2048,512]{1,0:T(8,128)(2,1)S(1)} %get-tuple-element.11.refs_4_), channel_id=1, source_target_pairs={{16,0},{24,8},{0,16},{8,24},{17,1},{25,9},{1,17},{9,25},{18,2},{26... | collective-permute-start | bytes 6291464 | tf_op jit(solution)/shard_map/ppermute | solution.py:175
  686.2 92.5 %collective-permute-start.15 = (bf16[2048,512]{1,0:T(8,128)(2,1)}, bf16[2048,512]{1,0:T(8,128)(2,1)}, u32[]{:S(2)}, u32[]{:S(2)}) collective-permute-start(bf16[2048,512]{1,0:T(8,128)(2,1)} %collective-permute-done.13.refs_5_), channel_id=1, source_target_pairs={{16,0},{24,8},{0,16},{8,24},{17,1},{25,9},{1,17},{9,25},{18,2},{26... | collective-permute-start | bytes 6291464 | tf_op jit(solution)/shard_map/ppermute | solution.py:175
  721.3 73.0 %all-to-all-start.1 = ((bf16[8,128,512]{2,1,0:T(8,128)(2,1)}), bf16[8,128,512]{2,1,0:T(8,128)(2,1)S(1)}, u32[]{:S(2)}, u32[]{:S(2)}) async-start(bf16[8,128,512]{2,1,0:T(8,128)(2,1)} %bitcast.24), calls=%async_computation.1 | async-start | bytes 2097152 | tf_op jit(solution)/shard_map/all_to_all | solution.py:222
  (9 other events, 8.4 us)
Sparse Core Ops, SparseCore 0:
  38.3 83.5 all-gather.9
  192.7 49.3 all-gather.11
  335.7 50.3 all-gather.13
  473.1 50.6 all-gather.15
  601.8 50.9 all-gather.17

commit v2 on v1

v2 whole, which is shorter than its diff:
```python
import functools

import jax
import jax.numpy as jnp
from jax import lax
from jax.experimental import pallas as pl
from jax.experimental.pallas import tpu as pltpu
from jax.sharding import PartitionSpec as P

HALO = 16
LANES = 128
EIGHTHS = (0, 2, 5, 7, 8)
CHUNKS = len(EIGHTHS) - 1
OUT_CHUNKS = 2
VMEM = 56 * 2**20
MARK = pl.BlockSpec((8, 128), lambda i: (0, 0))
MARK_SHAPE = jax.ShapeDtypeStruct((8, 128), jnp.float32)
LIGHT = pl.CostEstimate(flops=1024, bytes_accessed=1024, transcendentals=0)


def project_kernel(count, extra, *refs):
    x_ref = refs[0]
    weights = refs[1 : 1 + count]
    received = refs[1 + count : 1 + count + extra]
    out_ref, mark_ref = refs[-2:]
    mark_ref[...] = jnp.zeros_like(mark_ref)
    depth, width = weights[0].shape[1:]
    for part in range(weights[0].shape[0]):
        cut = slice(part * width, (part + 1) * width)
        total = jnp.dot(x_ref[:, :depth], weights[0][part], preferred_element_type=jnp.float32)
        for i in range(1, count):
            total += jnp.dot(
                x_ref[:, i * depth : (i + 1) * depth],
                weights[i][part],
                preferred_element_type=jnp.float32,
            )
        for ref in received:
            total += ref[:, cut].astype(jnp.float32)
        out_ref[:, cut] = total.astype(out_ref.dtype)


def project(x, weights, received=(), after=()):
    rows, depth = x.shape
    columns = weights[0].shape[0] * weights[0].shape[2]
    tile = min(rows, 256)
    whole = pl.BlockSpec(weights[0].shape, lambda i: (0, 0, 0), pipeline_mode=pl.Buffered(1))
    return pl.pallas_call(
        functools.partial(project_kernel, len(weights), len(received)),
        grid=(rows // tile,),
        in_specs=[pl.BlockSpec((tile, depth), lambda i: (i, 0))]
        + [whole] * len(weights)
        + [pl.BlockSpec((tile, columns), lambda i: (i, 0))] * len(received)
        + [pl.BlockSpec(memory_space=pl.ANY)] * len(after),
        out_specs=[pl.BlockSpec((tile, columns), lambda i: (i, 0)), MARK],
        out_shape=[jax.ShapeDtypeStruct((rows, columns), jnp.bfloat16), MARK_SHAPE],
        compiler_params=pltpu.CompilerParams(vmem_limit_bytes=VMEM),
        cost_estimate=LIGHT,
        name="project",
    )(x, *weights, *received, *after)


def mix_kernel(feat, filt, qh, kh, vh, q, k, v, taps, out_ref, mark_ref, ext, prod):
    rows = q.shape[0]
    mark_ref[...] = jnp.zeros_like(mark_ref)
    for i, (h, b) in enumerate(((qh, q), (kh, k), (vh, v))):
        ext[i, :HALO, :] = h[...].astype(jnp.float32)
        ext[i, HALO:, :] = b[...].astype(jnp.float32)
    tile = min(rows, 128)

    def featured(i, start, size):
        total = taps[i : i + 1, :] * ext[i, pl.ds(start, size), :]
        for j in range(1, feat):
            total += taps[3 * j + i : 3 * j + i + 1, :] * ext[i, pl.ds(start - j, size), :]
        return total

    for t in range(rows // tile):
        base = HALO + t * tile
        prod[...] = featured(1, base - 8, tile + 8) * featured(2, base - 8, tile + 8)
        total = taps[3 * feat : 3 * feat + 1, :] * prod[pl.ds(8, tile), :]
        for j in range(1, filt):
            total += taps[3 * feat + j : 3 * feat + j + 1, :] * prod[pl.ds(8 - j, tile), :]
        out_ref[t * tile : (t + 1) * tile, :] = (featured(0, base, tile) * total).astype(out_ref.dtype)


def short_mix(halo, projected, taps, feat, filt):
    rows, width = projected.shape[0], projected.shape[1] // 3
    lanes = LANES
    steps = width // lanes

    def part(i, size):
        return pl.BlockSpec((size, lanes), lambda b: (0, i * steps + b))

    tile = min(rows, 128)
    return pl.pallas_call(
        functools.partial(mix_kernel, feat, filt),
        grid=(steps,),
        in_specs=[part(i, HALO) for i in range(3)]
        + [part(i, rows) for i in range(3)]
        + [pl.BlockSpec((taps.shape[0], lanes), lambda b: (0, b))],
        out_specs=[pl.BlockSpec((rows, lanes), lambda b: (0, b)), MARK],
        out_shape=[jax.ShapeDtypeStruct((rows, width), jnp.bfloat16), MARK_SHAPE],
        scratch_shapes=[
            pltpu.VMEM((3, HALO + rows, lanes), jnp.float32),
            pltpu.VMEM((tile + 8, lanes), jnp.float32),
        ],
        compiler_params=pltpu.CompilerParams(vmem_limit_bytes=VMEM),
        cost_estimate=LIGHT,
        name="short_mix",
    )(halo, halo, halo, projected, projected, projected, taps)


def out_kernel(blocks, starts, order, *refs):
    gated = refs[: len(starts)]
    weights = refs[len(starts) : len(starts) + blocks]
    held, out_ref = refs[len(starts) + blocks : -1], refs[-1]
    depth = weights[0].shape[0]
    per_block = gated[0].shape[0] // blocks
    total = held[0][...] if held else jnp.zeros(out_ref.shape, jnp.float32)
    for b in range(blocks):
        for i in range(per_block):
            for ref, start in zip(gated, starts):
                row = i * (depth // per_block) + start
                total += jnp.dot(
                    ref[order[b] * per_block + i],
                    weights[b][row : row + ref.shape[2], :],
                    preferred_element_type=jnp.float32,
                )
    out_ref[...] = total.astype(out_ref.dtype)


def out_project(order, gated, starts, weights, kind, held=()):
    chans, rows, _ = gated[0].shape
    depth, columns = weights[0].shape
    tile, wide = min(rows, 256), min(columns, 512)
    cell = pl.BlockSpec((tile, wide), lambda n, i, o: (i, n))
    spec = pltpu.PrefetchScalarGridSpec(
        num_scalar_prefetch=1,
        grid=(columns // wide, rows // tile),
        in_specs=[pl.BlockSpec((chans, tile, block.shape[2]), lambda n, i, o: (0, i, 0)) for block in gated]
        + [pl.BlockSpec((depth, wide), lambda n, i, o: (0, n))] * len(weights)
        + [cell] * len(held),
        out_specs=cell,
    )
    return pl.pallas_call(
        functools.partial(out_kernel, len(weights), starts),
        grid_spec=spec,
        out_shape=jax.ShapeDtypeStruct((rows, columns), kind),
        compiler_params=pltpu.CompilerParams(vmem_limit_bytes=VMEM),
        cost_estimate=LIGHT,
        name="out_project",
    )(order, *gated, *weights, *held)


def normalised(x, gain):
    values = x.astype(jnp.float32)
    squares = jnp.mean(values * values, axis=1, keepdims=True)
    return (values * lax.rsqrt(squares + 1e-06) * gain).astype(jnp.bfloat16)


def per_device(x_rows, norm_gain, in_weight, feat_filter, inner_filter, out_weight):
    tokens, model = x_rows.shape
    depth, _, chans_here = in_weight.shape
    seqs, chans = lax.axis_size("seq"), lax.axis_size("chan")
    near = 2 if seqs % 2 == 0 else 1
    far = seqs // near
    seq, chan = lax.axis_index("seq"), lax.axis_index("chan")
    e, g = seq // near, seq % near
    feat, filt = feat_filter.shape[0], inner_filter.shape[0]

    def from_near(block, k):
        pairs = [(a * near + (b + k) % near, a * near + b) for a in range(far) for b in range(near)]
        return lax.ppermute(block, "seq", pairs)

    def from_far(block, k):
        pairs = [((a + k) % far * near + b, a * near + b) for a in range(far) for b in range(near)]
        return lax.ppermute(block, "seq", pairs)

    def columns_of(rows, group):
        return jnp.concatenate(
            [
                lax.dynamic_slice_in_dim(rows, (group * near + (g + i) % near) * depth, depth, 1)
                for i in range(near)
            ],
            axis=1,
        )

    together = lax.optimization_barrier
    units = chans_here // LANES
    edges = [LANES * (units * part // 8) for part in EIGHTHS]
    cuts = [slice(a, b) for a, b in zip(edges, edges[1:])]
    first = in_weight[:, :, cuts[0]].transpose(1, 0, 2)
    in_weight, first = together((in_weight, first))
    owns = [first] + [in_weight[:, :, cut].transpose(1, 0, 2) for cut in cuts[1:]]
    weights = [[own] + [from_near(own, k) for k in range(1, near)] for own in owns]
    width = out_weight.shape[1] // OUT_CHUNKS
    rows = [out_weight[:, m * width : (m + 1) * width] for m in range(OUT_CHUNKS)]

    share = tokens // chans
    part = normalised(lax.dynamic_slice_in_dim(x_rows, chan * share, share, 0), norm_gain)
    pieces = [
        from_far(columns_of(part, (e - k) % far), k) for k in range(1, far)
    ]
    pieces, rows, owns = together((pieces, rows, owns))
    theirs = [lax.all_gather(piece, "chan", axis=0, tiled=True) for piece in pieces]
    mine = columns_of(normalised(x_rows, norm_gain), e)
    taps = jnp.concatenate([feat_filter.reshape(feat * 3, chans_here), inner_filter], axis=0)

    across = [[from_far(block, a) for a in range(1, far)] for block in rows]
    theirs, weights[0], mine, across, rows = together(
        (theirs, weights[0], mine, across, rows)
    )
    near_rows = [[from_near(block, k) for k in range(1, near)] for block in rows]

    gated, done = [], []
    for j in range(CHUNKS):
        products = [project(block, weights[j], after=done)[0] for block in theirs]
        sums = [from_far(products[k - 1], far - k) for k in range(1, far)]
        if j < CHUNKS - 1:
            sums, weights[j + 1] = together((sums, weights[j + 1]))
        if j == CHUNKS - 1:
            sums, near_rows[0] = together((sums, near_rows[0]))
        projected, _ = project(mine, weights[j], sums)
        halo = lax.ppermute(
            projected[tokens - HALO :], "seq", [(a, a + 1) for a in range(seqs - 1)]
        )
        mixed, mark = short_mix(halo, projected, taps[:, cuts[j]], feat, filt)
        done = [mark]
        if j == CHUNKS - 1:
            mixed, near_rows = together((mixed, near_rows))
        if j > 0:
            mixed, gated[j - 1] = together((mixed, gated[j - 1]))
        gated.append(lax.all_gather(mixed, "chan", axis=0))

    order = jnp.stack(
        [(e + a) % far * near + (g + b) % near for a in range(far) for b in range(near)]
    ).astype(jnp.int32)
    sums = []
    blocks = []
    for m in range(OUT_CHUNKS):
        found = [rows[m]] + near_rows[m]
        for a in range(1, far):
            found += [across[m][a - 1]] + [from_far(block, a) for block in near_rows[m]]
        blocks.append(found)
        sums.append(out_project(order, gated[:-1], edges[: CHUNKS - 1], found, jnp.float32))
    sums, last = together((sums, gated[-1]))
    outs = [
        out_project(order, [last], [edges[CHUNKS - 1]], blocks[m], jnp.bfloat16, [sums[m]])
        for m in range(OUT_CHUNKS)
    ]
    out = jnp.concatenate(outs, axis=1).reshape(chans, share, -1)
    got = lax.all_to_all(out, "chan", split_axis=0, concat_axis=0, tiled=True)
    return got.transpose(1, 0, 2).reshape(share, -1)


def solution(mesh):
    return jax.shard_map(
        per_device,
        mesh=mesh,
        in_specs=(
            P("seq", None),
            P(),
            P("seq", None, "chan"),
            P(None, None, "chan"),
            P(None, "chan"),
            P("seq", "chan"),
        ),
        out_specs=P(("seq", "chan"), None),
        check_vma=False,
    )
```

time: 840 us -> 683 us (0.81)
  waiting for transfers between devices: 493 us -> 339 us
  local copies, waits for them, and re-layouts: 75.1 us -> 32.7 us
  Pallas kernels: 136 us -> 167 us
  blocking collectives: 32 us -> 51.5 us
  starting transfers between devices: 52.6 us -> 39 us
    ppermute x6, waiting for transfers between devices: 314 us -> 150 us  [from_near(): return lax.ppermute(block, 'seq', pairs)]
    ppermute x4, waiting for transfers between devices: 5.29 us -> 30 us  [per_device(): lax.ppermute(projected[tokens - HALO:], 'seq', [(a, a + 1) for a in range...]
    unnamed x36 -> x40, local copies, waits for them, and re-layouts: 29.4 us -> 8.03 us
    all_to_all x1, blocking collectives: 32 us -> 51.5 us  [per_device(): got = lax.all_to_all(out, 'chan', split_axis=0, concat_axis=0, tiled=True)]
    reshape x5 -> x1, local copies, waits for them, and re-layouts: 19.9 us -> 1.49 us  [per_device(): return got.transpose(1, 0, 2).reshape(share, -1)]
    pallas_call x2 -> x4, Pallas kernels: 31 us -> 48.4 us  [out_project(): pl.pallas_call(functools.partial(out_kernel, len(weights), starts), grid_...]
    ppermute x9, waiting for transfers between devices: 173 us -> 158 us  [from_far(): return lax.ppermute(block, 'seq', pairs)]
    pallas_call x8, Pallas kernels: 92 us -> 105 us  [project(): pl.pallas_call(functools.partial(project_kernel, len(weights), len(receiv...]
  transfers between devices with their start and end apart: 25 -> 24, of which waited for: 18 -> 16; matrix products, arithmetic and copies ran while one was open for 11% -> 8% of each run, Pallas kernels for 13% -> 20%
where the time goes in v2:
time: 683 us; the launch traced here: 682 us
  waiting for transfers between devices  339 us (50%)
  Pallas kernels  167 us (24%)
  blocking collectives  51.5 us (8%)
  starting transfers between devices  39 us (6%)
  other arithmetic  39 us (6%)
  local copies, waits for them, and re-layouts  32.7 us (5%)
  between operations  13.4 us (2%)
    ppermute x9, waiting for transfers between devices, from_far(): return lax.ppermute(block, 'seq', pairs)  158 us
    ppermute x6, waiting for transfers between devices, from_near(): return lax.ppermute(block, 'seq', pairs)  150 us
    pallas_call x8, Pallas kernels, project(): pl.pallas_call(functools.partial(project_kernel, len(weights), len(receiv...  105 us
    all_to_all x1, blocking collectives, per_device(): got = lax.all_to_all(out, 'chan', split_axis=0, concat_axis=0, tiled=True)  51.5 us
    pallas_call x4, Pallas kernels, out_project(): pl.pallas_call(functools.partial(out_kernel, len(weights), starts), grid_...  48.4 us
    ppermute x4, waiting for transfers between devices, per_device(): lax.ppermute(projected[tokens - HALO:], 'seq', [(a, a + 1) for a in range...  30 us
    convert_element_type x2, other arithmetic, normalised(): return (values * lax.rsqrt(squares + 1e-06) * gain).astype(jnp.bfloat16)  17.6 us
    ppermute x9, starting transfers between devices, from_far(): return lax.ppermute(block, 'seq', pairs)  15.7 us
  transfers between devices with their start and end apart: 24, of which 16 were waited for; matrix products, arithmetic and copies ran while one was open for 8% of the time, Pallas kernels for 20%

profile of v2, /device:TPU:0, one launch (start us, length us, event | category | flops | bytes accessed | tf_op | source)
XLA Modules:
  0.0 681.5 jit_solution(7053668944713916978)
XLA Ops:
  27.7 9.7 %collective-permute-done = bf16[128,4096]{1,0:T(8,128)(2,1)} collective-permute-done((bf16[128,4096]{1,0:T(8,128)(2,1)S(1)}, bf16[128,4096]{1,0:T(8,128)(2,1)}, u32[]{:S(2)}, u32[]{:S(2)}) %collective-permute-start) | collective-permute-done | bytes 1048608 | tf_op jit(solution)/shard_map/ppermute | solution.py:176
  39.7 7.4 %fusion = f32[1024]{0:T(1024)S(1)} fusion(bf16[1024,8192]{1,0:T(8,128)(2,1)} %param.6), kind=kLoop, calls=%fused_computation.2 | loop fusion | flops 25164800 | bytes 16781312 | tf_op jit(solution)/shard_map/reduce_sum | solution.py:156
  49.2 15.3 %fusion.2 = bf16[1024,8192]{1,0:T(8,128)(2,1)} fusion(bf16[1024,8192]{1,0:T(8,128)(2,1)} %param.6, f32[8192]{0:T(1024)S(1)} %copy-done.17, f32[1024]{0:T(1024)S(1)} %add_rsqrt_fusion), kind=kLoop, calls=%fused_computation.4 | loop fusion | flops 33554432 | bytes 33591296 | tf_op jit(solution)/shard_map/convert_element_type | solution.py:157
  64.5 8.6 %constant_dynamic-slice_fusion.1 = (bf16[1024,2048]{1,0:T(8,128)(2,1)}, bf16[1024,2048]{1,0:T(8,128)(2,1)}) fusion(bf16[1024,8192]{1,0:T(8,128)(2,1)} %fusion.2, s32[]{:T(128)S(6)} %select_n.72, s32[]{:T(128)S(6)} %select_n.73), kind=kLoop, calls=%fused_computation.29 | loop fusion | bytes 16777224 | tf_op jit(solution)/shard_map/dynamic_slice | solution.py:181
  73.1 7.9 %pad_maximum_fusion.refs_0_ = bf16[1024,4096]{1,0:T(8,128)(2,1)} fusion(bf16[1024,2048]{1,0:T(8,128)(2,1)} %get-tuple-element.108, bf16[1024,2048]{1,0:T(8,128)(2,1)} %get-tuple-element.107), kind=kLoop, calls=%fused_computation.5 | loop fusion | flops 16777216 | bytes 16777216 | tf_op jit(solution)/shard_map/concatenate | solution.py:179
  81.0 15.0 %collective-permute-done.2.refs_5_.refs_3_ = bf16[2048,512]{1,0:T(8,128)(2,1)} collective-permute-done((bf16[2048,512]{1,0:T(8,128)(2,1)}, bf16[2048,512]{1,0:T(8,128)(2,1)}, u32[]{:S(2)}, u32[]{:S(2)}) %collective-permute-start.2) | collective-permute-done | bytes 2097184 | tf_op jit(solution)/shard_map/ppermute | solution.py:176
  96.1 42.4 %collective-permute-done.3.refs_5_.refs_3_ = bf16[2048,512]{1,0:T(8,128)(2,1)} collective-permute-done((bf16[2048,512]{1,0:T(8,128)(2,1)}, bf16[2048,512]{1,0:T(8,128)(2,1)}, u32[]{:S(2)}, u32[]{:S(2)}) %collective-permute-start.3) | collective-permute-done | bytes 2097184 | tf_op jit(solution)/shard_map/ppermute | solution.py:176
  138.4 11.5 %project.8 = (bf16[1024,768]{1,0:T(8,128)(2,1)}, f32[8,128]{1,0:T(8,128)}) custom-call(bf16[1024,4096]{1,0:T(8,128)(2,1)} %all-gather.10.cloned.1.call-done.refs_0_, bf16[3,2048,256]{2,1,0:T(8,128)(2,1)} %copy-done, bf16[3,2048,256]{2,1,0:T(8,128)(2,1)} %collective-permute-done.1.refs_2_), custom_call_target="tpu_custom_call" | custom-call | flops 1024 | bytes 1024 | tf_op jit(solution)/shard_map/project/pallas_call | solution.py:47
  151.4 56.7 %collective-permute-done.5.refs_2_ = bf16[3,2048,384]{2,1,0:T(8,128)(2,1)} collective-permute-done((bf16[3,2048,384]{2,1,0:T(8,128)(2,1)}, bf16[3,2048,384]{2,1,0:T(8,128)(2,1)}, u32[]{:S(2)}, u32[]{:S(2)}) %collective-permute-start.5) | collective-permute-done | bytes 4718624 | tf_op jit(solution)/shard_map/ppermute | solution.py:172
  209.3 11.6 %project.9 = (bf16[1024,768]{1,0:T(8,128)(2,1)}, f32[8,128]{1,0:T(8,128)}) custom-call(bf16[1024,4096]{1,0:T(8,128)(2,1)} %pad_maximum_fusion.refs_0_, bf16[3,2048,256]{2,1,0:T(8,128)(2,1)} %copy-done, bf16[3,2048,256]{2,1,0:T(8,128)(2,1)} %collective-permute-done.1.refs_2_, bf16[1024,768]{1,0:T(8,128)(2,1)} %copy-done.10), custom_call_target="tpu_custom_call" | custom-call | flops 1024 | bytes 1024 | tf_op jit(solution)/shard_map/project/pallas_call | solution.py:47
  221.8 3.4 collective-permute-start.6
  233.2 19.0 %project.10 = (bf16[1024,1152]{1,0:T(8,128)(2,1)}, f32[8,128]{1,0:T(8,128)}) custom-call(bf16[1024,4096]{1,0:T(8,128)(2,1)} %all-gather.10.cloned.1.call-done.refs_0_, bf16[3,2048,384]{2,1,0:T(8,128)(2,1)} %slice_bitcast_fusion.refs_1_, bf16[3,2048,384]{2,1,0:T(8,128)(2,1)} %collective-permute-done.5.refs_2_, f32[8,128]{1,0:T(8,128)} %get-tuple-element.70.refs_3_), custom_call_target="tpu_custom_call" | custom-call | flops 1024 | bytes 1024 | tf_op jit(solution)/shard_map/project/pallas_call | solution.py:47
  253.7 44.7 %collective-permute-done.8.refs_2_ = bf16[3,2048,256]{2,1,0:T(8,128)(2,1)S(1)} collective-permute-done((bf16[3,2048,256]{2,1,0:T(8,128)(2,1)S(1)}, bf16[3,2048,256]{2,1,0:T(8,128)(2,1)S(1)}, u32[]{:S(2)}, u32[]{:S(2)}) %collective-permute-start.8) | collective-permute-done | bytes 3145760 | tf_op jit(solution)/shard_map/ppermute | solution.py:172
  298.4 3.9 collective-permute-done.7.refs_3_
  302.3 19.2 %project.11 = (bf16[1024,1152]{1,0:T(8,128)(2,1)}, f32[8,128]{1,0:T(8,128)}) custom-call(bf16[1024,4096]{1,0:T(8,128)(2,1)} %pad_maximum_fusion.refs_0_, bf16[3,2048,384]{2,1,0:T(8,128)(2,1)} %slice_bitcast_fusion.refs_1_, bf16[3,2048,384]{2,1,0:T(8,128)(2,1)} %collective-permute-done.5.refs_2_, bf16[1024,1152]{1,0:T(8,128)(2,1)} %collective-permute-done.7.refs_3_), custom_call_target="tpu_custom_call" | custom-call | flops 1024 | bytes 1024 | tf_op jit(solution)/shard_map/project/pallas_call | solution.py:47
  327.7 4.5 short_mix.5
  334.7 11.5 %project.12 = (bf16[1024,768]{1,0:T(8,128)(2,1)}, f32[8,128]{1,0:T(8,128)}) custom-call(bf16[1024,4096]{1,0:T(8,128)(2,1)} %all-gather.10.cloned.1.call-done.refs_0_, bf16[3,2048,256]{2,1,0:T(8,128)(2,1)} %slice_bitcast_fusion.1.refs_1_, bf16[3,2048,256]{2,1,0:T(8,128)(2,1)} %copy-done.4, f32[8,128]{1,0:T(8,128)} %get-tuple-element.79.refs_3_), custom_call_target="tpu_custom_call" | custom-call | flops 1024 | bytes 1024 | tf_op jit(solution)/shard_map/project/pallas_call | solution.py:47
  348.0 16.1 %collective-permute-done.11.refs_2_ = bf16[3,2048,128]{2,1,0:T(8,128)(2,1)S(1)} collective-permute-done((bf16[3,2048,128]{2,1,0:T(8,128)(2,1)S(1)}, bf16[3,2048,128]{2,1,0:T(8,128)(2,1)S(1)}, u32[]{:S(2)}, u32[]{:S(2)}) %collective-permute-start.11) | collective-permute-done | bytes 1572896 | tf_op jit(solution)/shard_map/ppermute | solution.py:172
  364.1 13.1 %collective-permute-done.10.refs_3_ = bf16[1024,768]{1,0:T(8,128)(2,1)S(1)} collective-permute-done((bf16[1024,768]{1,0:T(8,128)(2,1)}, bf16[1024,768]{1,0:T(8,128)(2,1)S(1)}, u32[]{:S(2)}, u32[]{:S(2)}) %collective-permute-start.10) | collective-permute-done | bytes 1572896 | tf_op jit(solution)/shard_map/ppermute | solution.py:176
  378.4 11.6 %project.13 = (bf16[1024,768]{1,0:T(8,128)(2,1)}, f32[8,128]{1,0:T(8,128)}) custom-call(bf16[1024,4096]{1,0:T(8,128)(2,1)} %pad_maximum_fusion.refs_0_, bf16[3,2048,256]{2,1,0:T(8,128)(2,1)} %slice_bitcast_fusion.1.refs_1_, bf16[3,2048,256]{2,1,0:T(8,128)(2,1)} %copy-done.4, bf16[1024,768]{1,0:T(8,128)(2,1)} %copy-done.11), custom_call_target="tpu_custom_call" | custom-call | flops 1024 | bytes 1024 | tf_op jit(solution)/shard_map/project/pallas_call | solution.py:47
  402.0 10.4 %project.14 = (bf16[1024,384]{1,0:T(8,128)(2,1)}, f32[8,128]{1,0:T(8,128)}) custom-call(bf16[1024,4096]{1,0:T(8,128)(2,1)} %all-gather.10.cloned.1.call-done.refs_0_, bf16[3,2048,128]{2,1,0:T(8,128)(2,1)} %slice_bitcast_fusion.3.refs_1_, bf16[3,2048,128]{2,1,0:T(8,128)(2,1)} %copy-done.7, f32[8,128]{1,0:T(8,128)} %get-tuple-element.88.refs_3_), custom_call_target="tpu_custom_call" | custom-call | flops 1024 | bytes 1024 | tf_op jit(solution)/shard_map/project/pallas_call | solution.py:47
  415.7 32.9 %collective-permute-done.14.refs_4_.refs_2_ = bf16[2048,512]{1,0:T(8,128)(2,1)S(1)} collective-permute-done((bf16[2048,512]{1,0:T(8,128)(2,1)}, bf16[2048,512]{1,0:T(8,128)(2,1)S(1)}, u32[]{:S(2)}, u32[]{:S(2)}) %collective-permute-start.14) | collective-permute-done | bytes 2097184 | tf_op jit(solution)/shard_map/ppermute | solution.py:172
  449.6 10.5 %project.15 = (bf16[1024,384]{1,0:T(8,128)(2,1)}, f32[8,128]{1,0:T(8,128)}) custom-call(bf16[1024,4096]{1,0:T(8,128)(2,1)} %pad_maximum_fusion.refs_0_, bf16[3,2048,128]{2,1,0:T(8,128)(2,1)} %slice_bitcast_fusion.3.refs_1_, bf16[3,2048,128]{2,1,0:T(8,128)(2,1)} %copy-done.7, bf16[1024,384]{1,0:T(8,128)(2,1)} %copy-done.12), custom_call_target="tpu_custom_call" | custom-call | flops 1024 | bytes 1024 | tf_op jit(solution)/shard_map/project/pallas_call | solution.py:47
  460.8 4.0 collective-permute-start.15
  465.4 26.6 %collective-permute-done.15.qh.kh.vh = bf16[16,384]{1,0:T(8,128)(2,1)S(1)} collective-permute-done((bf16[16,384]{1,0:T(8,128)(2,1)S(1)}, bf16[16,384]{1,0:T(8,128)(2,1)S(1)}, u32[]{:S(2)}, u32[]{:S(2)}) %collective-permute-start.15) | collective-permute-done | bytes 12320 | tf_op jit(solution)/shard_map/ppermute | solution.py:223
  498.4 46.0 %collective-permute-done.18.refs_6_.refs_4_ = bf16[2048,512]{1,0:T(8,128)(2,1)} collective-permute-done((bf16[2048,512]{1,0:T(8,128)(2,1)S(1)}, bf16[2048,512]{1,0:T(8,128)(2,1)}, u32[]{:S(2)}, u32[]{:S(2)}) %collective-permute-start.18) | collective-permute-done | bytes 2097184 | tf_op jit(solution)/shard_map/ppermute | solution.py:176
  544.4 15.5 %out_project.5.refs_5_ = f32[1024,512]{1,0:T(8,128)} custom-call(s32[4]{0:T(128)} %pad_add_fusion.order, bf16[8,1024,256]{2,1,0:T(8,128)(2,1)} %bitcast.22, bf16[8,1024,384]{2,1,0:T(8,128)(2,1)} %bitcast.20, bf16[8,1024,256]{2,1,0:T(8,128)(2,1)} %bitcast.24, bf16[2048,512]{1,0:T(8,128)(2,1)} %get-tuple-element.95.refs_3_.refs_1_, ...), custom_call_target="tpu_custom_call" | custom-call | flops 1024 | bytes 1024 | tf_op jit(solution)/shard_map/out_project/pallas_call | solution.py:144
  559.9 27.7 %collective-permute-done.17.refs_6_.refs_4_ = bf16[2048,512]{1,0:T(8,128)(2,1)} collective-permute-done((bf16[2048,512]{1,0:T(8,128)(2,1)}, bf16[2048,512]{1,0:T(8,128)(2,1)}, u32[]{:S(2)}, u32[]{:S(2)}) %collective-permute-start.17) | collective-permute-done | bytes 2097184 | tf_op jit(solution)/shard_map/ppermute | solution.py:176
  587.6 15.4 %out_project.4.refs_5_ = f32[1024,512]{1,0:T(8,128)} custom-call(s32[4]{0:T(128)} %pad_add_fusion.order, bf16[8,1024,256]{2,1,0:T(8,128)(2,1)} %bitcast.23, bf16[8,1024,384]{2,1,0:T(8,128)(2,1)} %bitcast.21, bf16[8,1024,256]{2,1,0:T(8,128)(2,1)} %bitcast.25, bf16[2048,512]{1,0:T(8,128)(2,1)} %get-tuple-element.90.refs_3_.refs_1_, ...), custom_call_target="tpu_custom_call" | custom-call | flops 1024 | bytes 1024 | tf_op jit(solution)/shard_map/out_project/pallas_call | solution.py:144
  603.0 8.7 %out_project.6 = bf16[1024,512]{1,0:T(8,128)(2,1)} custom-call(s32[4]{0:T(128)} %pad_add_fusion.order, bf16[8,1024,128]{2,1,0:T(8,128)(2,1)} %bitcast.28, bf16[2048,512]{1,0:T(8,128)(2,1)} %get-tuple-element.90.refs_3_.refs_1_, bf16[2048,512]{1,0:T(8,128)(2,1)} %copy-done.6, bf16[2048,512]{1,0:T(8,128)(2,1)} %collective-permute-done.2.refs_5_.refs_3_, ...), custom_call_target="tpu_custom_call" | custom-call | flops 1024 | bytes 1024 | tf_op jit(solution)/shard_map/out_project/pallas_call | solution.py:144
  611.7 8.8 %out_project.7 = bf16[1024,512]{1,0:T(8,128)(2,1)} custom-call(s32[4]{0:T(128)} %pad_add_fusion.order, bf16[8,1024,128]{2,1,0:T(8,128)(2,1)} %bitcast.29, bf16[2048,512]{1,0:T(8,128)(2,1)} %get-tuple-element.95.refs_3_.refs_1_, bf16[2048,512]{1,0:T(8,128)(2,1)} %copy-done.5, bf16[2048,512]{1,0:T(8,128)(2,1)} %collective-permute-done.3.refs_5_.refs_3_, ...), custom_call_target="tpu_custom_call" | custom-call | flops 1024 | bytes 1024 | tf_op jit(solution)/shard_map/out_project/pallas_call | solution.py:144
  622.0 51.5 %all_to_all.5 = bf16[8,128,1024]{2,1,0:T(8,128)(2,1)S(1)} all-to-all(bf16[8,128,1024]{2,1,0:T(8,128)(2,1)S(1)} %bitcast.26), channel_id=1, replica_groups=mesh['seq'=4,'chan'=8] {'chan'}, dimensions={0} | all-to-all | bytes 4194304 | tf_op jit(solution)/shard_map/all_to_all | solution.py:251
  (104 shorter events, 76.8 us)
Async XLA Ops:
  6.5 131.9 %all-gather.10.cloned.1.call-start = ((), (), s32[]{:S(2)}) async-start(), calls=%async_computation.1 | async-start | bytes 9437184 | tf_op jit(solution)/shard_map/all_gather | solution.py:204
  11.2 26.3 %collective-permute-start = (bf16[128,4096]{1,0:T(8,128)(2,1)S(1)}, bf16[128,4096]{1,0:T(8,128)(2,1)}, u32[]{:S(2)}, u32[]{:S(2)}) collective-permute-start(bf16[128,4096]{1,0:T(8,128)(2,1)S(1)} %pad_maximum_fusion.2), channel_id=1, source_target_pairs={{16,0},{24,8},{0,16},{8,24},{17,1},{25,9},{1,17},{9,25},{18,2},{26... | collective-permute-start | bytes 3145736 | tf_op jit(solution)/shard_map/ppermute | solution.py:176
  16.3 21.2 %copy-start = (bf16[3,2048,256]{2,1,0:T(8,128)(2,1)}, bf16[3,2048,256]{2,1,0:T(8,128)(2,1)S(1)}, u32[]{:S(2)}) copy-start(bf16[3,2048,256]{2,1,0:T(8,128)(2,1)S(1)} %slice_bitcast_fusion.2.refs_1_) | copy-start | bytes 9437188
  37.5 11.7 %copy-start.17 = (f32[8192]{0:T(1024)S(1)}, f32[8192]{0:T(1024)}, u32[]{:S(2)}) copy-start(f32[8192]{0:T(1024)} %param.7) | copy-start | bytes 98308
  37.5 294.7 %all-gather.12.cloned.1.call-start = ((), (), s32[]{:S(2)}) async-start(), calls=%async_computation.2 | async-start | bytes 4718592 | tf_op jit(solution)/shard_map/all_gather | solution.py:232
  37.6 100.9 %collective-permute-start.1 = (bf16[3,2048,256]{2,1,0:T(8,128)(2,1)S(1)}, bf16[3,2048,256]{2,1,0:T(8,128)(2,1)}, u32[]{:S(2)}, u32[]{:S(2)}) collective-permute-start(bf16[3,2048,256]{2,1,0:T(8,128)(2,1)S(1)} %slice_bitcast_fusion.2.refs_1_), channel_id=1, source_target_pairs={{8,0},{0,8},{24,16},{16,24},{9,1},{1,9},{25,17},{17,25},{10,2},{2,... | collective-permute-start | bytes 9437192 | tf_op jit(solution)/shard_map/ppermute | solution.py:172
  39.3 168.8 %collective-permute-start.5 = (bf16[3,2048,384]{2,1,0:T(8,128)(2,1)}, bf16[3,2048,384]{2,1,0:T(8,128)(2,1)}, u32[]{:S(2)}, u32[]{:S(2)}) collective-permute-start(bf16[3,2048,384]{2,1,0:T(8,128)(2,1)} %slice_bitcast_fusion.refs_1_), channel_id=1, source_target_pairs={{8,0},{0,8},{24,16},{16,24},{9,1},{1,9},{25,17},{17,25},{10,2},{2,... | collective-permute-start | bytes 14155784 | tf_op jit(solution)/shard_map/ppermute | solution.py:172
  47.1 48.9 %collective-permute-start.2 = (bf16[2048,512]{1,0:T(8,128)(2,1)}, bf16[2048,512]{1,0:T(8,128)(2,1)}, u32[]{:S(2)}, u32[]{:S(2)}) collective-permute-start(bf16[2048,512]{1,0:T(8,128)(2,1)} %get-tuple-element.90.refs_3_.refs_1_), channel_id=1, source_target_pairs={{16,0},{24,8},{0,16},{8,24},{17,1},{25,9},{1,17},{9,25},{18,2},{26... | collective-permute-start | bytes 6291464 | tf_op jit(solution)/shard_map/ppermute | solution.py:176
  48.8 89.6 %collective-permute-start.3 = (bf16[2048,512]{1,0:T(8,128)(2,1)}, bf16[2048,512]{1,0:T(8,128)(2,1)}, u32[]{:S(2)}, u32[]{:S(2)}) collective-permute-start(bf16[2048,512]{1,0:T(8,128)(2,1)} %get-tuple-element.95.refs_3_.refs_1_), channel_id=1, source_target_pairs={{16,0},{24,8},{0,16},{8,24},{17,1},{25,9},{1,17},{9,25},{18,2},{26... | collective-permute-start | bytes 6291464 | tf_op jit(solution)/shard_map/ppermute | solution.py:176
  81.0 70.3 %copy-start.19 = (f32[3,3,1024]{2,1,0:T(4,128)S(1)}, f32[3,3,1024]{2,1,0:T(4,128)}, u32[]{:S(2)}) copy-start(f32[3,3,1024]{2,1,0:T(4,128)} %param.9) | copy-start | bytes 110596
  149.9 58.2 %collective-permute-start.4 = (bf16[1024,768]{1,0:T(8,128)(2,1)}, bf16[1024,768]{1,0:T(8,128)(2,1)S(1)}, u32[]{:S(2)}, u32[]{:S(2)}) collective-permute-start(bf16[1024,768]{1,0:T(8,128)(2,1)} %get-tuple-element.65), channel_id=1, source_target_pairs={{16,0},{24,8},{0,16},{8,24},{17,1},{25,9},{1,17},{9,25},{18,2},{26... | collective-permute-start | bytes 4718600 | tf_op jit(solution)/shard_map/ppermute | solution.py:176
  151.4 73.8 %copy-start.14 = (f32[7,1024]{1,0:T(8,128)S(1)}, f32[7,1024]{1,0:T(8,128)}, u32[]{:S(2)}) copy-start(f32[7,1024]{1,0:T(8,128)} %param.10) | copy-start | bytes 86020
  221.8 4.9 collective-permute-start.6
  230.6 168.9 %all-gather.14.cloned.1.call-start = ((), (), s32[]{:S(2)}) async-start(), calls=%async_computation.3 | async-start | bytes 7077888 | tf_op jit(solution)/shard_map/all_gather | solution.py:232
  230.9 67.5 %collective-permute-start.8 = (bf16[3,2048,256]{2,1,0:T(8,128)(2,1)S(1)}, bf16[3,2048,256]{2,1,0:T(8,128)(2,1)S(1)}, u32[]{:S(2)}, u32[]{:S(2)}) collective-permute-start(bf16[3,2048,256]{2,1,0:T(8,128)(2,1)S(1)} %copy-done.1), channel_id=1, source_target_pairs={{8,0},{0,8},{24,16},{16,24},{9,1},{1,9},{25,17},{17,25},{10,2},{2,... | collective-permute-start | bytes 9437192 | tf_op jit(solution)/shard_map/ppermute | solution.py:172
  252.2 50.1 %collective-permute-start.7 = (bf16[1024,1152]{1,0:T(8,128)(2,1)}, bf16[1024,1152]{1,0:T(8,128)(2,1)}, u32[]{:S(2)}, u32[]{:S(2)}) collective-permute-start(bf16[1024,1152]{1,0:T(8,128)(2,1)} %get-tuple-element.71), channel_id=1, source_target_pairs={{16,0},{24,8},{0,16},{8,24},{17,1},{25,9},{1,17},{9,25},{18,2},{26... | collective-permute-start | bytes 7077896 | tf_op jit(solution)/shard_map/ppermute | solution.py:176
  298.4 23.1 %copy-start.4 = (bf16[3,2048,256]{2,1,0:T(8,128)(2,1)}, bf16[3,2048,256]{2,1,0:T(8,128)(2,1)S(1)}, u32[]{:S(2)}) copy-start(bf16[3,2048,256]{2,1,0:T(8,128)(2,1)S(1)} %collective-permute-done.8.refs_2_) | copy-start | bytes 9437188
  322.4 4.7 collective-permute-start.9
  332.2 162.9 %all-gather.16.cloned.1.call-start = ((), (), s32[]{:S(2)}) async-start(), calls=%async_computation.4 | async-start | bytes 4718592 | tf_op jit(solution)/shard_map/all_gather | solution.py:232
  332.3 31.8 %collective-permute-start.11 = (bf16[3,2048,128]{2,1,0:T(8,128)(2,1)S(1)}, bf16[3,2048,128]{2,1,0:T(8,128)(2,1)S(1)}, u32[]{:S(2)}, u32[]{:S(2)}) collective-permute-start(bf16[3,2048,128]{2,1,0:T(8,128)(2,1)S(1)} %copy-done.2), channel_id=1, source_target_pairs={{8,0},{0,8},{24,16},{16,24},{9,1},{1,9},{25,17},{17,25},{10,2},{2,... | collective-permute-start | bytes 4718600 | tf_op jit(solution)/shard_map/ppermute | solution.py:172
  346.2 31.0 %collective-permute-start.10 = (bf16[1024,768]{1,0:T(8,128)(2,1)}, bf16[1024,768]{1,0:T(8,128)(2,1)S(1)}, u32[]{:S(2)}, u32[]{:S(2)}) collective-permute-start(bf16[1024,768]{1,0:T(8,128)(2,1)} %get-tuple-element.80), channel_id=1, source_target_pairs={{16,0},{24,8},{0,16},{8,24},{17,1},{25,9},{1,17},{9,25},{18,2},{26... | collective-permute-start | bytes 4718600 | tf_op jit(solution)/shard_map/ppermute | solution.py:176
  364.1 25.9 %copy-start.7 = (bf16[3,2048,128]{2,1,0:T(8,128)(2,1)}, bf16[3,2048,128]{2,1,0:T(8,128)(2,1)S(1)}, u32[]{:S(2)}) copy-start(bf16[3,2048,128]{2,1,0:T(8,128)(2,1)S(1)} %collective-permute-done.11.refs_2_) | copy-start | bytes 4718596
  390.7 4.7 collective-permute-start.12
  399.5 203.5 %all-gather.18.cloned.1.call-start = ((), (), s32[]{:S(2)}) async-start(), calls=%async_computation.5 | async-start | bytes 2359296 | tf_op jit(solution)/shard_map/all_gather | solution.py:232
  399.8 48.8 %collective-permute-start.14 = (bf16[2048,512]{1,0:T(8,128)(2,1)}, bf16[2048,512]{1,0:T(8,128)(2,1)S(1)}, u32[]{:S(2)}, u32[]{:S(2)}) collective-permute-start(bf16[2048,512]{1,0:T(8,128)(2,1)} %get-tuple-element.90.refs_3_.refs_1_), channel_id=1, source_target_pairs={{8,0},{0,8},{24,16},{16,24},{9,1},{1,9},{25,17},{17,25},{10,2},{2,... | collective-permute-start | bytes 6291464 | tf_op jit(solution)/shard_map/ppermute | solution.py:172
  402.0 93.2 %collective-permute-start.16 = (bf16[2048,512]{1,0:T(8,128)(2,1)}, bf16[2048,512]{1,0:T(8,128)(2,1)S(1)}, u32[]{:S(2)}, u32[]{:S(2)}) collective-permute-start(bf16[2048,512]{1,0:T(8,128)(2,1)} %get-tuple-element.95.refs_3_.refs_1_), channel_id=1, source_target_pairs={{8,0},{0,8},{24,16},{16,24},{9,1},{1,9},{25,17},{17,25},{10,2},{2,... | collective-permute-start | bytes 6291464 | tf_op jit(solution)/shard_map/ppermute | solution.py:172
  412.5 36.2 %collective-permute-start.13 = (bf16[1024,384]{1,0:T(8,128)(2,1)}, bf16[1024,384]{1,0:T(8,128)(2,1)S(1)}, u32[]{:S(2)}, u32[]{:S(2)}) collective-permute-start(bf16[1024,384]{1,0:T(8,128)(2,1)} %get-tuple-element.89), channel_id=1, source_target_pairs={{16,0},{24,8},{0,16},{8,24},{17,1},{25,9},{1,17},{9,25},{18,2},{26... | collective-permute-start | bytes 2359304 | tf_op jit(solution)/shard_map/ppermute | solution.py:176
  448.6 11.5 %copy-start.6 = (bf16[2048,512]{1,0:T(8,128)(2,1)}, bf16[2048,512]{1,0:T(8,128)(2,1)S(1)}, u32[]{:S(2)}) copy-start(bf16[2048,512]{1,0:T(8,128)(2,1)S(1)} %collective-permute-done.14.refs_4_.refs_2_) | copy-start | bytes 6291460
  460.8 31.2 %collective-permute-start.15 = (bf16[16,384]{1,0:T(8,128)(2,1)S(1)}, bf16[16,384]{1,0:T(8,128)(2,1)S(1)}, u32[]{:S(2)}, u32[]{:S(2)}) collective-permute-start(bf16[16,384]{1,0:T(8,128)(2,1)S(1)} %slice.54), channel_id=1, source_target_pairs={{0,8},{8,16},{16,24},{1,9},{9,17},{17,25},{2,10},{10,18},{18,26},{... | collective-permute-start | bytes 36872 | tf_op jit(solution)/shard_map/ppermute | solution.py:223
  495.1 49.3 %copy-start.5 = (bf16[2048,512]{1,0:T(8,128)(2,1)}, bf16[2048,512]{1,0:T(8,128)(2,1)S(1)}, u32[]{:S(2)}) copy-start(bf16[2048,512]{1,0:T(8,128)(2,1)S(1)} %collective-permute-done.16.refs_4_.refs_2_) | copy-start | bytes 6291460
  495.2 49.2 %collective-permute-start.18 = (bf16[2048,512]{1,0:T(8,128)(2,1)S(1)}, bf16[2048,512]{1,0:T(8,128)(2,1)}, u32[]{:S(2)}, u32[]{:S(2)}) collective-permute-start(bf16[2048,512]{1,0:T(8,128)(2,1)S(1)} %collective-permute-done.16.refs_4_.refs_2_), channel_id=1, source_target_pairs={{16,0},{24,8},{0,16},{8,24},{17,1},{25,9},{1,17},{9,25},{18,2},{26... | collective-permute-start | bytes 6291464 | tf_op jit(solution)/shard_map/ppermute | solution.py:176
  497.7 89.9 %collective-permute-start.17 = (bf16[2048,512]{1,0:T(8,128)(2,1)}, bf16[2048,512]{1,0:T(8,128)(2,1)}, u32[]{:S(2)}, u32[]{:S(2)}) collective-permute-start(bf16[2048,512]{1,0:T(8,128)(2,1)} %copy-done.6), channel_id=1, source_target_pairs={{16,0},{24,8},{0,16},{8,24},{17,1},{25,9},{1,17},{9,25},{18,2},{26... | collective-permute-start | bytes 6291464 | tf_op jit(solution)/shard_map/ppermute | solution.py:176
  (12 other events, 47.4 us)
Sparse Core Ops, SparseCore 0:
  37.6 83.5 all-gather.9
  230.7 49.2 all-gather.11
  332.4 67.0 all-gather.13
  400.9 47.9 all-gather.15
  495.3 28.7 all-gather.17

commit v3 on v2

v3 whole, which is shorter than its diff:
```python
import functools

import jax
import jax.numpy as jnp
from jax import lax
from jax.experimental import pallas as pl
from jax.experimental.pallas import tpu as pltpu
from jax.sharding import PartitionSpec as P

HALO = 16
LANES = 128
EIGHTHS = (0, 2, 4, 6, 8)
CHUNKS = len(EIGHTHS) - 1
OUT_CHUNKS = 4
VMEM = 56 * 2**20
TILE = 512
MARK = pl.BlockSpec((8, 128), lambda i: (0, 0))
MARK_SHAPE = jax.ShapeDtypeStruct((8, 128), jnp.float32)
LIGHT = pl.CostEstimate(flops=1024, bytes_accessed=1024, transcendentals=0)


def project_kernel(count, extra, *refs):
    x_ref, halo_ref = refs[:2]
    weights = refs[2 : 2 + count]
    received = refs[2 + count : 2 + count + extra]
    received_halo = refs[2 + count + extra : 2 + count + 2 * extra]
    out_ref = refs[-1]
    parts, depth, width = weights[0].shape
    tile, halo = x_ref.shape[0], halo_ref.shape[0]
    step = pl.program_id(0)

    def products(ref, sums, start, size):
        for part in range(parts):
            cut = slice(part * width, (part + 1) * width)
            total = jnp.dot(ref[:, :depth], weights[0][part], preferred_element_type=jnp.float32)
            for i in range(1, count):
                total += jnp.dot(
                    ref[:, i * depth : (i + 1) * depth],
                    weights[i][part],
                    preferred_element_type=jnp.float32,
                )
            for other in sums:
                total += other[:, cut].astype(jnp.float32)
            out_ref[pl.ds(start, size), cut] = total.astype(out_ref.dtype)

    products(x_ref, received, pl.multiple_of(step * tile, tile), tile)

    @pl.when(step == 0)
    def _():
        products(halo_ref, received_halo, out_ref.shape[0] - halo, halo)


def project(x, halo, weights, received=(), after=()):
    rows, depth = x.shape
    extra = halo.shape[0]
    columns = weights[0].shape[0] * weights[0].shape[2]
    tile = min(rows, TILE)
    whole = pl.BlockSpec(weights[0].shape, lambda i: (0, 0, 0), pipeline_mode=pl.Buffered(1))
    return pl.pallas_call(
        functools.partial(project_kernel, len(weights), len(received)),
        grid=(rows // tile,),
        in_specs=[pl.BlockSpec((tile, depth), lambda i: (i, 0))]
        + [pl.BlockSpec((extra, depth), lambda i: (0, 0))]
        + [whole] * len(weights)
        + [pl.BlockSpec((tile, columns), lambda i: (i, 0))] * len(received)
        + [pl.BlockSpec((extra, columns), lambda i: (rows // extra, 0))] * len(received)
        + [pl.BlockSpec(memory_space=pl.ANY)] * len(after),
        out_specs=pl.BlockSpec((rows + extra, columns), lambda i: (0, 0)),
        out_shape=jax.ShapeDtypeStruct((rows + extra, columns), jnp.bfloat16),
        compiler_params=pltpu.CompilerParams(vmem_limit_bytes=VMEM),
        cost_estimate=LIGHT,
        name="project",
    )(x, halo, *weights, *received, *received, *after)


def mix_kernel(feat, filt, qh, kh, vh, q, k, v, taps, out_ref, mark_ref, ext, prod):
    rows = q.shape[0]
    mark_ref[...] = jnp.zeros_like(mark_ref)
    for i, (h, b) in enumerate(((qh, q), (kh, k), (vh, v))):
        ext[i, :HALO, :] = h[...].astype(jnp.float32)
        ext[i, HALO:, :] = b[...].astype(jnp.float32)
    tile = min(rows, 128)

    def featured(i, start, size):
        total = taps[i : i + 1, :] * ext[i, pl.ds(start, size), :]
        for j in range(1, feat):
            total += taps[3 * j + i : 3 * j + i + 1, :] * ext[i, pl.ds(start - j, size), :]
        return total

    for t in range(rows // tile):
        base = HALO + t * tile
        prod[...] = featured(1, base - 8, tile + 8) * featured(2, base - 8, tile + 8)
        total = taps[3 * feat : 3 * feat + 1, :] * prod[pl.ds(8, tile), :]
        for j in range(1, filt):
            total += taps[3 * feat + j : 3 * feat + j + 1, :] * prod[pl.ds(8 - j, tile), :]
        out_ref[t * tile : (t + 1) * tile, :] = (featured(0, base, tile) * total).astype(out_ref.dtype)


def short_mix(projected, taps, feat, filt):
    rows, width = projected.shape[0] - HALO, projected.shape[1] // 3
    lanes = LANES
    steps = width // lanes

    def part(i, size, row):
        return pl.BlockSpec((size, lanes), lambda b: (row, i * steps + b))

    tile = min(rows, 128)
    return pl.pallas_call(
        functools.partial(mix_kernel, feat, filt),
        grid=(steps,),
        in_specs=[part(i, HALO, rows // HALO) for i in range(3)]
        + [part(i, rows, 0) for i in range(3)]
        + [pl.BlockSpec((taps.shape[0], lanes), lambda b: (0, b))],
        out_specs=[pl.BlockSpec((rows, lanes), lambda b: (0, b)), MARK],
        out_shape=[jax.ShapeDtypeStruct((rows, width), jnp.bfloat16), MARK_SHAPE],
        scratch_shapes=[
            pltpu.VMEM((3, HALO + rows, lanes), jnp.float32),
            pltpu.VMEM((tile + 8, lanes), jnp.float32),
        ],
        compiler_params=pltpu.CompilerParams(vmem_limit_bytes=VMEM),
        cost_estimate=LIGHT,
        name="short_mix",
    )(*[projected] * 6, taps)


def out_kernel(blocks, count, columns, order, *refs):
    gated = refs[:count]
    weights = refs[count : count + blocks * columns]
    held, out_ref = refs[count + blocks * columns : -1], refs[-1]
    per_block, _, wide = weights[0].shape
    for m in range(columns):
        cut = slice(m * wide, (m + 1) * wide)
        total = held[0][:, cut] if held else jnp.zeros((out_ref.shape[0], wide), jnp.float32)
        for b in range(blocks):
            for i in range(per_block):
                row = 0
                for ref in gated:
                    size = ref.shape[2]
                    total += jnp.dot(
                        ref[order[b] * per_block + i],
                        weights[m * blocks + b][i, row : row + size, :],
                        preferred_element_type=jnp.float32,
                    )
                    row += size
        out_ref[:, cut] = total.astype(out_ref.dtype)


def out_project(order, gated, start, weights, kind, held=()):
    chans, rows, _ = gated[0].shape
    size = sum(block.shape[2] for block in gated)
    per_block, _, wide = weights[0][0].shape
    columns, blocks = len(weights), len(weights[0])
    tile = min(rows, 256)
    cell = pl.BlockSpec((tile, columns * wide), lambda i, o: (i, 0))
    piece = pl.BlockSpec(
        (per_block, size, wide), lambda i, o: (0, start // size, 0), pipeline_mode=pl.Buffered(1)
    )
    spec = pltpu.PrefetchScalarGridSpec(
        num_scalar_prefetch=1,
        grid=(rows // tile,),
        in_specs=[pl.BlockSpec((chans, tile, block.shape[2]), lambda i, o: (0, i, 0)) for block in gated]
        + [piece] * (columns * blocks)
        + [cell] * len(held),
        out_specs=cell,
    )
    return pl.pallas_call(
        functools.partial(out_kernel, blocks, len(gated), columns),
        grid_spec=spec,
        out_shape=jax.ShapeDtypeStruct((rows, columns * wide), kind),
        compiler_params=pltpu.CompilerParams(vmem_limit_bytes=VMEM),
        cost_estimate=LIGHT,
        name="out_project",
    )(order, *gated, *[block for found in weights for block in found], *held)


def normalised(x, gain):
    values = x.astype(jnp.float32)
    squares = jnp.mean(values * values, axis=1, keepdims=True)
    return (values * lax.rsqrt(squares + 1e-06) * gain).astype(jnp.bfloat16)


def per_device(x_rows, norm_gain, in_weight, feat_filter, inner_filter, out_weight):
    tokens, model = x_rows.shape
    depth, _, chans_here = in_weight.shape
    seqs, chans = lax.axis_size("seq"), lax.axis_size("chan")
    near = 2 if seqs % 2 == 0 else 1
    far = seqs // near
    seq, chan = lax.axis_index("seq"), lax.axis_index("chan")
    e, g = seq // near, seq % near
    feat, filt = feat_filter.shape[0], inner_filter.shape[0]

    def from_near(block, k):
        pairs = [(a * near + (b + k) % near, a * near + b) for a in range(far) for b in range(near)]
        return lax.ppermute(block, "seq", pairs)

    def from_far(block, k):
        pairs = [((a + k) % far * near + b, a * near + b) for a in range(far) for b in range(near)]
        return lax.ppermute(block, "seq", pairs)

    def columns_of(rows, group):
        return jnp.concatenate(
            [
                lax.dynamic_slice_in_dim(rows, (group * near + (g + i) % near) * depth, depth, 1)
                for i in range(near)
            ],
            axis=1,
        )

    together = lax.optimization_barrier
    units = chans_here // LANES
    edges = [LANES * (units * part // 8) for part in EIGHTHS]
    cuts = [slice(a, b) for a, b in zip(edges, edges[1:])]
    first = in_weight[:, :, cuts[0]].transpose(1, 0, 2)
    in_weight, first = together((in_weight, first))
    owns = [first] + [in_weight[:, :, cut].transpose(1, 0, 2) for cut in cuts[1:]]
    weights = [[own] + [from_near(own, k) for k in range(1, near)] for own in owns]
    width = out_weight.shape[1] // OUT_CHUNKS
    rows = [out_weight[:, m * width : (m + 1) * width] for m in range(OUT_CHUNKS)]

    near_rows = [[from_near(block, k) for k in range(1, near)] for block in rows]

    share = tokens // chans
    before = lax.ppermute(
        x_rows[tokens - HALO :], "seq", [(a, a + 1) for a in range(seqs - 1)]
    )
    part = normalised(lax.dynamic_slice_in_dim(x_rows, chan * share, share, 0), norm_gain)
    pieces = [
        from_far(columns_of(part, (e - k) % far), k) for k in range(1, far)
    ]
    pieces, rows, owns, near_rows[0] = together((pieces, rows, owns, near_rows[0]))
    theirs = [lax.all_gather(piece, "chan", axis=0, tiled=True) for piece in pieces]
    before = normalised(before, norm_gain)
    theirs_before = [from_far(columns_of(before, (e - k) % far), k) for k in range(1, far)]
    mine = columns_of(normalised(x_rows, norm_gain), e)
    mine_before = columns_of(before, e)
    taps = jnp.concatenate([feat_filter.reshape(feat * 3, chans_here), inner_filter], axis=0)

    across = [[from_far(block, a) for a in range(1, far)] for block in rows]
    theirs, theirs_before, weights[0], mine, mine_before, across = together(
        (theirs, theirs_before, weights[0], mine, mine_before, across)
    )

    gated, done = [], []
    for j in range(CHUNKS):
        sums = [
            from_far(project(theirs[k], theirs_before[k], weights[j], after=done), far - 1 - k)
            for k in range(far - 1)
        ]
        projected = project(mine, mine_before, weights[j], sums)
        if j == 0:
            projected, weights[1], near_rows[1] = together((projected, weights[1], near_rows[1]))
            beyond = [
                [from_far(block, a) for a in range(1, far) for block in found] for found in near_rows[:2]
            ]
        elif j < CHUNKS - 1:
            turn = min(j - 1, 1)
            projected, weights[j + 1], beyond[turn] = together(
                (projected, weights[j + 1], beyond[turn])
            )
        else:
            projected, near_rows[2:] = together((projected, near_rows[2:]))
            beyond += [
                [from_far(block, a) for a in range(1, far) for block in found] for found in near_rows[2:]
            ]
        mixed, mark = short_mix(projected, taps[:, cuts[j]], feat, filt)
        done = [mark]
        if j > 0:
            mixed, gated[j - 1] = together((mixed, gated[j - 1]))
        gated.append(lax.all_gather(mixed, "chan", axis=0))

    order = jnp.stack(
        [(e + a) % far * near + (g + b) % near for a in range(far) for b in range(near)]
    ).astype(jnp.int32)
    blocks = []
    for m in range(OUT_CHUNKS):
        found = [rows[m]] + near_rows[m]
        for a in range(1, far):
            found += [across[m][a - 1]] + beyond[m][(a - 1) * (near - 1) : a * (near - 1)]
        blocks.append([block.reshape(-1, chans_here, block.shape[1]) for block in found])
    half = OUT_CHUNKS // 2
    sums = [
        out_project(order, gated[:-1], 0, found, jnp.float32) for found in (blocks[:half], blocks[half:])
    ]
    sums, last = together((sums, gated[-1]))
    outs = [
        out_project(order, [last], edges[CHUNKS - 1], found, jnp.bfloat16, [total])
        for found, total in zip((blocks[:half], blocks[half:]), sums)
    ]
    out = jnp.concatenate(outs, axis=1).reshape(chans, share, -1)
    got = lax.all_to_all(out, "chan", split_axis=0, concat_axis=0, tiled=True)
    return got.transpose(1, 0, 2).reshape(share, -1)


def solution(mesh):
    return jax.shard_map(
        per_device,
        mesh=mesh,
        in_specs=(
            P("seq", None),
            P(),
            P("seq", None, "chan"),
            P(None, None, "chan"),
            P(None, "chan"),
            P("seq", "chan"),
        ),
        out_specs=P(("seq", "chan"), None),
        check_vma=False,
    )
```

time: 683 us -> 696 us (1.019)
  waiting for transfers between devices: 339 us -> 372 us
  local copies, waits for them, and re-layouts: 32.7 us -> 24.3 us
  Pallas kernels: 167 us -> 159 us
  starting transfers between devices: 39 us -> 31.6 us
    ppermute x6 -> x8, waiting for transfers between devices: 150 us -> 3.97 us  [from_near(): return lax.ppermute(block, 'seq', pairs)]
    ppermute x9 -> x14, waiting for transfers between devices: 158 us -> 258 us  [from_far(): return lax.ppermute(block, 'seq', pairs)]
    ppermute x4 -> x1, waiting for transfers between devices: 30 us -> 110 us  [per_device(): lax.ppermute(x_rows[tokens - HALO:], 'seq', [(a, a + 1) for a in range(se...]
    ppermute x4 -> x1, starting transfers between devices: 13.7 us -> 3.7 us  [per_device(): lax.ppermute(x_rows[tokens - HALO:], 'seq', [(a, a + 1) for a in range(se...]
    pallas_call x4, Pallas kernels: 48.4 us -> 40 us  [out_project(): pl.pallas_call(functools.partial(out_kernel, blocks, len(gated), columns)...]
    ppermute x9 -> x14, starting transfers between devices: 15.7 us -> 18.5 us  [from_far(): return lax.ppermute(block, 'seq', pairs)]
    convert_element_type x2 -> x3, other arithmetic: 17.6 us -> 17.8 us  [normalised(): return (values * lax.rsqrt(squares + 1e-06) * gain).astype(jnp.bfloat16)]
  transfers between devices with their start and end apart: 24 -> 28, of which waited for: 16 -> 15; matrix products, arithmetic and copies ran while one was open for 8% -> 7% of each run, Pallas kernels for 20% -> 20%
where the time goes in v3:
time: 696 us; the launch traced here: 693 us
  waiting for transfers between devices  372 us (53%)
  Pallas kernels  159 us (23%)
  blocking collectives  52.9 us (8%)
  other arithmetic  39.4 us (6%)
  starting transfers between devices  31.6 us (5%)
  local copies, waits for them, and re-layouts  24.3 us (3%)
  between operations  13.5 us (2%)
    ppermute x14, waiting for transfers between devices, from_far(): return lax.ppermute(block, 'seq', pairs)  258 us
    ppermute x1, waiting for transfers between devices, per_device(): lax.ppermute(x_rows[tokens - HALO:], 'seq', [(a, a + 1) for a in range(se...  110 us
    pallas_call x8, Pallas kernels, project(): pl.pallas_call(functools.partial(project_kernel, len(weights), len(receiv...  105 us
    all_to_all x1, blocking collectives, per_device(): got = lax.all_to_all(out, 'chan', split_axis=0, concat_axis=0, tiled=True)  52.9 us
    pallas_call x4, Pallas kernels, out_project(): pl.pallas_call(functools.partial(out_kernel, blocks, len(gated), columns)...  40 us
    ppermute x14, starting transfers between devices, from_far(): return lax.ppermute(block, 'seq', pairs)  18.5 us
    convert_element_type x3, other arithmetic, normalised(): return (values * lax.rsqrt(squares + 1e-06) * gain).astype(jnp.bfloat16)  17.8 us
    pallas_call x4, Pallas kernels, short_mix(): pl.pallas_call(functools.partial(mix_kernel, feat, filt), grid=(steps,),...  14 us
  transfers between devices with their start and end apart: 28, of which 15 were waited for; matrix products, arithmetic and copies ran while one was open for 7% of the time, Pallas kernels for 20%

profile of v3, /device:TPU:0, one launch (start us, length us, event | category | flops | bytes accessed | tf_op | source)
XLA Modules:
  0.0 692.5 jit_solution(4987669662000394120)
XLA Ops:
  23.3 14.2 %collective-permute-done = bf16[128,4096]{1,0:T(8,128)(2,1)} collective-permute-done((bf16[128,4096]{1,0:T(8,128)(2,1)S(1)}, bf16[128,4096]{1,0:T(8,128)(2,1)}, u32[]{:S(2)}, u32[]{:S(2)}) %collective-permute-start) | collective-permute-done | bytes 1048608 | tf_op jit(solution)/shard_map/ppermute | solution.py:198
  37.5 4.0 collective-permute-done.1
  45.3 3.7 collective-permute-start.2
  49.0 8.0 %fusion = f32[1024]{0:T(1024)S(1)} fusion(bf16[1024,8192]{1,0:T(8,128)(2,1)} %param.6), kind=kLoop, calls=%fused_computation.2 | loop fusion | flops 25164800 | bytes 16781312 | tf_op jit(solution)/shard_map/reduce_sum | solution.py:178
  57.1 15.3 %fusion.2 = bf16[1024,8192]{1,0:T(8,128)(2,1)} fusion(bf16[1024,8192]{1,0:T(8,128)(2,1)} %param.6, f32[8192]{0:T(1024)S(1)} %copy-done.12, f32[1024]{0:T(1024)S(1)} %add_rsqrt_fusion), kind=kLoop, calls=%fused_computation.4 | loop fusion | flops 33554432 | bytes 33591296 | tf_op jit(solution)/shard_map/convert_element_type | solution.py:179
  72.3 110.3 %collective-permute-done.2 = bf16[16,8192]{1,0:T(8,128)(2,1)S(1)} collective-permute-done((bf16[16,8192]{1,0:T(8,128)(2,1)}, bf16[16,8192]{1,0:T(8,128)(2,1)S(1)}, u32[]{:S(2)}, u32[]{:S(2)}) %collective-permute-start.2) | collective-permute-done | bytes 262176 | tf_op jit(solution)/shard_map/ppermute | solution.py:223
  185.6 8.4 %constant_dynamic-slice_fusion.3 = (bf16[1024,2048]{1,0:T(8,128)(2,1)}, bf16[1024,2048]{1,0:T(8,128)(2,1)}) fusion(bf16[1024,8192]{1,0:T(8,128)(2,1)} %fusion.2, s32[]{:T(128)S(6)} %select_n.86, s32[]{:T(128)S(6)} %select_n.87), kind=kLoop, calls=%fused_computation.38 | loop fusion | bytes 16777224 | tf_op jit(solution)/shard_map/dynamic_slice | solution.py:203
  196.0 16.6 %collective-permute-done.3.refs_1_ = bf16[16,4096]{1,0:T(8,128)(2,1)S(1)} collective-permute-done((bf16[16,4096]{1,0:T(8,128)(2,1)S(1)}, bf16[16,4096]{1,0:T(8,128)(2,1)S(1)}, u32[]{:S(2)}, u32[]{:S(2)}) %collective-permute-start.3) | collective-permute-done | bytes 131104 | tf_op jit(solution)/shard_map/ppermute | solution.py:198
  214.7 7.9 %pad_maximum_fusion.refs_0_ = bf16[1024,4096]{1,0:T(8,128)(2,1)} fusion(bf16[1024,2048]{1,0:T(8,128)(2,1)} %get-tuple-element.104, bf16[1024,2048]{1,0:T(8,128)(2,1)} %get-tuple-element.103), kind=kLoop, calls=%fused_computation.5 | loop fusion | flops 16777216 | bytes 16777216 | tf_op jit(solution)/shard_map/concatenate | solution.py:201
  223.2 11.9 %collective-permute-done.6 = bf16[2048,256]{1,0:T(8,128)(2,1)} collective-permute-done((bf16[2048,256]{1,0:T(8,128)(2,1)}, bf16[2048,256]{1,0:T(8,128)(2,1)}, u32[]{:S(2)}, u32[]{:S(2)}) %collective-permute-start.6) | collective-permute-done | bytes 1048608 | tf_op jit(solution)/shard_map/ppermute | solution.py:198
  235.2 22.5 %collective-permute-done.7 = bf16[2048,256]{1,0:T(8,128)(2,1)} collective-permute-done((bf16[2048,256]{1,0:T(8,128)(2,1)}, bf16[2048,256]{1,0:T(8,128)(2,1)}, u32[]{:S(2)}, u32[]{:S(2)}) %collective-permute-start.7) | collective-permute-done | bytes 1048608 | tf_op jit(solution)/shard_map/ppermute | solution.py:198
  257.6 19.6 %collective-permute-done.8 = bf16[2048,256]{1,0:T(8,128)(2,1)} collective-permute-done((bf16[2048,256]{1,0:T(8,128)(2,1)}, bf16[2048,256]{1,0:T(8,128)(2,1)}, u32[]{:S(2)}, u32[]{:S(2)}) %collective-permute-start.8) | collective-permute-done | bytes 1048608 | tf_op jit(solution)/shard_map/ppermute | solution.py:198
  277.2 13.0 %project.8 = bf16[1040,768]{1,0:T(8,128)(2,1)} custom-call(bf16[1024,4096]{1,0:T(8,128)(2,1)} %all-gather.10.cloned.1.call-done.refs_0_, bf16[16,4096]{1,0:T(8,128)(2,1)} %copy-done.11, bf16[3,2048,256]{2,1,0:T(8,128)(2,1)} %slice_bitcast_fusion.3.refs_2_, bf16[3,2048,256]{2,1,0:T(8,128)(2,1)} %collective-permute-done.4.refs_3_), custom_call_target="tpu_custom_call" | custom-call | flops 1024 | bytes 1024 | tf_op jit(solution)/shard_map/project/pallas_call | solution.py:59
  292.9 31.7 %collective-permute-done.9.refs_4_.refs_5_ = bf16[1040,768]{1,0:T(8,128)(2,1)} collective-permute-done((bf16[1040,768]{1,0:T(8,128)(2,1)}, bf16[1040,768]{1,0:T(8,128)(2,1)}, u32[]{:S(2)}, u32[]{:S(2)}) %collective-permute-start.9) | collective-permute-done | bytes 1597472 | tf_op jit(solution)/shard_map/ppermute | solution.py:198
  324.5 13.2 %project.9.qh.kh.vh.q.k.v = bf16[1040,768]{1,0:T(8,128)(2,1)} custom-call(bf16[1024,4096]{1,0:T(8,128)(2,1)} %pad_maximum_fusion.refs_0_, bf16[16,4096]{1,0:T(8,128)(2,1)} %pad_maximum_fusion.4.refs_1_, bf16[3,2048,256]{2,1,0:T(8,128)(2,1)} %slice_bitcast_fusion.3.refs_2_, bf16[3,2048,256]{2,1,0:T(8,128)(2,1)} %collective-permute-done.4.refs_3_, ...), custom_call_target="tpu_custom_call" | custom-call | flops 1024 | bytes 1024 | tf_op jit(solution)/shard_map/project/pallas_call | solution.py:59
  342.6 13.0 %project.10 = bf16[1040,768]{1,0:T(8,128)(2,1)} custom-call(bf16[1024,4096]{1,0:T(8,128)(2,1)} %all-gather.10.cloned.1.call-done.refs_0_, bf16[16,4096]{1,0:T(8,128)(2,1)} %copy-done.11, bf16[3,2048,256]{2,1,0:T(8,128)(2,1)} %get-tuple-element.67.refs_2_, bf16[3,2048,256]{2,1,0:T(8,128)(2,1)} %collective-permute-done.10.refs_3_, ...), custom_call_target="tpu_custom_call" | custom-call | flops 1024 | bytes 1024 | tf_op jit(solution)/shard_map/project/pallas_call | solution.py:59
  357.6 36.0 %collective-permute-done.12.refs_4_.refs_5_ = bf16[1040,768]{1,0:T(8,128)(2,1)S(1)} collective-permute-done((bf16[1040,768]{1,0:T(8,128)(2,1)}, bf16[1040,768]{1,0:T(8,128)(2,1)S(1)}, u32[]{:S(2)}, u32[]{:S(2)}) %collective-permute-start.12) | collective-permute-done | bytes 1597472 | tf_op jit(solution)/shard_map/ppermute | solution.py:198
  394.8 13.2 %project.11.qh.kh.vh.q.k.v = bf16[1040,768]{1,0:T(8,128)(2,1)} custom-call(bf16[1024,4096]{1,0:T(8,128)(2,1)} %pad_maximum_fusion.refs_0_, bf16[16,4096]{1,0:T(8,128)(2,1)} %pad_maximum_fusion.4.refs_1_, bf16[3,2048,256]{2,1,0:T(8,128)(2,1)} %get-tuple-element.67.refs_2_, bf16[3,2048,256]{2,1,0:T(8,128)(2,1)} %collective-permute-done.10.refs_3_, ...), custom_call_target="tpu_custom_call" | custom-call | flops 1024 | bytes 1024 | tf_op jit(solution)/shard_map/project/pallas_call | solution.py:59
  415.6 13.0 %project.12 = bf16[1040,768]{1,0:T(8,128)(2,1)} custom-call(bf16[1024,4096]{1,0:T(8,128)(2,1)} %all-gather.10.cloned.1.call-done.refs_0_, bf16[16,4096]{1,0:T(8,128)(2,1)} %copy-done.11, bf16[3,2048,256]{2,1,0:T(8,128)(2,1)} %get-tuple-element.76.refs_2_, bf16[3,2048,256]{2,1,0:T(8,128)(2,1)} %collective-permute-done.13.refs_3_, ...), custom_call_target="tpu_custom_call" | custom-call | flops 1024 | bytes 1024 | tf_op jit(solution)/shard_map/project/pallas_call | solution.py:59
  430.6 36.0 %collective-permute-done.15.refs_4_.refs_5_ = bf16[1040,768]{1,0:T(8,128)(2,1)S(1)} collective-permute-done((bf16[1040,768]{1,0:T(8,128)(2,1)}, bf16[1040,768]{1,0:T(8,128)(2,1)S(1)}, u32[]{:S(2)}, u32[]{:S(2)}) %collective-permute-start.15) | collective-permute-done | bytes 1597472 | tf_op jit(solution)/shard_map/ppermute | solution.py:198
  467.8 13.3 %project.13.qh.kh.vh.q.k.v = bf16[1040,768]{1,0:T(8,128)(2,1)} custom-call(bf16[1024,4096]{1,0:T(8,128)(2,1)} %pad_maximum_fusion.refs_0_, bf16[16,4096]{1,0:T(8,128)(2,1)} %pad_maximum_fusion.4.refs_1_, bf16[3,2048,256]{2,1,0:T(8,128)(2,1)} %get-tuple-element.76.refs_2_, bf16[3,2048,256]{2,1,0:T(8,128)(2,1)} %collective-permute-done.13.refs_3_, ...), custom_call_target="tpu_custom_call" | custom-call | flops 1024 | bytes 1024 | tf_op jit(solution)/shard_map/project/pallas_call | solution.py:59
  486.8 13.0 %project.14 = bf16[1040,768]{1,0:T(8,128)(2,1)} custom-call(bf16[1024,4096]{1,0:T(8,128)(2,1)} %all-gather.10.cloned.1.call-done.refs_0_, bf16[16,4096]{1,0:T(8,128)(2,1)} %copy-done.11, bf16[3,2048,256]{2,1,0:T(8,128)(2,1)} %copy-done, bf16[3,2048,256]{2,1,0:T(8,128)(2,1)} %copy-done.2, f32[8,128]{1,0:T(8,128)} %get-tuple-element.86.refs_4_), custom_call_target="tpu_custom_call" | custom-call | flops 1024 | bytes 1024 | tf_op jit(solution)/shard_map/project/pallas_call | solution.py:59
  502.8 28.0 %collective-permute-done.18.refs_4_.refs_5_ = bf16[1040,768]{1,0:T(8,128)(2,1)S(1)} collective-permute-done((bf16[1040,768]{1,0:T(8,128)(2,1)}, bf16[1040,768]{1,0:T(8,128)(2,1)S(1)}, u32[]{:S(2)}, u32[]{:S(2)}) %collective-permute-start.18) | collective-permute-done | bytes 1597472 | tf_op jit(solution)/shard_map/ppermute | solution.py:198
  531.9 13.3 %project.15.qh.kh.vh.q.k.v = bf16[1040,768]{1,0:T(8,128)(2,1)} custom-call(bf16[1024,4096]{1,0:T(8,128)(2,1)} %pad_maximum_fusion.refs_0_, bf16[16,4096]{1,0:T(8,128)(2,1)} %pad_maximum_fusion.4.refs_1_, bf16[3,2048,256]{2,1,0:T(8,128)(2,1)} %copy-done, bf16[3,2048,256]{2,1,0:T(8,128)(2,1)} %copy-done.2, bf16[1040,768]{1,0:T(8,128)(2,1)} %copy-done.3, ...), custom_call_target="tpu_custom_call" | custom-call | flops 1024 | bytes 1024 | tf_op jit(solution)/shard_map/project/pallas_call | solution.py:59
  545.2 4.0 short_mix.7
  551.9 23.5 %collective-permute-done.21 = bf16[2048,256]{1,0:T(8,128)(2,1)S(1)} collective-permute-done((bf16[2048,256]{1,0:T(8,128)(2,1)S(1)}, bf16[2048,256]{1,0:T(8,128)(2,1)S(1)}, u32[]{:S(2)}, u32[]{:S(2)}) %collective-permute-start.21) | collective-permute-done | bytes 1048608 | tf_op jit(solution)/shard_map/ppermute | solution.py:198
  575.4 14.7 %collective-permute-done.22 = bf16[2048,256]{1,0:T(8,128)(2,1)} collective-permute-done((bf16[2048,256]{1,0:T(8,128)(2,1)S(1)}, bf16[2048,256]{1,0:T(8,128)(2,1)}, u32[]{:S(2)}, u32[]{:S(2)}) %collective-permute-start.22) | collective-permute-done | bytes 1048608 | tf_op jit(solution)/shard_map/ppermute | solution.py:198
  590.0 12.8 %out_project.5.refs_9_ = f32[1024,512]{1,0:T(8,128)} custom-call(s32[4]{0:T(128)} %pad_add_fusion.order, bf16[8,1024,256]{2,1,0:T(8,128)(2,1)} %bitcast.36, bf16[8,1024,256]{2,1,0:T(8,128)(2,1)} %bitcast.38, bf16[8,1024,256]{2,1,0:T(8,128)(2,1)} %bitcast.40, bf16[2,1024,256]{2,1,0:T(8,128)(2,1)} %bitcast.19.refs_3_.refs_1_, bf16[2,1024,256]{2,1,0:T(8,128)(2,1)} %bitcast.46, ...), custom_call_target="tpu_custom_call" | custom-call | flops 1024 | bytes 1024 | tf_op jit(solution)/shard_map/out_project/pallas_call | solution.py:166
  602.8 12.7 %out_project.4.refs_9_ = f32[1024,512]{1,0:T(8,128)} custom-call(s32[4]{0:T(128)} %pad_add_fusion.order, bf16[8,1024,256]{2,1,0:T(8,128)(2,1)} %bitcast.37, bf16[8,1024,256]{2,1,0:T(8,128)(2,1)} %bitcast.39, bf16[8,1024,256]{2,1,0:T(8,128)(2,1)} %bitcast.41, bf16[2,1024,256]{2,1,0:T(8,128)(2,1)} %bitcast.11.refs_3_.refs_1_, ...), custom_call_target="tpu_custom_call" | custom-call | flops 1024 | bytes 1024 | tf_op jit(solution)/shard_map/out_project/pallas_call | solution.py:166
  615.5 7.2 %out_project.6 = bf16[1024,512]{1,0:T(8,128)(2,1)} custom-call(s32[4]{0:T(128)} %pad_add_fusion.order, bf16[8,1024,256]{2,1,0:T(8,128)(2,1)} %bitcast.42, bf16[2,1024,256]{2,1,0:T(8,128)(2,1)} %bitcast.11.refs_3_.refs_1_, bf16[2,1024,256]{2,1,0:T(8,128)(2,1)} %bitcast.12.refs_4_.refs_2_, bf16[2,1024,256]{2,1,0:T(8,128)(2,1)} %bitcast.13.refs_5_.refs_3_, ...), custom_call_target="tpu_custom_call" | custom-call | flops 1024 | bytes 1024 | tf_op jit(solution)/shard_map/out_project/pallas_call | solution.py:166
  622.7 7.3 %out_project.7 = bf16[1024,512]{1,0:T(8,128)(2,1)} custom-call(s32[4]{0:T(128)} %pad_add_fusion.order, bf16[8,1024,256]{2,1,0:T(8,128)(2,1)} %bitcast.43, bf16[2,1024,256]{2,1,0:T(8,128)(2,1)} %bitcast.19.refs_3_.refs_1_, bf16[2,1024,256]{2,1,0:T(8,128)(2,1)} %bitcast.47, bf16[2,1024,256]{2,1,0:T(8,128)(2,1)} %bitcast.21.refs_5_.refs_3_, ...), custom_call_target="tpu_custom_call" | custom-call | flops 1024 | bytes 1024 | tf_op jit(solution)/shard_map/out_project/pallas_call | solution.py:166
  631.5 52.9 %all_to_all.5 = bf16[8,128,1024]{2,1,0:T(8,128)(2,1)S(1)} all-to-all(bf16[8,128,1024]{2,1,0:T(8,128)(2,1)S(1)} %bitcast.44), channel_id=1, replica_groups=mesh['seq'=4,'chan'=8] {'chan'}, dimensions={0} | all-to-all | bytes 4194304 | tf_op jit(solution)/shard_map/all_to_all | solution.py:290
  (101 shorter events, 65.1 us)
Async XLA Ops:
  6.5 270.7 %all-gather.10.cloned.1.call-start = ((), (), s32[]{:S(2)}) async-start(), calls=%async_computation.1 | async-start | bytes 9437184 | tf_op jit(solution)/shard_map/all_gather | solution.py:231
  11.2 26.3 %collective-permute-start = (bf16[128,4096]{1,0:T(8,128)(2,1)S(1)}, bf16[128,4096]{1,0:T(8,128)(2,1)}, u32[]{:S(2)}, u32[]{:S(2)}) collective-permute-start(bf16[128,4096]{1,0:T(8,128)(2,1)S(1)} %pad_maximum_fusion.2), channel_id=1, source_target_pairs={{16,0},{24,8},{0,16},{8,24},{17,1},{25,9},{1,17},{9,25},{18,2},{26... | collective-permute-start | bytes 3145736 | tf_op jit(solution)/shard_map/ppermute | solution.py:198
  16.4 25.0 %collective-permute-start.1 = (bf16[2048,256]{1,0:T(8,128)(2,1)}, bf16[2048,256]{1,0:T(8,128)(2,1)}, u32[]{:S(2)}, u32[]{:S(2)}) collective-permute-start(bf16[2048,256]{1,0:T(8,128)(2,1)} %get-tuple-element.57), channel_id=1, source_target_pairs={{8,0},{0,8},{24,16},{16,24},{9,1},{1,9},{25,17},{17,25},{10,2},{2,... | collective-permute-start | bytes 3145736 | tf_op jit(solution)/shard_map/ppermute | solution.py:194
  23.3 390.9 %copy-start = (bf16[3,2048,256]{2,1,0:T(8,128)(2,1)}, bf16[3,2048,256]{2,1,0:T(8,128)(2,1)S(1)}, u32[]{:S(2)}) copy-start(bf16[3,2048,256]{2,1,0:T(8,128)(2,1)S(1)} %get-tuple-element.84.refs_2_) | copy-start | bytes 9437188
  41.5 372.7 %all-gather.12.cloned.1.call-start = ((), (), s32[]{:S(2)}) async-start(), calls=%async_computation.2 | async-start | bytes 4718592 | tf_op jit(solution)/shard_map/all_gather | solution.py:269
  41.5 235.7 %collective-permute-start.4 = (bf16[3,2048,256]{2,1,0:T(8,128)(2,1)}, bf16[3,2048,256]{2,1,0:T(8,128)(2,1)}, u32[]{:S(2)}, u32[]{:S(2)}) collective-permute-start(bf16[3,2048,256]{2,1,0:T(8,128)(2,1)} %slice_bitcast_fusion.3.refs_2_), channel_id=1, source_target_pairs={{8,0},{0,8},{24,16},{16,24},{9,1},{1,9},{25,17},{17,25},{10,2},{2,... | collective-permute-start | bytes 9437192 | tf_op jit(solution)/shard_map/ppermute | solution.py:194
  43.1 294.7 %collective-permute-start.10 = (bf16[3,2048,256]{2,1,0:T(8,128)(2,1)}, bf16[3,2048,256]{2,1,0:T(8,128)(2,1)}, u32[]{:S(2)}, u32[]{:S(2)}) collective-permute-start(bf16[3,2048,256]{2,1,0:T(8,128)(2,1)} %get-tuple-element.67.refs_2_), channel_id=1, source_target_pairs={{8,0},{0,8},{24,16},{16,24},{9,1},{1,9},{25,17},{17,25},{10,2},{2,... | collective-permute-start | bytes 9437192 | tf_op jit(solution)/shard_map/ppermute | solution.py:194
  45.3 137.3 %collective-permute-start.2 = (bf16[16,8192]{1,0:T(8,128)(2,1)}, bf16[16,8192]{1,0:T(8,128)(2,1)S(1)}, u32[]{:S(2)}, u32[]{:S(2)}) collective-permute-start(bf16[16,8192]{1,0:T(8,128)(2,1)} %slice.47), channel_id=1, source_target_pairs={{0,8},{8,16},{16,24},{1,9},{9,17},{17,25},{2,10},{10,18},{18,26},{... | collective-permute-start | bytes 786440 | tf_op jit(solution)/shard_map/ppermute | solution.py:223
  182.9 31.7 %collective-permute-start.5 = (bf16[2048,256]{1,0:T(8,128)(2,1)}, bf16[2048,256]{1,0:T(8,128)(2,1)}, u32[]{:S(2)}, u32[]{:S(2)}) collective-permute-start(bf16[2048,256]{1,0:T(8,128)(2,1)} %get-tuple-element.57), channel_id=1, source_target_pairs={{16,0},{24,8},{0,16},{8,24},{17,1},{25,9},{1,17},{9,25},{18,2},{26... | collective-permute-start | bytes 3145736 | tf_op jit(solution)/shard_map/ppermute | solution.py:198
  185.5 27.1 %collective-permute-start.3 = (bf16[16,4096]{1,0:T(8,128)(2,1)S(1)}, bf16[16,4096]{1,0:T(8,128)(2,1)S(1)}, u32[]{:S(2)}, u32[]{:S(2)}) collective-permute-start(bf16[16,4096]{1,0:T(8,128)(2,1)S(1)} %pad_maximum_fusion.3), channel_id=1, source_target_pairs={{16,0},{24,8},{0,16},{8,24},{17,1},{25,9},{1,17},{9,25},{18,2},{26... | collective-permute-start | bytes 393224 | tf_op jit(solution)/shard_map/ppermute | solution.py:198
  194.0 41.1 %collective-permute-start.6 = (bf16[2048,256]{1,0:T(8,128)(2,1)}, bf16[2048,256]{1,0:T(8,128)(2,1)}, u32[]{:S(2)}, u32[]{:S(2)}) collective-permute-start(bf16[2048,256]{1,0:T(8,128)(2,1)} %get-tuple-element.58), channel_id=1, source_target_pairs={{16,0},{24,8},{0,16},{8,24},{17,1},{25,9},{1,17},{9,25},{18,2},{26... | collective-permute-start | bytes 3145736 | tf_op jit(solution)/shard_map/ppermute | solution.py:198
  212.6 45.0 %collective-permute-start.7 = (bf16[2048,256]{1,0:T(8,128)(2,1)}, bf16[2048,256]{1,0:T(8,128)(2,1)}, u32[]{:S(2)}, u32[]{:S(2)}) collective-permute-start(bf16[2048,256]{1,0:T(8,128)(2,1)} %get-tuple-element.59), channel_id=1, source_target_pairs={{16,0},{24,8},{0,16},{8,24},{17,1},{25,9},{1,17},{9,25},{18,2},{26... | collective-permute-start | bytes 3145736 | tf_op jit(solution)/shard_map/ppermute | solution.py:198
  214.6 62.6 %collective-permute-start.8 = (bf16[2048,256]{1,0:T(8,128)(2,1)}, bf16[2048,256]{1,0:T(8,128)(2,1)}, u32[]{:S(2)}, u32[]{:S(2)}) collective-permute-start(bf16[2048,256]{1,0:T(8,128)(2,1)} %get-tuple-element.60), channel_id=1, source_target_pairs={{16,0},{24,8},{0,16},{8,24},{17,1},{25,9},{1,17},{9,25},{18,2},{26... | collective-permute-start | bytes 3145736 | tf_op jit(solution)/shard_map/ppermute | solution.py:198
  223.2 69.0 %copy-start.13 = (f32[3,3,1024]{2,1,0:T(4,128)S(1)}, f32[3,3,1024]{2,1,0:T(4,128)}, u32[]{:S(2)}) copy-start(f32[3,3,1024]{2,1,0:T(4,128)} %param.9) | copy-start | bytes 110596
  223.2 69.0 %copy-start.14 = (f32[7,1024]{1,0:T(8,128)S(1)}, f32[7,1024]{1,0:T(8,128)}, u32[]{:S(2)}) copy-start(f32[7,1024]{1,0:T(8,128)} %param.10) | copy-start | bytes 86020
  290.2 34.3 %collective-permute-start.9 = (bf16[1040,768]{1,0:T(8,128)(2,1)}, bf16[1040,768]{1,0:T(8,128)(2,1)}, u32[]{:S(2)}, u32[]{:S(2)}) collective-permute-start(bf16[1040,768]{1,0:T(8,128)(2,1)} %project.8), channel_id=1, source_target_pairs={{16,0},{24,8},{0,16},{8,24},{17,1},{25,9},{1,17},{9,25},{18,2},{26... | collective-permute-start | bytes 4792328 | tf_op jit(solution)/shard_map/ppermute | solution.py:198
  291.9 45.9 %collective-permute-start.11 = (bf16[2048,256]{1,0:T(8,128)(2,1)}, bf16[2048,256]{1,0:T(8,128)(2,1)}, u32[]{:S(2)}, u32[]{:S(2)}) collective-permute-start(bf16[2048,256]{1,0:T(8,128)(2,1)} %get-tuple-element.58), channel_id=1, source_target_pairs={{8,0},{0,8},{24,16},{16,24},{9,1},{1,9},{25,17},{17,25},{10,2},{2,... | collective-permute-start | bytes 3145736 | tf_op jit(solution)/shard_map/ppermute | solution.py:194
  341.2 145.2 %all-gather.14.cloned.1.call-start = ((), (), s32[]{:S(2)}) async-start(), calls=%async_computation.3 | async-start | bytes 4718592 | tf_op jit(solution)/shard_map/all_gather | solution.py:269
  341.4 69.4 %collective-permute-start.13 = (bf16[3,2048,256]{2,1,0:T(8,128)(2,1)}, bf16[3,2048,256]{2,1,0:T(8,128)(2,1)}, u32[]{:S(2)}, u32[]{:S(2)}) collective-permute-start(bf16[3,2048,256]{2,1,0:T(8,128)(2,1)} %get-tuple-element.76.refs_2_), channel_id=1, source_target_pairs={{8,0},{0,8},{24,16},{16,24},{9,1},{1,9},{25,17},{17,25},{10,2},{2,... | collective-permute-start | bytes 9437192 | tf_op jit(solution)/shard_map/ppermute | solution.py:194
  355.6 38.1 %collective-permute-start.12 = (bf16[1040,768]{1,0:T(8,128)(2,1)}, bf16[1040,768]{1,0:T(8,128)(2,1)S(1)}, u32[]{:S(2)}, u32[]{:S(2)}) collective-permute-start(bf16[1040,768]{1,0:T(8,128)(2,1)} %project.10), channel_id=1, source_target_pairs={{16,0},{24,8},{0,16},{8,24},{17,1},{25,9},{1,17},{9,25},{18,2},{26... | collective-permute-start | bytes 4792328 | tf_op jit(solution)/shard_map/ppermute | solution.py:198
  356.1 54.7 %collective-permute-start.14 = (bf16[2048,256]{1,0:T(8,128)(2,1)}, bf16[2048,256]{1,0:T(8,128)(2,1)}, u32[]{:S(2)}, u32[]{:S(2)}) collective-permute-start(bf16[2048,256]{1,0:T(8,128)(2,1)} %collective-permute-done.1), channel_id=1, source_target_pairs={{16,0},{24,8},{0,16},{8,24},{17,1},{25,9},{1,17},{9,25},{18,2},{26... | collective-permute-start | bytes 3145736 | tf_op jit(solution)/shard_map/ppermute | solution.py:198
  414.2 135.0 %all-gather.16.cloned.1.call-start = ((), (), s32[]{:S(2)}) async-start(), calls=%async_computation.4 | async-start | bytes 4718592 | tf_op jit(solution)/shard_map/all_gather | solution.py:269
  414.2 66.9 %collective-permute-start.16 = (bf16[3,2048,256]{2,1,0:T(8,128)(2,1)S(1)}, bf16[3,2048,256]{2,1,0:T(8,128)(2,1)S(1)}, u32[]{:S(2)}, u32[]{:S(2)}) collective-permute-start(bf16[3,2048,256]{2,1,0:T(8,128)(2,1)S(1)} %get-tuple-element.84.refs_2_), channel_id=1, source_target_pairs={{8,0},{0,8},{24,16},{16,24},{9,1},{1,9},{25,17},{17,25},{10,2},{2,... | collective-permute-start | bytes 9437192 | tf_op jit(solution)/shard_map/ppermute | solution.py:194
  428.6 38.1 %collective-permute-start.15 = (bf16[1040,768]{1,0:T(8,128)(2,1)}, bf16[1040,768]{1,0:T(8,128)(2,1)S(1)}, u32[]{:S(2)}, u32[]{:S(2)}) collective-permute-start(bf16[1040,768]{1,0:T(8,128)(2,1)} %project.12), channel_id=1, source_target_pairs={{16,0},{24,8},{0,16},{8,24},{17,1},{25,9},{1,17},{9,25},{18,2},{26... | collective-permute-start | bytes 4792328 | tf_op jit(solution)/shard_map/ppermute | solution.py:198
  429.8 53.2 %collective-permute-start.17 = (bf16[2048,256]{1,0:T(8,128)(2,1)}, bf16[2048,256]{1,0:T(8,128)(2,1)}, u32[]{:S(2)}, u32[]{:S(2)}) collective-permute-start(bf16[2048,256]{1,0:T(8,128)(2,1)} %collective-permute-done.11), channel_id=1, source_target_pairs={{16,0},{24,8},{0,16},{8,24},{17,1},{25,9},{1,17},{9,25},{18,2},{26... | collective-permute-start | bytes 3145736 | tf_op jit(solution)/shard_map/ppermute | solution.py:198
  486.4 129.2 %all-gather.18.cloned.1.call-start = ((), (), s32[]{:S(2)}) async-start(), calls=%async_computation.5 | async-start | bytes 4718592 | tf_op jit(solution)/shard_map/all_gather | solution.py:269
  499.8 30.9 %collective-permute-start.18 = (bf16[1040,768]{1,0:T(8,128)(2,1)}, bf16[1040,768]{1,0:T(8,128)(2,1)S(1)}, u32[]{:S(2)}, u32[]{:S(2)}) collective-permute-start(bf16[1040,768]{1,0:T(8,128)(2,1)} %project.14), channel_id=1, source_target_pairs={{16,0},{24,8},{0,16},{8,24},{17,1},{25,9},{1,17},{9,25},{18,2},{26... | collective-permute-start | bytes 4792328 | tf_op jit(solution)/shard_map/ppermute | solution.py:198
  500.7 44.4 %collective-permute-start.19 = (bf16[2048,256]{1,0:T(8,128)(2,1)}, bf16[2048,256]{1,0:T(8,128)(2,1)S(1)}, u32[]{:S(2)}, u32[]{:S(2)}) collective-permute-start(bf16[2048,256]{1,0:T(8,128)(2,1)} %get-tuple-element.59), channel_id=1, source_target_pairs={{8,0},{0,8},{24,16},{16,24},{9,1},{1,9},{25,17},{17,25},{10,2},{2,... | collective-permute-start | bytes 3145736 | tf_op jit(solution)/shard_map/ppermute | solution.py:194
  501.2 44.0 %collective-permute-start.20 = (bf16[2048,256]{1,0:T(8,128)(2,1)}, bf16[2048,256]{1,0:T(8,128)(2,1)S(1)}, u32[]{:S(2)}, u32[]{:S(2)}) collective-permute-start(bf16[2048,256]{1,0:T(8,128)(2,1)} %get-tuple-element.60), channel_id=1, source_target_pairs={{8,0},{0,8},{24,16},{16,24},{9,1},{1,9},{25,17},{17,25},{10,2},{2,... | collective-permute-start | bytes 3145736 | tf_op jit(solution)/shard_map/ppermute | solution.py:194
  549.2 26.2 %collective-permute-start.21 = (bf16[2048,256]{1,0:T(8,128)(2,1)S(1)}, bf16[2048,256]{1,0:T(8,128)(2,1)S(1)}, u32[]{:S(2)}, u32[]{:S(2)}) collective-permute-start(bf16[2048,256]{1,0:T(8,128)(2,1)S(1)} %collective-permute-done.19), channel_id=1, source_target_pairs={{16,0},{24,8},{0,16},{8,24},{17,1},{25,9},{1,17},{9,25},{18,2},{26... | collective-permute-start | bytes 3145736 | tf_op jit(solution)/shard_map/ppermute | solution.py:198
  549.9 40.1 %collective-permute-start.22 = (bf16[2048,256]{1,0:T(8,128)(2,1)S(1)}, bf16[2048,256]{1,0:T(8,128)(2,1)}, u32[]{:S(2)}, u32[]{:S(2)}) collective-permute-start(bf16[2048,256]{1,0:T(8,128)(2,1)S(1)} %collective-permute-done.20), channel_id=1, source_target_pairs={{16,0},{24,8},{0,16},{8,24},{17,1},{25,9},{1,17},{9,25},{18,2},{26... | collective-permute-start | bytes 3145736 | tf_op jit(solution)/shard_map/ppermute | solution.py:198
  575.4 14.7 %copy-start.8 = (bf16[2048,256]{1,0:T(8,128)(2,1)}, bf16[2048,256]{1,0:T(8,128)(2,1)S(1)}, u32[]{:S(2)}) copy-start(bf16[2048,256]{1,0:T(8,128)(2,1)S(1)} %collective-permute-done.21) | copy-start | bytes 3145732
  (11 other events, 55.6 us)
Sparse Core Ops, SparseCore 0:
  41.6 82.3 all-gather.9
  341.3 47.0 all-gather.11
  414.3 47.3 all-gather.13
  486.5 46.3 all-gather.15
  549.3 45.8 all-gather.17

commit v4 on v3

--- a/solution.py
+++ b/solution.py
@@ -13,7 +13,6 @@
 CHUNKS = len(EIGHTHS) - 1
 OUT_CHUNKS = 4
 VMEM = 56 * 2**20
-TILE = 512
 MARK = pl.BlockSpec((8, 128), lambda i: (0, 0))
 MARK_SHAPE = jax.ShapeDtypeStruct((8, 128), jnp.float32)
 LIGHT = pl.CostEstimate(flops=1024, bytes_accessed=1024, transcendentals=0)
@@ -23,54 +22,62 @@
     x_ref, halo_ref = refs[:2]
     weights = refs[2 : 2 + count]
     received = refs[2 + count : 2 + count + extra]
-    received_halo = refs[2 + count + extra : 2 + count + 2 * extra]
-    out_ref = refs[-1]
-    parts, depth, width = weights[0].shape
-    tile, halo = x_ref.shape[0], halo_ref.shape[0]
-    step = pl.program_id(0)
-
-    def products(ref, sums, start, size):
-        for part in range(parts):
-            cut = slice(part * width, (part + 1) * width)
-            total = jnp.dot(ref[:, :depth], weights[0][part], preferred_element_type=jnp.float32)
-            for i in range(1, count):
-                total += jnp.dot(
-                    ref[:, i * depth : (i + 1) * depth],
-                    weights[i][part],
-                    preferred_element_type=jnp.float32,
-                )
-            for other in sums:
-                total += other[:, cut].astype(jnp.float32)
-            out_ref[pl.ds(start, size), cut] = total.astype(out_ref.dtype)
-
-    products(x_ref, received, pl.multiple_of(step * tile, tile), tile)
-
-    @pl.when(step == 0)
-    def _():
-        products(halo_ref, received_halo, out_ref.shape[0] - halo, halo)
+    out_ref, total = refs[-2:]
+    parts, _, width = weights[0].shape
+    step, steps = pl.program_id(0), pl.num_programs(0)
+    per_weight = steps // count
+    lhs = jnp.concatenate([x_ref[...], halo_ref[...]], axis=0)
+    for i, weight in enumerate(weights):
+
+        @pl.when(step // per_weight == i)
+        def _(weight=weight):
+            for part in range(parts):
+                cut = slice(part * width, (part + 1) * width)
+                product = jnp.dot(lhs, weight[part], preferred_element_type=jnp.float32)
+
+                @pl.when(step == 0)
+                def _():
+                    total[:, cut] = product
+
+                @pl.when((step > 0) & (step < steps - 1))
+                def _():
+                    total[:, cut] += product
+
+                @pl.when(step == steps - 1)
+                def _():
+                    value = total[:, cut] + product
+                    for ref in received:
+                        value += ref[:, cut].astype(jnp.float32)
+                    out_ref[:, cut] = value.astype(out_ref.dtype)
 
 
 def project(x, halo, weights, received=(), after=()):
     rows, depth = x.shape
     extra = halo.shape[0]
-    columns = weights[0].shape[0] * weights[0].shape[2]
-    tile = min(rows, TILE)
-    whole = pl.BlockSpec(weights[0].shape, lambda i: (0, 0, 0), pipeline_mode=pl.Buffered(1))
+    parts, weight_depth, width = weights[0].shape
+    columns = parts * width
+    slab = weight_depth // 2
+    steps = depth // slab
+
+    def weight_spec(i):
+        return pl.BlockSpec((parts, slab, width), lambda k: (0, jnp.clip(k - 2 * i, 0, 1), 0))
+
+    result = pl.BlockSpec((rows + extra, columns), lambda k: (0, 0))
     return pl.pallas_call(
         functools.partial(project_kernel, len(weights), len(received)),
-        grid=(rows // tile,),
-        in_specs=[pl.BlockSpec((tile, depth), lambda i: (i, 0))]
-        + [pl.BlockSpec((extra, depth), lambda i: (0, 0))]
-        + [whole] * len(weights)
-        + [pl.BlockSpec((tile, columns), lambda i: (i, 0))] * len(received)
-        + [pl.BlockSpec((extra, columns), lambda i: (rows // extra, 0))] * len(received)
+        grid=(steps,),
+        in_specs=[pl.BlockSpec((rows, slab), lambda k: (0, k))]
+        + [pl.BlockSpec((extra, slab), lambda k: (0, k))]
+        + [weight_spec(i) for i in range(len(weights))]
+        + [result] * len(received)
         + [pl.BlockSpec(memory_space=pl.ANY)] * len(after),
-        out_specs=pl.BlockSpec((rows + extra, columns), lambda i: (0, 0)),
+        out_specs=result,
         out_shape=jax.ShapeDtypeStruct((rows + extra, columns), jnp.bfloat16),
+        scratch_shapes=[pltpu.VMEM((rows + extra, columns), jnp.float32)],
         compiler_params=pltpu.CompilerParams(vmem_limit_bytes=VMEM),
         cost_estimate=LIGHT,
         name="project",
-    )(x, halo, *weights, *received, *received, *after)
+    )(x, halo, *weights, *received, *after)
 
 
 def mix_kernel(feat, filt, qh, kh, vh, q, k, v, taps, out_ref, mark_ref, ext, prod):
@@ -123,26 +130,32 @@
     )(*[projected] * 6, taps)
 
 
-def out_kernel(blocks, count, columns, order, *refs):
+def out_kernel(blocks, columns, count, order, *refs):
     gated = refs[:count]
-    weights = refs[count : count + blocks * columns]
-    held, out_ref = refs[count + blocks * columns : -1], refs[-1]
+    weights = refs[count : count + columns * blocks]
+    held, (out_ref, total) = refs[count + columns * blocks : -2], refs[-2:]
     per_block, _, wide = weights[0].shape
-    for m in range(columns):
-        cut = slice(m * wide, (m + 1) * wide)
-        total = held[0][:, cut] if held else jnp.zeros((out_ref.shape[0], wide), jnp.float32)
-        for b in range(blocks):
-            for i in range(per_block):
-                row = 0
-                for ref in gated:
-                    size = ref.shape[2]
-                    total += jnp.dot(
-                        ref[order[b] * per_block + i],
-                        weights[m * blocks + b][i, row : row + size, :],
-                        preferred_element_type=jnp.float32,
+    step, steps = pl.program_id(0), pl.num_programs(0)
+    lhs = jnp.concatenate([ref[0] for ref in gated], axis=1)
+    for b in range(blocks):
+        for i in range(per_block):
+
+            @pl.when(step == b * per_block + i)
+            def _(b=b, i=i):
+                for m in range(columns):
+                    cut = slice(m * wide, (m + 1) * wide)
+                    value = jnp.dot(
+                        lhs, weights[m * blocks + b][i], preferred_element_type=jnp.float32
                     )
-                    row += size
-        out_ref[:, cut] = total.astype(out_ref.dtype)
+                    if b + i > 0:
+                        value += total[:, cut]
+                    elif held:
+                        each = columns // len(held)
+                        value += held[m // each][:, m % each * wide : (m % each + 1) * wide]
+                    if b == blocks - 1 and i == per_block - 1:
+                        out_ref[:, cut] = value.astype(out_ref.dtype)
+                    else:
+                        total[:, cut] = value
 
 
 def out_project(order, gated, start, weights, kind, held=()):
@@ -150,21 +163,29 @@
     size = sum(block.shape[2] for block in gated)
     per_block, _, wide = weights[0][0].shape
     columns, blocks = len(weights), len(weights[0])
-    tile = min(rows, 256)
-    cell = pl.BlockSpec((tile, columns * wide), lambda i, o: (i, 0))
+    whole = [
+        pl.BlockSpec(block.shape, lambda k, o: (0, 0), pipeline_mode=pl.Buffered(1)) for block in held
+    ]
     piece = pl.BlockSpec(
-        (per_block, size, wide), lambda i, o: (0, start // size, 0), pipeline_mode=pl.Buffered(1)
+        (per_block, size, wide), lambda k, o: (0, start // size, 0), pipeline_mode=pl.Buffered(1)
     )
     spec = pltpu.PrefetchScalarGridSpec(
         num_scalar_prefetch=1,
-        grid=(rows // tile,),
-        in_specs=[pl.BlockSpec((chans, tile, block.shape[2]), lambda i, o: (0, i, 0)) for block in gated]
+        grid=(chans,),
+        in_specs=[
+            pl.BlockSpec(
+                (1, rows, block.shape[2]),
+                lambda k, o: (o[k // per_block] * per_block + k % per_block, 0, 0),
+            )
+            for block in gated
+        ]
         + [piece] * (columns * blocks)
-        + [cell] * len(held),
-        out_specs=cell,
+        + whole,
+        out_specs=pl.BlockSpec((rows, columns * wide), lambda k, o: (0, 0)),
+        scratch_shapes=[pltpu.VMEM((rows, columns * wide), jnp.float32)],
     )
     return pl.pallas_call(
-        functools.partial(out_kernel, blocks, len(gated), columns),
+        functools.partial(out_kernel, blocks, columns, len(gated)),
         grid_spec=spec,
         out_shape=jax.ShapeDtypeStruct((rows, columns * wide), kind),
         compiler_params=pltpu.CompilerParams(vmem_limit_bytes=VMEM),
@@ -227,7 +248,9 @@
     pieces = [
         from_far(columns_of(part, (e - k) % far), k) for k in range(1, far)
     ]
-    pieces, rows, owns, near_rows[0] = together((pieces, rows, owns, near_rows[0]))
+    pieces, before, rows, owns, near_rows[0] = together(
+        (pieces, before, rows, owns, near_rows[0])
+    )
     theirs = [lax.all_gather(piece, "chan", axis=0, tiled=True) for piece in pieces]
     before = normalised(before, norm_gain)
     theirs_before = [from_far(columns_of(before, (e - k) % far), k) for k in range(1, far)]
@@ -278,16 +301,14 @@
             found += [across[m][a - 1]] + beyond[m][(a - 1) * (near - 1) : a * (near - 1)]
         blocks.append([block.reshape(-1, chans_here, block.shape[1]) for block in found])
     half = OUT_CHUNKS // 2
-    sums = [
-        out_project(order, gated[:-1], 0, found, jnp.float32) for found in (blocks[:half], blocks[half:])
-    ]
-    sums, last = together((sums, gated[-1]))
-    outs = [
-        out_project(order, [last], edges[CHUNKS - 1], found, jnp.bfloat16, [total])
-        for found, total in zip((blocks[:half], blocks[half:]), sums)
-    ]
-    out = jnp.concatenate(outs, axis=1).reshape(chans, share, -1)
-    got = lax.all_to_all(out, "chan", split_axis=0, concat_axis=0, tiled=True)
+    first = out_project(order, gated[:-1], 0, blocks[:half], jnp.float32)
+    first, blocks[half:] = together((first, blocks[half:]))
+    second = out_project(order, gated[:-1], 0, blocks[half:], jnp.float32)
+    first, second, last = together((first, second, gated[-1]))
+    out = out_project(order, [last], edges[CHUNKS - 1], blocks, jnp.bfloat16, [first, second])
+    got = lax.all_to_all(
+        out.reshape(chans, share, -1), "chan", split_axis=0, concat_axis=0, tiled=True
+    )
     return got.transpose(1, 0, 2).reshape(share, -1)
 
 

time: 696 us -> 600 us (0.86)
  waiting for transfers between devices: 372 us -> 223 us
  Pallas kernels: 159 us -> 210 us
    ppermute x1, waiting for transfers between devices: 110 us -> 18.7 us  [per_device(): lax.ppermute(x_rows[tokens - HALO:], 'seq', [(a, a + 1) for a in range(se...]
    ppermute x14, waiting for transfers between devices: 258 us -> 204 us  [from_far(): return lax.ppermute(block, 'seq', pairs)]
    pallas_call x8, Pallas kernels: 105 us -> 151 us  [project(): pl.pallas_call(functools.partial(project_kernel, len(weights), len(receiv...]
    pallas_call x4 -> x3, Pallas kernels: 40 us -> 45.3 us  [out_project(): pl.pallas_call(functools.partial(out_kernel, blocks, columns, len(gated))...]
  transfers between devices with their start and end apart: 28 -> 28, of which waited for: 15 -> 12; matrix products, arithmetic and copies ran while one was open for 7% -> 9% of each run, Pallas kernels for 20% -> 33%
where the time goes in v4:
time: 600 us; the launch traced here: 591 us
  waiting for transfers between devices  223 us (37%)
  Pallas kernels  210 us (35%)
  blocking collectives  52.6 us (9%)
  other arithmetic  38 us (6%)
  starting transfers between devices  30.5 us (5%)
  local copies, waits for them, and re-layouts  23.4 us (4%)
  between operations  13.5 us (2%)
    ppermute x14, waiting for transfers between devices, from_far(): return lax.ppermute(block, 'seq', pairs)  204 us
    pallas_call x8, Pallas kernels, project(): pl.pallas_call(functools.partial(project_kernel, len(weights), len(receiv...  151 us
    all_to_all x1, blocking collectives, per_device(): lax.all_to_all(out.reshape(chans, share, -1), 'chan', split_axis=0, conca...  52.6 us
    pallas_call x3, Pallas kernels, out_project(): pl.pallas_call(functools.partial(out_kernel, blocks, columns, len(gated))...  45.3 us
    ppermute x1, waiting for transfers between devices, per_device(): lax.ppermute(x_rows[tokens - HALO:], 'seq', [(a, a + 1) for a in range(se...  18.7 us
    ppermute x14, starting transfers between devices, from_far(): return lax.ppermute(block, 'seq', pairs)  18.5 us
    convert_element_type x3, other arithmetic, normalised(): return (values * lax.rsqrt(squares + 1e-06) * gain).astype(jnp.bfloat16)  18.2 us
    pallas_call x4, Pallas kernels, short_mix(): pl.pallas_call(functools.partial(mix_kernel, feat, filt), grid=(steps,),...  14.1 us
  transfers between devices with their start and end apart: 28, of which 12 were waited for; matrix products, arithmetic and copies ran while one was open for 9% of the time, Pallas kernels for 33%

profile of v4, /device:TPU:0, one launch (start us, length us, event | category | flops | bytes accessed | tf_op | source)
XLA Modules:
  0.0 591.1 jit_solution(2555651520926904347)
XLA Ops:
  11.2 3.0 collective-permute-start
  24.0 3.2 slice_bitcast_fusion
  27.2 18.7 %collective-permute-done.1 = bf16[16,8192]{1,0:T(8,128)(2,1)S(1)} collective-permute-done((bf16[16,8192]{1,0:T(8,128)(2,1)S(1)}, bf16[16,8192]{1,0:T(8,128)(2,1)S(1)}, u32[]{:S(2)}, u32[]{:S(2)}) %collective-permute-start.1) | collective-permute-done | bytes 262176 | tf_op jit(solution)/shard_map/ppermute | solution.py:244
  48.7 7.5 %fusion = f32[1024]{0:T(1024)S(1)} fusion(bf16[1024,8192]{1,0:T(8,128)(2,1)} %param.6), kind=kLoop, calls=%fused_computation.2 | loop fusion | flops 25164800 | bytes 16781312 | tf_op jit(solution)/shard_map/reduce_sum | solution.py:199
  56.2 15.8 %fusion.2 = bf16[1024,8192]{1,0:T(8,128)(2,1)} fusion(bf16[1024,8192]{1,0:T(8,128)(2,1)} %param.6, f32[8192]{0:T(1024)S(1)} %copy-done.11, f32[1024]{0:T(1024)S(1)} %add_rsqrt_fusion), kind=kLoop, calls=%fused_computation.4 | loop fusion | flops 33554432 | bytes 33591296 | tf_op jit(solution)/shard_map/convert_element_type | solution.py:200
  74.5 8.4 %constant_dynamic-slice_fusion.3 = (bf16[1024,2048]{1,0:T(8,128)(2,1)}, bf16[1024,2048]{1,0:T(8,128)(2,1)}) fusion(bf16[1024,8192]{1,0:T(8,128)(2,1)} %fusion.2, s32[]{:T(128)S(6)} %select_n.86, s32[]{:T(128)S(6)} %select_n.87), kind=kLoop, calls=%fused_computation.37 | loop fusion | bytes 16777224 | tf_op jit(solution)/shard_map/dynamic_slice | solution.py:224
  84.8 16.4 %collective-permute-done.3.refs_1_ = bf16[16,4096]{1,0:T(8,128)(2,1)S(1)} collective-permute-done((bf16[16,4096]{1,0:T(8,128)(2,1)S(1)}, bf16[16,4096]{1,0:T(8,128)(2,1)S(1)}, u32[]{:S(2)}, u32[]{:S(2)}) %collective-permute-start.3) | collective-permute-done | bytes 131104 | tf_op jit(solution)/shard_map/ppermute | solution.py:219
  103.2 7.9 %pad_maximum_fusion.refs_0_ = bf16[1024,4096]{1,0:T(8,128)(2,1)} fusion(bf16[1024,2048]{1,0:T(8,128)(2,1)} %get-tuple-element.124, bf16[1024,2048]{1,0:T(8,128)(2,1)} %get-tuple-element.123), kind=kLoop, calls=%fused_computation.5 | loop fusion | flops 16777216 | bytes 16777216 | tf_op jit(solution)/shard_map/concatenate | solution.py:222
  111.7 12.0 %collective-permute-done.6 = bf16[2048,256]{1,0:T(8,128)(2,1)} collective-permute-done((bf16[2048,256]{1,0:T(8,128)(2,1)}, bf16[2048,256]{1,0:T(8,128)(2,1)}, u32[]{:S(2)}, u32[]{:S(2)}) %collective-permute-start.6) | collective-permute-done | bytes 1048608 | tf_op jit(solution)/shard_map/ppermute | solution.py:219
  123.7 22.5 %collective-permute-done.7 = bf16[2048,256]{1,0:T(8,128)(2,1)} collective-permute-done((bf16[2048,256]{1,0:T(8,128)(2,1)}, bf16[2048,256]{1,0:T(8,128)(2,1)}, u32[]{:S(2)}, u32[]{:S(2)}) %collective-permute-start.7) | collective-permute-done | bytes 1048608 | tf_op jit(solution)/shard_map/ppermute | solution.py:219
  146.2 19.3 %collective-permute-done.8 = bf16[2048,256]{1,0:T(8,128)(2,1)} collective-permute-done((bf16[2048,256]{1,0:T(8,128)(2,1)}, bf16[2048,256]{1,0:T(8,128)(2,1)}, u32[]{:S(2)}, u32[]{:S(2)}) %collective-permute-start.8) | collective-permute-done | bytes 1048608 | tf_op jit(solution)/shard_map/ppermute | solution.py:219
  165.5 18.5 %project.8 = bf16[1040,768]{1,0:T(8,128)(2,1)} custom-call(bf16[1024,4096]{1,0:T(8,128)(2,1)} %all-gather.10.cloned.1.call-done.refs_0_, bf16[16,4096]{1,0:T(8,128)(2,1)} %copy-done.8, bf16[3,2048,256]{2,1,0:T(8,128)(2,1)} %slice_bitcast_fusion.3.refs_2_, bf16[3,2048,256]{2,1,0:T(8,128)(2,1)} %collective-permute-done.4.refs_3_), custom_call_target="tpu_custom_call" | custom-call | flops 1024 | bytes 1024 | tf_op jit(solution)/shard_map/project/pallas_call | solution.py:66
  186.8 31.2 %collective-permute-done.9.refs_4_ = bf16[1040,768]{1,0:T(8,128)(2,1)} collective-permute-done((bf16[1040,768]{1,0:T(8,128)(2,1)}, bf16[1040,768]{1,0:T(8,128)(2,1)}, u32[]{:S(2)}, u32[]{:S(2)}) %collective-permute-start.9) | collective-permute-done | bytes 1597472 | tf_op jit(solution)/shard_map/ppermute | solution.py:219
  218.0 19.5 %project.9.qh.kh.vh.q.k.v = bf16[1040,768]{1,0:T(8,128)(2,1)} custom-call(bf16[1024,4096]{1,0:T(8,128)(2,1)} %pad_maximum_fusion.refs_0_, bf16[16,4096]{1,0:T(8,128)(2,1)} %pad_maximum_fusion.3.refs_1_, bf16[3,2048,256]{2,1,0:T(8,128)(2,1)} %slice_bitcast_fusion.3.refs_2_, bf16[3,2048,256]{2,1,0:T(8,128)(2,1)} %collective-permute-done.4.refs_3_, ...), custom_call_target="tpu_custom_call" | custom-call | flops 1024 | bytes 1024 | tf_op jit(solution)/shard_map/project/pallas_call | solution.py:66
  237.5 3.4 short_mix.4
  242.5 18.4 %project.10 = bf16[1040,768]{1,0:T(8,128)(2,1)} custom-call(bf16[1024,4096]{1,0:T(8,128)(2,1)} %all-gather.10.cloned.1.call-done.refs_0_, bf16[16,4096]{1,0:T(8,128)(2,1)} %copy-done.8, bf16[3,2048,256]{2,1,0:T(8,128)(2,1)} %get-tuple-element.78.refs_2_, bf16[3,2048,256]{2,1,0:T(8,128)(2,1)} %collective-permute-done.10.refs_3_, ...), custom_call_target="tpu_custom_call" | custom-call | flops 1024 | bytes 1024 | tf_op jit(solution)/shard_map/project/pallas_call | solution.py:66
  262.9 36.0 %collective-permute-done.12.refs_4_ = bf16[1040,768]{1,0:T(8,128)(2,1)S(1)} collective-permute-done((bf16[1040,768]{1,0:T(8,128)(2,1)}, bf16[1040,768]{1,0:T(8,128)(2,1)S(1)}, u32[]{:S(2)}, u32[]{:S(2)}) %collective-permute-start.12) | collective-permute-done | bytes 1597472 | tf_op jit(solution)/shard_map/ppermute | solution.py:219
  300.1 19.0 %project.11.qh.kh.vh.q.k.v = bf16[1040,768]{1,0:T(8,128)(2,1)} custom-call(bf16[1024,4096]{1,0:T(8,128)(2,1)} %pad_maximum_fusion.refs_0_, bf16[16,4096]{1,0:T(8,128)(2,1)} %pad_maximum_fusion.3.refs_1_, bf16[3,2048,256]{2,1,0:T(8,128)(2,1)} %get-tuple-element.78.refs_2_, bf16[3,2048,256]{2,1,0:T(8,128)(2,1)} %collective-permute-done.10.refs_3_, ...), custom_call_target="tpu_custom_call" | custom-call | flops 1024 | bytes 1024 | tf_op jit(solution)/shard_map/project/pallas_call | solution.py:66
  319.2 3.4 short_mix.5
  323.3 18.6 %project.12 = bf16[1040,768]{1,0:T(8,128)(2,1)} custom-call(bf16[1024,4096]{1,0:T(8,128)(2,1)} %all-gather.10.cloned.1.call-done.refs_0_, bf16[16,4096]{1,0:T(8,128)(2,1)} %copy-done.8, bf16[3,2048,256]{2,1,0:T(8,128)(2,1)} %get-tuple-element.87.refs_2_, bf16[3,2048,256]{2,1,0:T(8,128)(2,1)} %collective-permute-done.13.refs_3_, ...), custom_call_target="tpu_custom_call" | custom-call | flops 1024 | bytes 1024 | tf_op jit(solution)/shard_map/project/pallas_call | solution.py:66
  343.9 36.1 %collective-permute-done.15.refs_4_ = bf16[1040,768]{1,0:T(8,128)(2,1)} collective-permute-done((bf16[1040,768]{1,0:T(8,128)(2,1)}, bf16[1040,768]{1,0:T(8,128)(2,1)}, u32[]{:S(2)}, u32[]{:S(2)}) %collective-permute-start.15) | collective-permute-done | bytes 1597472 | tf_op jit(solution)/shard_map/ppermute | solution.py:219
  380.1 19.0 %project.13.qh.kh.vh.q.k.v = bf16[1040,768]{1,0:T(8,128)(2,1)} custom-call(bf16[1024,4096]{1,0:T(8,128)(2,1)} %pad_maximum_fusion.refs_0_, bf16[16,4096]{1,0:T(8,128)(2,1)} %pad_maximum_fusion.3.refs_1_, bf16[3,2048,256]{2,1,0:T(8,128)(2,1)} %get-tuple-element.87.refs_2_, bf16[3,2048,256]{2,1,0:T(8,128)(2,1)} %collective-permute-done.13.refs_3_, ...), custom_call_target="tpu_custom_call" | custom-call | flops 1024 | bytes 1024 | tf_op jit(solution)/shard_map/project/pallas_call | solution.py:66
  401.7 3.3 short_mix.6
  405.1 18.7 %project.14 = bf16[1040,768]{1,0:T(8,128)(2,1)} custom-call(bf16[1024,4096]{1,0:T(8,128)(2,1)} %all-gather.10.cloned.1.call-done.refs_0_, bf16[16,4096]{1,0:T(8,128)(2,1)} %copy-done.8, bf16[3,2048,256]{2,1,0:T(8,128)(2,1)} %copy-done, bf16[3,2048,256]{2,1,0:T(8,128)(2,1)} %copy-done.1, f32[8,128]{1,0:T(8,128)} %get-tuple-element.97.refs_4_), custom_call_target="tpu_custom_call" | custom-call | flops 1024 | bytes 1024 | tf_op jit(solution)/shard_map/project/pallas_call | solution.py:66
  427.5 17.2 %collective-permute-done.18.refs_4_ = bf16[1040,768]{1,0:T(8,128)(2,1)S(1)} collective-permute-done((bf16[1040,768]{1,0:T(8,128)(2,1)}, bf16[1040,768]{1,0:T(8,128)(2,1)S(1)}, u32[]{:S(2)}, u32[]{:S(2)}) %collective-permute-start.18) | collective-permute-done | bytes 1597472 | tf_op jit(solution)/shard_map/ppermute | solution.py:219
  445.8 19.1 %project.15.qh.kh.vh.q.k.v = bf16[1040,768]{1,0:T(8,128)(2,1)} custom-call(bf16[1024,4096]{1,0:T(8,128)(2,1)} %pad_maximum_fusion.refs_0_, bf16[16,4096]{1,0:T(8,128)(2,1)} %pad_maximum_fusion.3.refs_1_, bf16[3,2048,256]{2,1,0:T(8,128)(2,1)} %copy-done, bf16[3,2048,256]{2,1,0:T(8,128)(2,1)} %copy-done.1, bf16[1040,768]{1,0:T(8,128)(2,1)} %copy-done.9), custom_call_target="tpu_custom_call" | custom-call | flops 1024 | bytes 1024 | tf_op jit(solution)/shard_map/project/pallas_call | solution.py:66
  464.9 4.0 short_mix.7
  471.8 16.1 %out_project.3.refs_17_ = f32[1024,512]{1,0:T(8,128)} custom-call(s32[4]{0:T(128)} %pad_add_fusion.order, bf16[8,1024,256]{2,1,0:T(8,128)(2,1)} %bitcast.36, bf16[8,1024,256]{2,1,0:T(8,128)(2,1)} %bitcast.38, bf16[8,1024,256]{2,1,0:T(8,128)(2,1)} %bitcast.40, bf16[2,1024,256]{2,1,0:T(8,128)(2,1)} %bitcast.11.refs_3_.refs_1_, ...), custom_call_target="tpu_custom_call" | custom-call | flops 1024 | bytes 1024 | tf_op jit(solution)/shard_map/out_project/pallas_call | solution.py:187
  489.4 11.3 %collective-permute-done.22 = bf16[2048,256]{1,0:T(8,128)(2,1)} collective-permute-done((bf16[2048,256]{1,0:T(8,128)(2,1)S(1)}, bf16[2048,256]{1,0:T(8,128)(2,1)}, u32[]{:S(2)}, u32[]{:S(2)}) %collective-permute-start.22) | collective-permute-done | bytes 1048608 | tf_op jit(solution)/shard_map/ppermute | solution.py:219
  500.8 15.5 %out_project.4.refs_18_ = f32[1024,512]{1,0:T(8,128)} custom-call(s32[4]{0:T(128)} %pad_add_fusion.order, bf16[8,1024,256]{2,1,0:T(8,128)(2,1)} %bitcast.37, bf16[8,1024,256]{2,1,0:T(8,128)(2,1)} %bitcast.39, bf16[8,1024,256]{2,1,0:T(8,128)(2,1)} %bitcast.41, bf16[2,1024,256]{2,1,0:T(8,128)(2,1)} %bitcast.19.refs_3_.refs_9_, bf16[2,1024,256]{2,1,0:T(8,128)(2,1)} %bitcast.46, ...), custom_call_target="tpu_custom_call" | custom-call | flops 1024 | bytes 1024 | tf_op jit(solution)/shard_map/out_project/pallas_call | solution.py:187
  516.7 13.6 %out_project.5 = bf16[1024,1024]{1,0:T(8,128)(2,1)} custom-call(s32[4]{0:T(128)} %pad_add_fusion.order, bf16[8,1024,256]{2,1,0:T(8,128)(2,1)} %bitcast.52, bf16[2,1024,256]{2,1,0:T(8,128)(2,1)} %bitcast.11.refs_3_.refs_1_, bf16[2,1024,256]{2,1,0:T(8,128)(2,1)} %bitcast.12.refs_4_.refs_2_, bf16[2,1024,256]{2,1,0:T(8,128)(2,1)} %bitcast.13.refs_5_.refs_3_, ...), custom_call_target="tpu_custom_call" | custom-call | flops 1024 | bytes 1024 | tf_op jit(solution)/shard_map/out_project/pallas_call | solution.py:187
  530.3 52.6 %all_to_all.5 = bf16[8,128,1024]{2,1,0:T(8,128)(2,1)S(1)} all-to-all(bf16[8,128,1024]{2,1,0:T(8,128)(2,1)} %bitcast.42), channel_id=1, replica_groups=mesh['seq'=4,'chan'=8] {'chan'}, dimensions={0} | all-to-all | bytes 4194304 | tf_op jit(solution)/shard_map/all_to_all | solution.py:309
  (97 shorter events, 48.1 us)
Async XLA Ops:
  6.5 158.9 %all-gather.10.cloned.1.call-start = ((), (), s32[]{:S(2)}) async-start(), calls=%async_computation.1 | async-start | bytes 9437184 | tf_op jit(solution)/shard_map/all_gather | solution.py:254
  11.2 34.8 %collective-permute-start = (bf16[128,4096]{1,0:T(8,128)(2,1)S(1)}, bf16[128,4096]{1,0:T(8,128)(2,1)}, u32[]{:S(2)}, u32[]{:S(2)}) collective-permute-start(bf16[128,4096]{1,0:T(8,128)(2,1)S(1)} %pad_maximum_fusion.1), channel_id=1, source_target_pairs={{16,0},{24,8},{0,16},{8,24},{17,1},{25,9},{1,17},{9,25},{18,2},{26... | collective-permute-start | bytes 3145736 | tf_op jit(solution)/shard_map/ppermute | solution.py:219
  16.4 29.6 %collective-permute-start.2 = (bf16[2048,256]{1,0:T(8,128)(2,1)}, bf16[2048,256]{1,0:T(8,128)(2,1)}, u32[]{:S(2)}, u32[]{:S(2)}) collective-permute-start(bf16[2048,256]{1,0:T(8,128)(2,1)} %get-tuple-element.68), channel_id=1, source_target_pairs={{8,0},{0,8},{24,16},{16,24},{9,1},{1,9},{25,17},{17,25},{10,2},{2,... | collective-permute-start | bytes 3145736 | tf_op jit(solution)/shard_map/ppermute | solution.py:215
  19.0 27.0 %collective-permute-start.1 = (bf16[16,8192]{1,0:T(8,128)(2,1)S(1)}, bf16[16,8192]{1,0:T(8,128)(2,1)S(1)}, u32[]{:S(2)}, u32[]{:S(2)}) collective-permute-start(bf16[16,8192]{1,0:T(8,128)(2,1)S(1)} %slice.39), channel_id=1, source_target_pairs={{0,8},{8,16},{16,24},{1,9},{9,17},{17,25},{2,10},{10,18},{18,26},{... | collective-permute-start | bytes 786440 | tf_op jit(solution)/shard_map/ppermute | solution.py:244
  27.2 295.4 %copy-start = (bf16[3,2048,256]{2,1,0:T(8,128)(2,1)}, bf16[3,2048,256]{2,1,0:T(8,128)(2,1)S(1)}, u32[]{:S(2)}) copy-start(bf16[3,2048,256]{2,1,0:T(8,128)(2,1)S(1)} %get-tuple-element.95.refs_2_) | copy-start | bytes 9437188
  46.0 276.5 %all-gather.12.cloned.1.call-start = ((), (), s32[]{:S(2)}) async-start(), calls=%async_computation.2 | async-start | bytes 4718592 | tf_op jit(solution)/shard_map/all_gather | solution.py:292
  46.1 119.4 %collective-permute-start.4 = (bf16[3,2048,256]{2,1,0:T(8,128)(2,1)}, bf16[3,2048,256]{2,1,0:T(8,128)(2,1)}, u32[]{:S(2)}, u32[]{:S(2)}) collective-permute-start(bf16[3,2048,256]{2,1,0:T(8,128)(2,1)} %slice_bitcast_fusion.3.refs_2_), channel_id=1, source_target_pairs={{8,0},{0,8},{24,16},{16,24},{9,1},{1,9},{25,17},{17,25},{10,2},{2,... | collective-permute-start | bytes 9437192 | tf_op jit(solution)/shard_map/ppermute | solution.py:215
  48.6 188.9 %collective-permute-start.10 = (bf16[3,2048,256]{2,1,0:T(8,128)(2,1)}, bf16[3,2048,256]{2,1,0:T(8,128)(2,1)}, u32[]{:S(2)}, u32[]{:S(2)}) collective-permute-start(bf16[3,2048,256]{2,1,0:T(8,128)(2,1)} %get-tuple-element.78.refs_2_), channel_id=1, source_target_pairs={{8,0},{0,8},{24,16},{16,24},{9,1},{1,9},{25,17},{17,25},{10,2},{2,... | collective-permute-start | bytes 9437192 | tf_op jit(solution)/shard_map/ppermute | solution.py:215
  72.0 31.0 %collective-permute-start.5 = (bf16[2048,256]{1,0:T(8,128)(2,1)}, bf16[2048,256]{1,0:T(8,128)(2,1)}, u32[]{:S(2)}, u32[]{:S(2)}) collective-permute-start(bf16[2048,256]{1,0:T(8,128)(2,1)} %get-tuple-element.68), channel_id=1, source_target_pairs={{16,0},{24,8},{0,16},{8,24},{17,1},{25,9},{1,17},{9,25},{18,2},{26... | collective-permute-start | bytes 3145736 | tf_op jit(solution)/shard_map/ppermute | solution.py:219
  74.2 26.9 %collective-permute-start.3 = (bf16[16,4096]{1,0:T(8,128)(2,1)S(1)}, bf16[16,4096]{1,0:T(8,128)(2,1)S(1)}, u32[]{:S(2)}, u32[]{:S(2)}) collective-permute-start(bf16[16,4096]{1,0:T(8,128)(2,1)S(1)} %pad_maximum_fusion.2), channel_id=1, source_target_pairs={{16,0},{24,8},{0,16},{8,24},{17,1},{25,9},{1,17},{9,25},{18,2},{26... | collective-permute-start | bytes 393224 | tf_op jit(solution)/shard_map/ppermute | solution.py:219
  82.9 40.8 %collective-permute-start.6 = (bf16[2048,256]{1,0:T(8,128)(2,1)}, bf16[2048,256]{1,0:T(8,128)(2,1)}, u32[]{:S(2)}, u32[]{:S(2)}) collective-permute-start(bf16[2048,256]{1,0:T(8,128)(2,1)} %get-tuple-element.69), channel_id=1, source_target_pairs={{16,0},{24,8},{0,16},{8,24},{17,1},{25,9},{1,17},{9,25},{18,2},{26... | collective-permute-start | bytes 3145736 | tf_op jit(solution)/shard_map/ppermute | solution.py:219
  101.1 45.0 %collective-permute-start.7 = (bf16[2048,256]{1,0:T(8,128)(2,1)}, bf16[2048,256]{1,0:T(8,128)(2,1)}, u32[]{:S(2)}, u32[]{:S(2)}) collective-permute-start(bf16[2048,256]{1,0:T(8,128)(2,1)} %get-tuple-element.70), channel_id=1, source_target_pairs={{16,0},{24,8},{0,16},{8,24},{17,1},{25,9},{1,17},{9,25},{18,2},{26... | collective-permute-start | bytes 3145736 | tf_op jit(solution)/shard_map/ppermute | solution.py:219
  103.0 62.5 %collective-permute-start.8 = (bf16[2048,256]{1,0:T(8,128)(2,1)}, bf16[2048,256]{1,0:T(8,128)(2,1)}, u32[]{:S(2)}, u32[]{:S(2)}) collective-permute-start(bf16[2048,256]{1,0:T(8,128)(2,1)} %get-tuple-element.71), channel_id=1, source_target_pairs={{16,0},{24,8},{0,16},{8,24},{17,1},{25,9},{1,17},{9,25},{18,2},{26... | collective-permute-start | bytes 3145736 | tf_op jit(solution)/shard_map/ppermute | solution.py:219
  111.7 74.4 %copy-start.12 = (f32[3,3,1024]{2,1,0:T(4,128)S(1)}, f32[3,3,1024]{2,1,0:T(4,128)}, u32[]{:S(2)}) copy-start(f32[3,3,1024]{2,1,0:T(4,128)} %param.9) | copy-start | bytes 110596
  111.7 74.5 %copy-start.13 = (f32[7,1024]{1,0:T(8,128)S(1)}, f32[7,1024]{1,0:T(8,128)}, u32[]{:S(2)}) copy-start(f32[7,1024]{1,0:T(8,128)} %param.10) | copy-start | bytes 86020
  183.9 34.1 %collective-permute-start.9 = (bf16[1040,768]{1,0:T(8,128)(2,1)}, bf16[1040,768]{1,0:T(8,128)(2,1)}, u32[]{:S(2)}, u32[]{:S(2)}) collective-permute-start(bf16[1040,768]{1,0:T(8,128)(2,1)} %project.8), channel_id=1, source_target_pairs={{16,0},{24,8},{0,16},{8,24},{17,1},{25,9},{1,17},{9,25},{18,2},{26... | collective-permute-start | bytes 4792328 | tf_op jit(solution)/shard_map/ppermute | solution.py:219
  185.7 51.9 %collective-permute-start.11 = (bf16[2048,256]{1,0:T(8,128)(2,1)}, bf16[2048,256]{1,0:T(8,128)(2,1)}, u32[]{:S(2)}, u32[]{:S(2)}) collective-permute-start(bf16[2048,256]{1,0:T(8,128)(2,1)} %get-tuple-element.69), channel_id=1, source_target_pairs={{8,0},{0,8},{24,16},{16,24},{9,1},{1,9},{25,17},{17,25},{10,2},{2,... | collective-permute-start | bytes 3145736 | tf_op jit(solution)/shard_map/ppermute | solution.py:215
  241.0 164.1 %all-gather.14.cloned.1.call-start = ((), (), s32[]{:S(2)}) async-start(), calls=%async_computation.3 | async-start | bytes 4718592 | tf_op jit(solution)/shard_map/all_gather | solution.py:292
  241.0 78.2 %collective-permute-start.13 = (bf16[3,2048,256]{2,1,0:T(8,128)(2,1)}, bf16[3,2048,256]{2,1,0:T(8,128)(2,1)}, u32[]{:S(2)}, u32[]{:S(2)}) collective-permute-start(bf16[3,2048,256]{2,1,0:T(8,128)(2,1)} %get-tuple-element.87.refs_2_), channel_id=1, source_target_pairs={{8,0},{0,8},{24,16},{16,24},{9,1},{1,9},{25,17},{17,25},{10,2},{2,... | collective-permute-start | bytes 9437192 | tf_op jit(solution)/shard_map/ppermute | solution.py:215
  260.9 38.1 %collective-permute-start.12 = (bf16[1040,768]{1,0:T(8,128)(2,1)}, bf16[1040,768]{1,0:T(8,128)(2,1)S(1)}, u32[]{:S(2)}, u32[]{:S(2)}) collective-permute-start(bf16[1040,768]{1,0:T(8,128)(2,1)} %project.10), channel_id=1, source_target_pairs={{16,0},{24,8},{0,16},{8,24},{17,1},{25,9},{1,17},{9,25},{18,2},{26... | collective-permute-start | bytes 4792328 | tf_op jit(solution)/shard_map/ppermute | solution.py:219
  261.9 57.3 %collective-permute-start.14 = (bf16[2048,256]{1,0:T(8,128)(2,1)}, bf16[2048,256]{1,0:T(8,128)(2,1)}, u32[]{:S(2)}, u32[]{:S(2)}) collective-permute-start(bf16[2048,256]{1,0:T(8,128)(2,1)} %collective-permute-done.2), channel_id=1, source_target_pairs={{16,0},{24,8},{0,16},{8,24},{17,1},{25,9},{1,17},{9,25},{18,2},{26... | collective-permute-start | bytes 3145736 | tf_op jit(solution)/shard_map/ppermute | solution.py:219
  322.6 146.4 %all-gather.16.cloned.1.call-start = ((), (), s32[]{:S(2)}) async-start(), calls=%async_computation.4 | async-start | bytes 4718592 | tf_op jit(solution)/shard_map/all_gather | solution.py:292
  322.6 76.5 %collective-permute-start.16 = (bf16[3,2048,256]{2,1,0:T(8,128)(2,1)S(1)}, bf16[3,2048,256]{2,1,0:T(8,128)(2,1)S(1)}, u32[]{:S(2)}, u32[]{:S(2)}) collective-permute-start(bf16[3,2048,256]{2,1,0:T(8,128)(2,1)S(1)} %get-tuple-element.95.refs_2_), channel_id=1, source_target_pairs={{8,0},{0,8},{24,16},{16,24},{9,1},{1,9},{25,17},{17,25},{10,2},{2,... | collective-permute-start | bytes 9437192 | tf_op jit(solution)/shard_map/ppermute | solution.py:215
  341.9 38.2 %collective-permute-start.15 = (bf16[1040,768]{1,0:T(8,128)(2,1)}, bf16[1040,768]{1,0:T(8,128)(2,1)}, u32[]{:S(2)}, u32[]{:S(2)}) collective-permute-start(bf16[1040,768]{1,0:T(8,128)(2,1)} %project.12), channel_id=1, source_target_pairs={{16,0},{24,8},{0,16},{8,24},{17,1},{25,9},{1,17},{9,25},{18,2},{26... | collective-permute-start | bytes 4792328 | tf_op jit(solution)/shard_map/ppermute | solution.py:219
  343.6 57.2 %collective-permute-start.17 = (bf16[2048,256]{1,0:T(8,128)(2,1)}, bf16[2048,256]{1,0:T(8,128)(2,1)S(1)}, u32[]{:S(2)}, u32[]{:S(2)}) collective-permute-start(bf16[2048,256]{1,0:T(8,128)(2,1)} %collective-permute-done.11), channel_id=1, source_target_pairs={{16,0},{24,8},{0,16},{8,24},{17,1},{25,9},{1,17},{9,25},{18,2},{26... | collective-permute-start | bytes 3145736 | tf_op jit(solution)/shard_map/ppermute | solution.py:219
  405.1 111.7 %all-gather.18.cloned.1.call-start = ((), (), s32[]{:S(2)}) async-start(), calls=%async_computation.5 | async-start | bytes 4718592 | tf_op jit(solution)/shard_map/all_gather | solution.py:292
  423.8 20.9 %collective-permute-start.18 = (bf16[1040,768]{1,0:T(8,128)(2,1)}, bf16[1040,768]{1,0:T(8,128)(2,1)S(1)}, u32[]{:S(2)}, u32[]{:S(2)}) collective-permute-start(bf16[1040,768]{1,0:T(8,128)(2,1)} %project.14), channel_id=1, source_target_pairs={{16,0},{24,8},{0,16},{8,24},{17,1},{25,9},{1,17},{9,25},{18,2},{26... | collective-permute-start | bytes 4792328 | tf_op jit(solution)/shard_map/ppermute | solution.py:219
  425.4 39.5 %collective-permute-start.19 = (bf16[2048,256]{1,0:T(8,128)(2,1)}, bf16[2048,256]{1,0:T(8,128)(2,1)S(1)}, u32[]{:S(2)}, u32[]{:S(2)}) collective-permute-start(bf16[2048,256]{1,0:T(8,128)(2,1)} %get-tuple-element.70), channel_id=1, source_target_pairs={{8,0},{0,8},{24,16},{16,24},{9,1},{1,9},{25,17},{17,25},{10,2},{2,... | collective-permute-start | bytes 3145736 | tf_op jit(solution)/shard_map/ppermute | solution.py:215
  426.2 38.7 %collective-permute-start.20 = (bf16[2048,256]{1,0:T(8,128)(2,1)}, bf16[2048,256]{1,0:T(8,128)(2,1)S(1)}, u32[]{:S(2)}, u32[]{:S(2)}) collective-permute-start(bf16[2048,256]{1,0:T(8,128)(2,1)} %get-tuple-element.71), channel_id=1, source_target_pairs={{8,0},{0,8},{24,16},{16,24},{9,1},{1,9},{25,17},{17,25},{10,2},{2,... | collective-permute-start | bytes 3145736 | tf_op jit(solution)/shard_map/ppermute | solution.py:215
  469.0 20.4 %collective-permute-start.21 = (bf16[2048,256]{1,0:T(8,128)(2,1)S(1)}, bf16[2048,256]{1,0:T(8,128)(2,1)S(1)}, u32[]{:S(2)}, u32[]{:S(2)}) collective-permute-start(bf16[2048,256]{1,0:T(8,128)(2,1)S(1)} %collective-permute-done.19), channel_id=1, source_target_pairs={{16,0},{24,8},{0,16},{8,24},{17,1},{25,9},{1,17},{9,25},{18,2},{26... | collective-permute-start | bytes 3145736 | tf_op jit(solution)/shard_map/ppermute | solution.py:219
  470.7 30.0 %collective-permute-start.22 = (bf16[2048,256]{1,0:T(8,128)(2,1)S(1)}, bf16[2048,256]{1,0:T(8,128)(2,1)}, u32[]{:S(2)}, u32[]{:S(2)}) collective-permute-start(bf16[2048,256]{1,0:T(8,128)(2,1)S(1)} %collective-permute-done.20), channel_id=1, source_target_pairs={{16,0},{24,8},{0,16},{8,24},{17,1},{25,9},{1,17},{9,25},{18,2},{26... | collective-permute-start | bytes 3145736 | tf_op jit(solution)/shard_map/ppermute | solution.py:219
  489.4 11.3 %copy-start.6 = (bf16[2048,256]{1,0:T(8,128)(2,1)}, bf16[2048,256]{1,0:T(8,128)(2,1)S(1)}, u32[]{:S(2)}) copy-start(bf16[2048,256]{1,0:T(8,128)(2,1)S(1)} %collective-permute-done.21) | copy-start | bytes 3145732
  (10 other events, 48.7 us)
Sparse Core Ops, SparseCore 0:
  46.1 83.3 all-gather.9
  241.1 47.6 all-gather.11
  322.7 47.5 all-gather.13
  405.2 47.5 all-gather.15
  469.1 47.5 all-gather.17

commit v5 on v3

--- a/solution.py
+++ b/solution.py
@@ -12,21 +12,21 @@
 EIGHTHS = (0, 2, 4, 6, 8)
 CHUNKS = len(EIGHTHS) - 1
 OUT_CHUNKS = 4
-VMEM = 56 * 2**20
-TILE = 512
+VMEM = 40 * 2**20
 MARK = pl.BlockSpec((8, 128), lambda i: (0, 0))
 MARK_SHAPE = jax.ShapeDtypeStruct((8, 128), jnp.float32)
 LIGHT = pl.CostEstimate(flops=1024, bytes_accessed=1024, transcendentals=0)
 
 
-def project_kernel(count, extra, *refs):
-    x_ref, halo_ref = refs[:2]
-    weights = refs[2 : 2 + count]
-    received = refs[2 + count : 2 + count + extra]
-    received_halo = refs[2 + count + extra : 2 + count + 2 * extra]
-    out_ref = refs[-1]
+def project_kernel(count, extra, tail, *refs):
+    x_ref, refs = refs[0], refs[1:]
+    halo_ref = refs[0] if tail else None
+    weights = refs[tail : tail + count]
+    received = refs[tail + count : tail + count + extra]
+    received_tail = refs[tail + count + extra : tail + count + extra * (1 + tail)]
+    out_ref, mark_ref = refs[-2:]
     parts, depth, width = weights[0].shape
-    tile, halo = x_ref.shape[0], halo_ref.shape[0]
+    tile = x_ref.shape[0]
     step = pl.program_id(0)
 
     def products(ref, sums, start, size):
@@ -47,38 +47,45 @@
 
     @pl.when(step == 0)
     def _():
-        products(halo_ref, received_halo, out_ref.shape[0] - halo, halo)
-
-
-def project(x, halo, weights, received=(), after=()):
-    rows, depth = x.shape
-    extra = halo.shape[0]
+        mark_ref[...] = jnp.zeros_like(mark_ref)
+        if tail:
+            size = halo_ref.shape[0]
+            products(halo_ref, received_tail, out_ref.shape[0] - size, size)
+
+
+def project(x, half, halo, weights, received=(), after=()):
+    rows, depth = x.shape[0] // 2, x.shape[1]
+    extra = HALO if halo else 0
     columns = weights[0].shape[0] * weights[0].shape[2]
-    tile = min(rows, TILE)
+    tile = min(rows, 256)
+    steps = rows // tile
     whole = pl.BlockSpec(weights[0].shape, lambda i: (0, 0, 0), pipeline_mode=pl.Buffered(1))
+    tails = [pl.BlockSpec((HALO, columns), lambda i: (rows // HALO, 0))] if halo else []
     return pl.pallas_call(
-        functools.partial(project_kernel, len(weights), len(received)),
-        grid=(rows // tile,),
-        in_specs=[pl.BlockSpec((tile, depth), lambda i: (i, 0))]
-        + [pl.BlockSpec((extra, depth), lambda i: (0, 0))]
+        functools.partial(project_kernel, len(weights), len(received), len(halo)),
+        grid=(steps,),
+        in_specs=[pl.BlockSpec((tile, depth), lambda i: (half * steps + i, 0))]
+        + [pl.BlockSpec((HALO, depth), lambda i: (0, 0))] * len(halo)
         + [whole] * len(weights)
         + [pl.BlockSpec((tile, columns), lambda i: (i, 0))] * len(received)
-        + [pl.BlockSpec((extra, columns), lambda i: (rows // extra, 0))] * len(received)
+        + tails * len(received)
         + [pl.BlockSpec(memory_space=pl.ANY)] * len(after),
-        out_specs=pl.BlockSpec((rows + extra, columns), lambda i: (0, 0)),
-        out_shape=jax.ShapeDtypeStruct((rows + extra, columns), jnp.bfloat16),
+        out_specs=[pl.BlockSpec((rows + extra, columns), lambda i: (0, 0)), MARK],
+        out_shape=[jax.ShapeDtypeStruct((rows + extra, columns), jnp.bfloat16), MARK_SHAPE],
         compiler_params=pltpu.CompilerParams(vmem_limit_bytes=VMEM),
         cost_estimate=LIGHT,
         name="project",
-    )(x, halo, *weights, *received, *received, *after)
-
-
-def mix_kernel(feat, filt, qh, kh, vh, q, k, v, taps, out_ref, mark_ref, ext, prod):
-    rows = q.shape[0]
+    )(x, *halo, *weights, *received, *(received if halo else ()), *after)
+
+
+def mix_kernel(feat, filt, qh, kh, vh, qa, ka, va, qb, kb, vb, taps, out_ref, mark_ref, ext, prod):
+    half = qa.shape[0]
+    rows = 2 * half
     mark_ref[...] = jnp.zeros_like(mark_ref)
-    for i, (h, b) in enumerate(((qh, q), (kh, k), (vh, v))):
+    for i, (h, a, b) in enumerate(((qh, qa, qb), (kh, ka, kb), (vh, va, vb))):
         ext[i, :HALO, :] = h[...].astype(jnp.float32)
-        ext[i, HALO:, :] = b[...].astype(jnp.float32)
+        ext[i, HALO : HALO + half, :] = a[...].astype(jnp.float32)
+        ext[i, HALO + half :, :] = b[...].astype(jnp.float32)
     tile = min(rows, 128)
 
     def featured(i, start, size):
@@ -97,7 +104,8 @@
 
 
 def short_mix(projected, taps, feat, filt):
-    rows, width = projected.shape[0] - HALO, projected.shape[1] // 3
+    half, width = projected[1].shape[0], projected[1].shape[1] // 3
+    rows = 2 * half
     lanes = LANES
     steps = width // lanes
 
@@ -108,8 +116,8 @@
     return pl.pallas_call(
         functools.partial(mix_kernel, feat, filt),
         grid=(steps,),
-        in_specs=[part(i, HALO, rows // HALO) for i in range(3)]
-        + [part(i, rows, 0) for i in range(3)]
+        in_specs=[part(i, HALO, half // HALO) for i in range(3)]
+        + [part(i, half, 0) for i in range(3)] * 2
         + [pl.BlockSpec((taps.shape[0], lanes), lambda b: (0, b))],
         out_specs=[pl.BlockSpec((rows, lanes), lambda b: (0, b)), MARK],
         out_shape=[jax.ShapeDtypeStruct((rows, width), jnp.bfloat16), MARK_SHAPE],
@@ -120,17 +128,20 @@
         compiler_params=pltpu.CompilerParams(vmem_limit_bytes=VMEM),
         cost_estimate=LIGHT,
         name="short_mix",
-    )(*[projected] * 6, taps)
-
-
-def out_kernel(blocks, count, columns, order, *refs):
+    )(*projected[:1] * 6, *projected[1:] * 3, taps)
+
+
+def out_kernel(blocks, columns, count, order, *refs):
     gated = refs[:count]
-    weights = refs[count : count + blocks * columns]
-    held, out_ref = refs[count + blocks * columns : -1], refs[-1]
+    weights = refs[count : count + columns * blocks]
+    held, out_ref = refs[count + columns * blocks : -1], refs[-1]
     per_block, _, wide = weights[0].shape
     for m in range(columns):
-        cut = slice(m * wide, (m + 1) * wide)
-        total = held[0][:, cut] if held else jnp.zeros((out_ref.shape[0], wide), jnp.float32)
+        if held:
+            each = columns // len(held)
+            total = held[m // each][:, m % each * wide : (m % each + 1) * wide]
+        else:
+            total = jnp.zeros((out_ref.shape[0], wide), jnp.float32)
         for b in range(blocks):
             for i in range(per_block):
                 row = 0
@@ -142,7 +153,7 @@
                         preferred_element_type=jnp.float32,
                     )
                     row += size
-        out_ref[:, cut] = total.astype(out_ref.dtype)
+        out_ref[:, m * wide : (m + 1) * wide] = total.astype(out_ref.dtype)
 
 
 def out_project(order, gated, start, weights, kind, held=()):
@@ -151,20 +162,21 @@
     per_block, _, wide = weights[0][0].shape
     columns, blocks = len(weights), len(weights[0])
     tile = min(rows, 256)
-    cell = pl.BlockSpec((tile, columns * wide), lambda i, o: (i, 0))
     piece = pl.BlockSpec(
         (per_block, size, wide), lambda i, o: (0, start // size, 0), pipeline_mode=pl.Buffered(1)
     )
     spec = pltpu.PrefetchScalarGridSpec(
         num_scalar_prefetch=1,
         grid=(rows // tile,),
-        in_specs=[pl.BlockSpec((chans, tile, block.shape[2]), lambda i, o: (0, i, 0)) for block in gated]
+        in_specs=[
+            pl.BlockSpec((chans, tile, block.shape[2]), lambda i, o: (0, i, 0)) for block in gated
+        ]
         + [piece] * (columns * blocks)
-        + [cell] * len(held),
-        out_specs=cell,
+        + [pl.BlockSpec((tile, block.shape[1]), lambda i, o: (i, 0)) for block in held],
+        out_specs=pl.BlockSpec((tile, columns * wide), lambda i, o: (i, 0)),
     )
     return pl.pallas_call(
-        functools.partial(out_kernel, blocks, len(gated), columns),
+        functools.partial(out_kernel, blocks, columns, len(gated)),
         grid_spec=spec,
         out_shape=jax.ShapeDtypeStruct((rows, columns * wide), kind),
         compiler_params=pltpu.CompilerParams(vmem_limit_bytes=VMEM),
@@ -227,41 +239,48 @@
     pieces = [
         from_far(columns_of(part, (e - k) % far), k) for k in range(1, far)
     ]
-    pieces, rows, owns, near_rows[0] = together((pieces, rows, owns, near_rows[0]))
+    pieces, before, rows, owns, near_rows[0] = together(
+        (pieces, before, rows, owns, near_rows[0])
+    )
     theirs = [lax.all_gather(piece, "chan", axis=0, tiled=True) for piece in pieces]
     before = normalised(before, norm_gain)
     theirs_before = [from_far(columns_of(before, (e - k) % far), k) for k in range(1, far)]
-    mine = columns_of(normalised(x_rows, norm_gain), e)
+    taps = jnp.concatenate([feat_filter.reshape(feat * 3, chans_here), inner_filter], axis=0)
+    across = [[from_far(block, a) for a in range(1, far)] for block in rows]
+    x_rows, across[0] = together((x_rows, across[0]))
+    normed, across[1] = together((normalised(x_rows, norm_gain), across[1]))
+    mine = columns_of(normed, e)
     mine_before = columns_of(before, e)
-    taps = jnp.concatenate([feat_filter.reshape(feat * 3, chans_here), inner_filter], axis=0)
-
-    across = [[from_far(block, a) for a in range(1, far)] for block in rows]
     theirs, theirs_before, weights[0], mine, mine_before, across = together(
         (theirs, theirs_before, weights[0], mine, mine_before, across)
     )
 
-    gated, done = [], []
+    def beyond(m):
+        return [[from_far(block, a) for block in near_rows[m]] for a in range(1, far)]
+
+    gated, done, diagonal = [], [], []
     for j in range(CHUNKS):
-        sums = [
-            from_far(project(theirs[k], theirs_before[k], weights[j], after=done), far - 1 - k)
-            for k in range(far - 1)
-        ]
-        projected = project(mine, mine_before, weights[j], sums)
+        sums, after = [], list(done)
+        for half in (0, 1):
+            made = [
+                project(theirs[k], half, [] if half else [theirs_before[k]], weights[j], after=after)
+                for k in range(far - 1)
+            ]
+            after = [mark for _, mark in made]
+            sums.append([from_far(made[k][0], far - 1 - k) for k in range(far - 1)])
+        first, mark = project(mine, 0, [mine_before], weights[j], sums[0])
+        second, _ = project(mine, 1, [], weights[j], sums[1], after=[mark])
+        projected = [first, second]
         if j == 0:
             projected, weights[1], near_rows[1] = together((projected, weights[1], near_rows[1]))
-            beyond = [
-                [from_far(block, a) for a in range(1, far) for block in found] for found in near_rows[:2]
-            ]
         elif j < CHUNKS - 1:
-            turn = min(j - 1, 1)
-            projected, weights[j + 1], beyond[turn] = together(
-                (projected, weights[j + 1], beyond[turn])
+            diagonal.append(beyond(j - 1))
+            projected, weights[j + 1], diagonal[-1] = together(
+                (projected, weights[j + 1], diagonal[-1])
             )
         else:
             projected, near_rows[2:] = together((projected, near_rows[2:]))
-            beyond += [
-                [from_far(block, a) for a in range(1, far) for block in found] for found in near_rows[2:]
-            ]
+            diagonal += [beyond(2), beyond(3)]
         mixed, mark = short_mix(projected, taps[:, cuts[j]], feat, filt)
         done = [mark]
         if j > 0:
@@ -275,19 +294,17 @@
     for m in range(OUT_CHUNKS):
         found = [rows[m]] + near_rows[m]
         for a in range(1, far):
-            found += [across[m][a - 1]] + beyond[m][(a - 1) * (near - 1) : a * (near - 1)]
+            found += [across[m][a - 1]] + diagonal[m][a - 1]
         blocks.append([block.reshape(-1, chans_here, block.shape[1]) for block in found])
     half = OUT_CHUNKS // 2
-    sums = [
-        out_project(order, gated[:-1], 0, found, jnp.float32) for found in (blocks[:half], blocks[half:])
-    ]
-    sums, last = together((sums, gated[-1]))
-    outs = [
-        out_project(order, [last], edges[CHUNKS - 1], found, jnp.bfloat16, [total])
-        for found, total in zip((blocks[:half], blocks[half:]), sums)
-    ]
-    out = jnp.concatenate(outs, axis=1).reshape(chans, share, -1)
-    got = lax.all_to_all(out, "chan", split_axis=0, concat_axis=0, tiled=True)
+    first = out_project(order, gated[:-1], 0, blocks[:half], jnp.float32)
+    first, blocks[half:] = together((first, blocks[half:]))
+    second = out_project(order, gated[:-1], 0, blocks[half:], jnp.float32)
+    first, second, last = together((first, second, gated[-1]))
+    out = out_project(order, [last], edges[CHUNKS - 1], blocks, jnp.bfloat16, [first, second])
+    got = lax.all_to_all(
+        out.reshape(chans, share, -1), "chan", split_axis=0, concat_axis=0, tiled=True
+    )
     return got.transpose(1, 0, 2).reshape(share, -1)
 
 

time: 696 us -> 540 us (0.78)
  waiting for transfers between devices: 372 us -> 210 us
  local copies, waits for them, and re-layouts: 24.3 us -> 41.3 us
  Pallas kernels: 159 us -> 148 us
    ppermute x1, waiting for transfers between devices: 110 us -> 19.4 us  [per_device(): lax.ppermute(x_rows[tokens - HALO:], 'seq', [(a, a + 1) for a in range(se...]
    ppermute x14 -> x18, waiting for transfers between devices: 258 us -> 181 us  [from_far(): return lax.ppermute(block, 'seq', pairs)]
    unnamed x30 -> x58, local copies, waits for them, and re-layouts: 5.1 us -> 23.5 us
    pallas_call x4 -> x3, Pallas kernels: 40 us -> 32 us  [out_project(): pl.pallas_call(functools.partial(out_kernel, blocks, columns, len(gated))...]
    pallas_call x8 -> x16, Pallas kernels: 105 us -> 108 us  [project(): pl.pallas_call(functools.partial(project_kernel, len(weights), len(receiv...]
    ppermute x14 -> x18, starting transfers between devices: 18.5 us -> 20.5 us  [from_far(): return lax.ppermute(block, 'seq', pairs)]
  transfers between devices with their start and end apart: 28 -> 32, of which waited for: 15 -> 16; matrix products, arithmetic and copies ran while one was open for 7% -> 9% of each run, Pallas kernels for 20% -> 25%
where the time goes in v5:
time: 540 us; the launch traced here: 536 us
  waiting for transfers between devices  210 us (39%)
  Pallas kernels  148 us (27%)
  blocking collectives  52.6 us (10%)
  local copies, waits for them, and re-layouts  41.3 us (8%)
  starting transfers between devices  36 us (7%)
  other arithmetic  35.5 us (7%)
  between operations  13.8 us (3%)
    ppermute x18, waiting for transfers between devices, from_far(): return lax.ppermute(block, 'seq', pairs)  181 us
    pallas_call x16, Pallas kernels, project(): pl.pallas_call(functools.partial(project_kernel, len(weights), len(receiv...  108 us
    all_to_all x1, blocking collectives, per_device(): lax.all_to_all(out.reshape(chans, share, -1), 'chan', split_axis=0, conca...  52.6 us
    pallas_call x3, Pallas kernels, out_project(): pl.pallas_call(functools.partial(out_kernel, blocks, columns, len(gated))...  32 us
    unnamed x58, local copies, waits for them, and re-layouts  23.5 us
    ppermute x18, starting transfers between devices, from_far(): return lax.ppermute(block, 'seq', pairs)  20.5 us
    ppermute x1, waiting for transfers between devices, per_device(): lax.ppermute(x_rows[tokens - HALO:], 'seq', [(a, a + 1) for a in range(se...  19.4 us
    convert_element_type x3, other arithmetic, normalised(): return (values * lax.rsqrt(squares + 1e-06) * gain).astype(jnp.bfloat16)  17.7 us
  transfers between devices with their start and end apart: 32, of which 16 were waited for; matrix products, arithmetic and copies ran while one was open for 9% of the time, Pallas kernels for 25%

profile of v5, /device:TPU:0, one launch (start us, length us, event | category | flops | bytes accessed | tf_op | source)
XLA Modules:
  0.0 536.5 jit_solution(875685004757944354)
XLA Ops:
  26.6 19.4 %collective-permute-done.1 = bf16[16,8192]{1,0:T(8,128)(2,1)S(1)} collective-permute-done((bf16[16,8192]{1,0:T(8,128)(2,1)S(1)}, bf16[16,8192]{1,0:T(8,128)(2,1)S(1)}, u32[]{:S(2)}, u32[]{:S(2)}) %collective-permute-start.1) | collective-permute-done | bytes 262176 | tf_op jit(solution)/shard_map/ppermute | solution.py:235
  53.6 21.9 %collective-permute-done.5 = bf16[2048,256]{1,0:T(8,128)(2,1)S(1)} collective-permute-done((bf16[2048,256]{1,0:T(8,128)(2,1)}, bf16[2048,256]{1,0:T(8,128)(2,1)S(1)}, u32[]{:S(2)}, u32[]{:S(2)}) %collective-permute-start.5) | collective-permute-done | bytes 1048608 | tf_op jit(solution)/shard_map/ppermute | solution.py:210
  78.4 7.3 %fusion = f32[1024]{0:T(1024)S(1)} fusion(bf16[1024,8192]{1,0:T(8,128)(2,1)} %param.6), kind=kLoop, calls=%fused_computation.2 | loop fusion | flops 25164800 | bytes 16781312 | tf_op jit(solution)/shard_map/reduce_sum | solution.py:190
  85.8 15.3 %fusion.2 = bf16[1024,8192]{1,0:T(8,128)(2,1)} fusion(bf16[1024,8192]{1,0:T(8,128)(2,1)} %param.6, f32[8192]{0:T(1024)S(1)} %copy-done.26, f32[1024]{0:T(1024)S(1)} %add_rsqrt_fusion), kind=kLoop, calls=%fused_computation.4 | loop fusion | flops 33554432 | bytes 33591296 | tf_op jit(solution)/shard_map/convert_element_type | solution.py:191
  102.1 8.5 %constant_dynamic-slice_fusion.3 = (bf16[1024,2048]{1,0:T(8,128)(2,1)}, bf16[1024,2048]{1,0:T(8,128)(2,1)}) fusion(bf16[1024,8192]{1,0:T(8,128)(2,1)} %fusion.2, s32[]{:T(128)S(6)} %select_n.86, s32[]{:T(128)S(6)} %select_n.87), kind=kLoop, calls=%fused_computation.37 | loop fusion | bytes 16777224 | tf_op jit(solution)/shard_map/dynamic_slice | solution.py:215
  110.6 32.6 %collective-permute-done.3.refs_1_ = bf16[16,4096]{1,0:T(8,128)(2,1)S(1)} collective-permute-done((bf16[16,4096]{1,0:T(8,128)(2,1)S(1)}, bf16[16,4096]{1,0:T(8,128)(2,1)S(1)}, u32[]{:S(2)}, u32[]{:S(2)}) %collective-permute-start.3) | collective-permute-done | bytes 131104 | tf_op jit(solution)/shard_map/ppermute | solution.py:210
  144.7 7.9 %pad_maximum_fusion.refs_0_ = bf16[1024,4096]{1,0:T(8,128)(2,1)} fusion(bf16[1024,2048]{1,0:T(8,128)(2,1)} %get-tuple-element.188, bf16[1024,2048]{1,0:T(8,128)(2,1)} %get-tuple-element.187), kind=kLoop, calls=%fused_computation.5 | loop fusion | flops 16777216 | bytes 16777216 | tf_op jit(solution)/shard_map/concatenate | solution.py:213
  152.7 7.9 %project.16 = (bf16[528,768]{1,0:T(8,128)(2,1)}, f32[8,128]{1,0:T(8,128)S(1)}) custom-call(bf16[1024,4096]{1,0:T(8,128)(2,1)} %all-gather.10.cloned.1.call-done.refs_0_, bf16[16,4096]{1,0:T(8,128)(2,1)S(1)} %collective-permute-done.3.refs_1_, bf16[3,2048,256]{2,1,0:T(8,128)(2,1)S(1)} %slice_bitcast_fusion.3.refs_2_.refs_1_, ...), custom_call_target="tpu_custom_call" | custom-call | flops 1024 | bytes 1024 | tf_op jit(solution)/shard_map/project/pallas_call | solution.py:64
  161.2 7.0 %project.18 = (bf16[512,768]{1,0:T(8,128)(2,1)}, f32[8,128]{1,0:T(8,128)}) custom-call(bf16[1024,4096]{1,0:T(8,128)(2,1)} %all-gather.10.cloned.1.call-done.refs_0_, bf16[3,2048,256]{2,1,0:T(8,128)(2,1)S(1)} %slice_bitcast_fusion.3.refs_2_.refs_1_, bf16[3,2048,256]{2,1,0:T(8,128)(2,1)} %collective-permute-done.4.refs_3_.refs_2_, ...), custom_call_target="tpu_custom_call" | custom-call | flops 1024 | bytes 1024 | tf_op jit(solution)/shard_map/project/pallas_call | solution.py:64
  169.8 12.2 %collective-permute-done.9.refs_4_.refs_5_ = bf16[528,768]{1,0:T(8,128)(2,1)} collective-permute-done((bf16[528,768]{1,0:T(8,128)(2,1)}, bf16[528,768]{1,0:T(8,128)(2,1)}, u32[]{:S(2)}, u32[]{:S(2)}) %collective-permute-start.9) | collective-permute-done | bytes 811040 | tf_op jit(solution)/shard_map/ppermute | solution.py:210
  182.0 7.2 %project.17 = (bf16[528,768]{1,0:T(8,128)(2,1)S(1)}, f32[8,128]{1,0:T(8,128)S(1)}) custom-call(bf16[1024,4096]{1,0:T(8,128)(2,1)} %pad_maximum_fusion.refs_0_, bf16[16,4096]{1,0:T(8,128)(2,1)S(1)} %pad_maximum_fusion.3.refs_1_, bf16[3,2048,256]{2,1,0:T(8,128)(2,1)S(1)} %slice_bitcast_fusion.3.refs_2_.refs_1_, ...), custom_call_target="tpu_custom_call" | custom-call | flops 1024 | bytes 1024 | tf_op jit(solution)/shard_map/project/pallas_call | solution.py:64
  194.8 6.8 %project.19 = (bf16[512,768]{1,0:T(8,128)(2,1)S(1)}, f32[8,128]{1,0:T(8,128)}) custom-call(bf16[1024,4096]{1,0:T(8,128)(2,1)} %pad_maximum_fusion.refs_0_, bf16[3,2048,256]{2,1,0:T(8,128)(2,1)S(1)} %slice_bitcast_fusion.3.refs_2_.refs_1_, bf16[3,2048,256]{2,1,0:T(8,128)(2,1)} %collective-permute-done.4.refs_3_.refs_2_, ...), custom_call_target="tpu_custom_call" | custom-call | flops 1024 | bytes 1024 | tf_op jit(solution)/shard_map/project/pallas_call | solution.py:64
  211.2 7.0 %project.20 = (bf16[528,768]{1,0:T(8,128)(2,1)S(1)}, f32[8,128]{1,0:T(8,128)S(1)}) custom-call(bf16[1024,4096]{1,0:T(8,128)(2,1)} %all-gather.10.cloned.1.call-done.refs_0_, bf16[16,4096]{1,0:T(8,128)(2,1)S(1)} %collective-permute-done.3.refs_1_, bf16[3,2048,256]{2,1,0:T(8,128)(2,1)S(1)} %copy-done.1, ...), custom_call_target="tpu_custom_call" | custom-call | flops 1024 | bytes 1024 | tf_op jit(solution)/shard_map/project/pallas_call | solution.py:64
  219.9 6.7 %project.22 = (bf16[512,768]{1,0:T(8,128)(2,1)S(1)}, f32[8,128]{1,0:T(8,128)}) custom-call(bf16[1024,4096]{1,0:T(8,128)(2,1)} %all-gather.10.cloned.1.call-done.refs_0_, bf16[3,2048,256]{2,1,0:T(8,128)(2,1)S(1)} %copy-done.1, bf16[3,2048,256]{2,1,0:T(8,128)(2,1)} %collective-permute-done.11.refs_3_.refs_2_, f32[8,128]{1,0:T(8,128)S(1)} %get-tuple-element.127.refs_3_), custom_call_target="tpu_custom_call" | custom-call | flops 1024 | bytes 1024 | tf_op jit(solution)/shard_map/project/pallas_call | solution.py:64
  227.1 27.3 %collective-permute-done.13.refs_4_.refs_5_ = bf16[528,768]{1,0:T(8,128)(2,1)S(1)} collective-permute-done((bf16[528,768]{1,0:T(8,128)(2,1)S(1)}, bf16[528,768]{1,0:T(8,128)(2,1)S(1)}, u32[]{:S(2)}, u32[]{:S(2)}) %collective-permute-start.13) | collective-permute-done | bytes 811040 | tf_op jit(solution)/shard_map/ppermute | solution.py:210
  254.4 7.1 %project.21 = (bf16[528,768]{1,0:T(8,128)(2,1)S(1)}, f32[8,128]{1,0:T(8,128)S(1)}) custom-call(bf16[1024,4096]{1,0:T(8,128)(2,1)} %pad_maximum_fusion.refs_0_, bf16[16,4096]{1,0:T(8,128)(2,1)S(1)} %pad_maximum_fusion.3.refs_1_, bf16[3,2048,256]{2,1,0:T(8,128)(2,1)S(1)} %copy-done.1, bf16[3,2048,256]{2,1,0:T(8,128)(2,1)} %collective-permute-done.11.refs_3_.refs_2_, ...), custom_call_target="tpu_custom_call" | custom-call | flops 1024 | bytes 1024 | tf_op jit(solution)/shard_map/project/pallas_call | solution.py:64
  261.5 6.2 %collective-permute-done.14.refs_3_ = bf16[512,768]{1,0:T(8,128)(2,1)S(1)} collective-permute-done((bf16[512,768]{1,0:T(8,128)(2,1)S(1)}, bf16[512,768]{1,0:T(8,128)(2,1)S(1)}, u32[]{:S(2)}, u32[]{:S(2)}) %collective-permute-start.14) | collective-permute-done | bytes 786464 | tf_op jit(solution)/shard_map/ppermute | solution.py:210
  267.7 6.7 %project.23 = (bf16[512,768]{1,0:T(8,128)(2,1)S(1)}, f32[8,128]{1,0:T(8,128)}) custom-call(bf16[1024,4096]{1,0:T(8,128)(2,1)} %pad_maximum_fusion.refs_0_, bf16[3,2048,256]{2,1,0:T(8,128)(2,1)S(1)} %copy-done.1, bf16[3,2048,256]{2,1,0:T(8,128)(2,1)} %collective-permute-done.11.refs_3_.refs_2_, bf16[512,768]{1,0:T(8,128)(2,1)S(1)} %collective-permute-done.14.refs_3_, ...), custom_call_target="tpu_custom_call" | custom-call | flops 1024 | bytes 1024 | tf_op jit(solution)/shard_map/project/pallas_call | solution.py:64
  285.9 7.0 %project.24 = (bf16[528,768]{1,0:T(8,128)(2,1)S(1)}, f32[8,128]{1,0:T(8,128)S(1)}) custom-call(bf16[1024,4096]{1,0:T(8,128)(2,1)} %all-gather.10.cloned.1.call-done.refs_0_, bf16[16,4096]{1,0:T(8,128)(2,1)S(1)} %collective-permute-done.3.refs_1_, bf16[3,2048,256]{2,1,0:T(8,128)(2,1)} %get-tuple-element.137.refs_2_.refs_1_, ...), custom_call_target="tpu_custom_call" | custom-call | flops 1024 | bytes 1024 | tf_op jit(solution)/shard_map/project/pallas_call | solution.py:64
  294.4 6.7 %project.26 = (bf16[512,768]{1,0:T(8,128)(2,1)S(1)}, f32[8,128]{1,0:T(8,128)}) custom-call(bf16[1024,4096]{1,0:T(8,128)(2,1)} %all-gather.10.cloned.1.call-done.refs_0_, bf16[3,2048,256]{2,1,0:T(8,128)(2,1)} %get-tuple-element.137.refs_2_.refs_1_, bf16[3,2048,256]{2,1,0:T(8,128)(2,1)S(1)} %copy-done.5, f32[8,128]{1,0:T(8,128)S(1)} %get-tuple-element.142.refs_3_), custom_call_target="tpu_custom_call" | custom-call | flops 1024 | bytes 1024 | tf_op jit(solution)/shard_map/project/pallas_call | solution.py:64
  301.7 25.3 %collective-permute-done.17.refs_4_.refs_5_ = bf16[528,768]{1,0:T(8,128)(2,1)S(1)} collective-permute-done((bf16[528,768]{1,0:T(8,128)(2,1)S(1)}, bf16[528,768]{1,0:T(8,128)(2,1)S(1)}, u32[]{:S(2)}, u32[]{:S(2)}) %collective-permute-start.17) | collective-permute-done | bytes 811040 | tf_op jit(solution)/shard_map/ppermute | solution.py:210
  327.1 7.1 %project.25 = (bf16[528,768]{1,0:T(8,128)(2,1)S(1)}, f32[8,128]{1,0:T(8,128)S(1)}) custom-call(bf16[1024,4096]{1,0:T(8,128)(2,1)} %pad_maximum_fusion.refs_0_, bf16[16,4096]{1,0:T(8,128)(2,1)S(1)} %pad_maximum_fusion.3.refs_1_, bf16[3,2048,256]{2,1,0:T(8,128)(2,1)} %get-tuple-element.137.refs_2_.refs_1_, bf16[3,2048,256]{2,1,0:T(8,128)(2,1)S(1)} %copy-done.5, ...), custom_call_target="tpu_custom_call" | custom-call | flops 1024 | bytes 1024 | tf_op jit(solution)/shard_map/project/pallas_call | solution.py:64
  339.4 6.7 %project.27 = (bf16[512,768]{1,0:T(8,128)(2,1)S(1)}, f32[8,128]{1,0:T(8,128)}) custom-call(bf16[1024,4096]{1,0:T(8,128)(2,1)} %pad_maximum_fusion.refs_0_, bf16[3,2048,256]{2,1,0:T(8,128)(2,1)} %get-tuple-element.137.refs_2_.refs_1_, bf16[3,2048,256]{2,1,0:T(8,128)(2,1)S(1)} %copy-done.5, bf16[512,768]{1,0:T(8,128)(2,1)S(1)} %collective-permute-done.18.refs_3_, ...), custom_call_target="tpu_custom_call" | custom-call | flops 1024 | bytes 1024 | tf_op jit(solution)/shard_map/project/pallas_call | solution.py:64
  358.5 6.1 %project.28 = (bf16[528,768]{1,0:T(8,128)(2,1)S(1)}, f32[8,128]{1,0:T(8,128)S(1)}) custom-call(bf16[1024,4096]{1,0:T(8,128)(2,1)} %all-gather.10.cloned.1.call-done.refs_0_, bf16[16,4096]{1,0:T(8,128)(2,1)S(1)} %collective-permute-done.3.refs_1_, bf16[3,2048,256]{2,1,0:T(8,128)(2,1)S(1)} %copy-done, bf16[3,2048,256]{2,1,0:T(8,128)(2,1)S(1)} %copy-done.3, ...), custom_call_target="tpu_custom_call" | custom-call | flops 1024 | bytes 1024 | tf_op jit(solution)/shard_map/project/pallas_call | solution.py:64
  372.5 13.2 %collective-permute-done.21.refs_4_.refs_5_ = bf16[528,768]{1,0:T(8,128)(2,1)S(1)} collective-permute-done((bf16[528,768]{1,0:T(8,128)(2,1)S(1)}, bf16[528,768]{1,0:T(8,128)(2,1)S(1)}, u32[]{:S(2)}, u32[]{:S(2)}) %collective-permute-start.21) | collective-permute-done | bytes 811040 | tf_op jit(solution)/shard_map/ppermute | solution.py:210
  385.7 6.1 %project.29 = (bf16[528,768]{1,0:T(8,128)(2,1)S(1)}, f32[8,128]{1,0:T(8,128)S(1)}) custom-call(bf16[1024,4096]{1,0:T(8,128)(2,1)} %pad_maximum_fusion.refs_0_, bf16[16,4096]{1,0:T(8,128)(2,1)S(1)} %pad_maximum_fusion.3.refs_1_, bf16[3,2048,256]{2,1,0:T(8,128)(2,1)S(1)} %copy-done, bf16[3,2048,256]{2,1,0:T(8,128)(2,1)S(1)} %copy-done.3, ...), custom_call_target="tpu_custom_call" | custom-call | flops 1024 | bytes 1024 | tf_op jit(solution)/shard_map/project/pallas_call | solution.py:64
  411.3 11.4 %out_project.3.refs_17_ = f32[1024,512]{1,0:T(8,128)S(1)} custom-call(s32[4]{0:T(128)S(1)} %pad_add_fusion.order, bf16[8,1024,256]{2,1,0:T(8,128)(2,1)} %bitcast.48, bf16[8,1024,256]{2,1,0:T(8,128)(2,1)} %bitcast.50, bf16[8,1024,256]{2,1,0:T(8,128)(2,1)} %bitcast.52, bf16[2,1024,256]{2,1,0:T(8,128)(2,1)} %bitcast.11.refs_3_.refs_1_, ...), custom_call_target="tpu_custom_call" | custom-call | flops 1024 | bytes 1024 | tf_op jit(solution)/shard_map/out_project/pallas_call | solution.py:178
  424.0 7.9 %collective-permute-done.25 = bf16[2048,256]{1,0:T(8,128)(2,1)} collective-permute-done((bf16[2048,256]{1,0:T(8,128)(2,1)}, bf16[2048,256]{1,0:T(8,128)(2,1)}, u32[]{:S(2)}, u32[]{:S(2)}) %collective-permute-start.25) | collective-permute-done | bytes 1048608 | tf_op jit(solution)/shard_map/ppermute | solution.py:210
  431.9 18.1 %collective-permute-done.26 = bf16[2048,256]{1,0:T(8,128)(2,1)} collective-permute-done((bf16[2048,256]{1,0:T(8,128)(2,1)}, bf16[2048,256]{1,0:T(8,128)(2,1)}, u32[]{:S(2)}, u32[]{:S(2)}) %collective-permute-start.26) | collective-permute-done | bytes 1048608 | tf_op jit(solution)/shard_map/ppermute | solution.py:210
  450.0 11.3 %out_project.4.refs_18_ = f32[1024,512]{1,0:T(8,128)S(1)} custom-call(s32[4]{0:T(128)S(1)} %pad_add_fusion.order, bf16[8,1024,256]{2,1,0:T(8,128)(2,1)} %bitcast.49, bf16[8,1024,256]{2,1,0:T(8,128)(2,1)} %bitcast.51, bf16[8,1024,256]{2,1,0:T(8,128)(2,1)} %bitcast.53, bf16[2,1024,256]{2,1,0:T(8,128)(2,1)S(1)} %bitcast.38, ...), custom_call_target="tpu_custom_call" | custom-call | flops 1024 | bytes 1024 | tf_op jit(solution)/shard_map/out_project/pallas_call | solution.py:178
  466.2 9.4 %out_project.5 = bf16[1024,1024]{1,0:T(8,128)(2,1)} custom-call(s32[4]{0:T(128)S(1)} %pad_add_fusion.order, bf16[8,1024,256]{2,1,0:T(8,128)(2,1)} %bitcast.56, bf16[2,1024,256]{2,1,0:T(8,128)(2,1)} %bitcast.11.refs_3_.refs_1_, bf16[2,1024,256]{2,1,0:T(8,128)(2,1)} %bitcast.12.refs_4_.refs_2_, bf16[2,1024,256]{2,1,0:T(8,128)(2,1)S(1)} %bitcast.41, ...), custom_call_target="tpu_custom_call" | custom-call | flops 1024 | bytes 1024 | tf_op jit(solution)/shard_map/out_project/pallas_call | solution.py:178
  475.6 52.6 %all_to_all.5 = bf16[8,128,1024]{2,1,0:T(8,128)(2,1)S(1)} all-to-all(bf16[8,128,1024]{2,1,0:T(8,128)(2,1)} %bitcast.54), channel_id=1, replica_groups=mesh['seq'=4,'chan'=8] {'chan'}, dimensions={0} | all-to-all | bytes 4194304 | tf_op jit(solution)/shard_map/all_to_all | solution.py:305
  (143 shorter events, 118.7 us)
Async XLA Ops:
  6.5 146.2 %all-gather.10.cloned.1.call-start = ((), (), s32[]{:S(2)}) async-start(), calls=%async_computation.1 | async-start | bytes 9437184 | tf_op jit(solution)/shard_map/all_gather | solution.py:245
  11.2 34.8 %collective-permute-start = (bf16[128,4096]{1,0:T(8,128)(2,1)S(1)}, bf16[128,4096]{1,0:T(8,128)(2,1)}, u32[]{:S(2)}, u32[]{:S(2)}) collective-permute-start(bf16[128,4096]{1,0:T(8,128)(2,1)S(1)} %pad_maximum_fusion.1), channel_id=1, source_target_pairs={{16,0},{24,8},{0,16},{8,24},{17,1},{25,9},{1,17},{9,25},{18,2},{26... | collective-permute-start | bytes 3145736 | tf_op jit(solution)/shard_map/ppermute | solution.py:210
  16.4 29.6 %collective-permute-start.2 = (bf16[2048,256]{1,0:T(8,128)(2,1)}, bf16[2048,256]{1,0:T(8,128)(2,1)}, u32[]{:S(2)}, u32[]{:S(2)}) collective-permute-start(bf16[2048,256]{1,0:T(8,128)(2,1)} %get-tuple-element.100), channel_id=1, source_target_pairs={{8,0},{0,8},{24,16},{16,24},{9,1},{1,9},{25,17},{17,25},{10,2},{2,... | collective-permute-start | bytes 3145736 | tf_op jit(solution)/shard_map/ppermute | solution.py:206
  19.0 27.0 %collective-permute-start.1 = (bf16[16,8192]{1,0:T(8,128)(2,1)S(1)}, bf16[16,8192]{1,0:T(8,128)(2,1)S(1)}, u32[]{:S(2)}, u32[]{:S(2)}) collective-permute-start(bf16[16,8192]{1,0:T(8,128)(2,1)S(1)} %slice.39), channel_id=1, source_target_pairs={{0,8},{8,16},{16,24},{1,9},{9,17},{17,25},{2,10},{10,18},{18,26},{... | collective-permute-start | bytes 786440 | tf_op jit(solution)/shard_map/ppermute | solution.py:235
  46.0 235.5 %all-gather.12.cloned.1.call-start = ((), (), s32[]{:S(2)}) async-start(), calls=%async_computation.2 | async-start | bytes 4718592 | tf_op jit(solution)/shard_map/all_gather | solution.py:288
  46.6 106.1 %collective-permute-start.4 = (bf16[3,2048,256]{2,1,0:T(8,128)(2,1)S(1)}, bf16[3,2048,256]{2,1,0:T(8,128)(2,1)}, u32[]{:S(2)}, u32[]{:S(2)}) collective-permute-start(bf16[3,2048,256]{2,1,0:T(8,128)(2,1)S(1)} %slice_bitcast_fusion.3.refs_2_.refs_1_), channel_id=1, source_target_pairs={{8,0},{0,8},{24,16},{16,24},{9,1},{1,9},{25,17},{17,25},{10,2},{2,... | collective-permute-start | bytes 9437192 | tf_op jit(solution)/shard_map/ppermute | solution.py:206
  49.1 156.9 %collective-permute-start.11 = (bf16[3,2048,256]{2,1,0:T(8,128)(2,1)}, bf16[3,2048,256]{2,1,0:T(8,128)(2,1)}, u32[]{:S(2)}, u32[]{:S(2)}) collective-permute-start(bf16[3,2048,256]{2,1,0:T(8,128)(2,1)} %get-tuple-element.120.refs_2_.refs_1_), channel_id=1, source_target_pairs={{8,0},{0,8},{24,16},{16,24},{9,1},{1,9},{25,17},{17,25},{10,2},{2,... | collective-permute-start | bytes 9437192 | tf_op jit(solution)/shard_map/ppermute | solution.py:206
  49.2 26.3 %collective-permute-start.5 = (bf16[2048,256]{1,0:T(8,128)(2,1)}, bf16[2048,256]{1,0:T(8,128)(2,1)S(1)}, u32[]{:S(2)}, u32[]{:S(2)}) collective-permute-start(bf16[2048,256]{1,0:T(8,128)(2,1)} %get-tuple-element.100), channel_id=1, source_target_pairs={{16,0},{24,8},{0,16},{8,24},{17,1},{25,9},{1,17},{9,25},{18,2},{26... | collective-permute-start | bytes 3145736 | tf_op jit(solution)/shard_map/ppermute | solution.py:210
  51.1 49.9 %collective-permute-start.6 = (bf16[2048,256]{1,0:T(8,128)(2,1)}, bf16[2048,256]{1,0:T(8,128)(2,1)S(1)}, u32[]{:S(2)}, u32[]{:S(2)}) collective-permute-start(bf16[2048,256]{1,0:T(8,128)(2,1)} %get-tuple-element.102), channel_id=1, source_target_pairs={{16,0},{24,8},{0,16},{8,24},{17,1},{25,9},{1,17},{9,25},{18,2},{26... | collective-permute-start | bytes 3145736 | tf_op jit(solution)/shard_map/ppermute | solution.py:210
  51.2 101.5 %collective-permute-start.7 = (bf16[2048,256]{1,0:T(8,128)(2,1)}, bf16[2048,256]{1,0:T(8,128)(2,1)}, u32[]{:S(2)}, u32[]{:S(2)}) collective-permute-start(bf16[2048,256]{1,0:T(8,128)(2,1)} %get-tuple-element.106), channel_id=1, source_target_pairs={{16,0},{24,8},{0,16},{8,24},{17,1},{25,9},{1,17},{9,25},{18,2},{26... | collective-permute-start | bytes 3145736 | tf_op jit(solution)/shard_map/ppermute | solution.py:210
  76.5 76.2 %collective-permute-start.8 = (bf16[2048,256]{1,0:T(8,128)(2,1)}, bf16[2048,256]{1,0:T(8,128)(2,1)}, u32[]{:S(2)}, u32[]{:S(2)}) collective-permute-start(bf16[2048,256]{1,0:T(8,128)(2,1)} %get-tuple-element.107), channel_id=1, source_target_pairs={{16,0},{24,8},{0,16},{8,24},{17,1},{25,9},{1,17},{9,25},{18,2},{26... | collective-permute-start | bytes 3145736 | tf_op jit(solution)/shard_map/ppermute | solution.py:210
  102.0 41.1 %collective-permute-start.3 = (bf16[16,4096]{1,0:T(8,128)(2,1)S(1)}, bf16[16,4096]{1,0:T(8,128)(2,1)S(1)}, u32[]{:S(2)}, u32[]{:S(2)}) collective-permute-start(bf16[16,4096]{1,0:T(8,128)(2,1)S(1)} %pad_maximum_fusion.2), channel_id=1, source_target_pairs={{16,0},{24,8},{0,16},{8,24},{17,1},{25,9},{1,17},{9,25},{18,2},{26... | collective-permute-start | bytes 393224 | tf_op jit(solution)/shard_map/ppermute | solution.py:210
  143.2 62.9 %collective-permute-start.12 = (bf16[2048,256]{1,0:T(8,128)(2,1)}, bf16[2048,256]{1,0:T(8,128)(2,1)}, u32[]{:S(2)}, u32[]{:S(2)}) collective-permute-start(bf16[2048,256]{1,0:T(8,128)(2,1)} %get-tuple-element.102), channel_id=1, source_target_pairs={{8,0},{0,8},{24,16},{16,24},{9,1},{1,9},{25,17},{17,25},{10,2},{2,... | collective-permute-start | bytes 3145736 | tf_op jit(solution)/shard_map/ppermute | solution.py:206
  160.6 21.3 %collective-permute-start.9 = (bf16[528,768]{1,0:T(8,128)(2,1)}, bf16[528,768]{1,0:T(8,128)(2,1)}, u32[]{:S(2)}, u32[]{:S(2)}) collective-permute-start(bf16[528,768]{1,0:T(8,128)(2,1)} %get-tuple-element.114), channel_id=1, source_target_pairs={{16,0},{24,8},{0,16},{8,24},{17,1},{25,9},{1,17},{9,25},{18,2},{26... | collective-permute-start | bytes 2433032 | tf_op jit(solution)/shard_map/ppermute | solution.py:210
  168.2 26.6 %collective-permute-start.10 = (bf16[512,768]{1,0:T(8,128)(2,1)}, bf16[512,768]{1,0:T(8,128)(2,1)}, u32[]{:S(2)}, u32[]{:S(2)}) collective-permute-start(bf16[512,768]{1,0:T(8,128)(2,1)} %get-tuple-element.117), channel_id=1, source_target_pairs={{16,0},{24,8},{0,16},{8,24},{17,1},{25,9},{1,17},{9,25},{18,2},{26... | collective-permute-start | bytes 2359304 | tf_op jit(solution)/shard_map/ppermute | solution.py:210
  208.7 145.5 %all-gather.14.cloned.1.call-start = ((), (), s32[]{:S(2)}) async-start(), calls=%async_computation.3 | async-start | bytes 4718592 | tf_op jit(solution)/shard_map/all_gather | solution.py:288
  208.9 68.3 %collective-permute-start.15 = (bf16[3,2048,256]{2,1,0:T(8,128)(2,1)}, bf16[3,2048,256]{2,1,0:T(8,128)(2,1)S(1)}, u32[]{:S(2)}, u32[]{:S(2)}) collective-permute-start(bf16[3,2048,256]{2,1,0:T(8,128)(2,1)} %get-tuple-element.137.refs_2_.refs_1_), channel_id=1, source_target_pairs={{8,0},{0,8},{24,16},{16,24},{9,1},{1,9},{25,17},{17,25},{10,2},{2,... | collective-permute-start | bytes 9437192 | tf_op jit(solution)/shard_map/ppermute | solution.py:206
  210.7 63.7 %collective-permute-start.16 = (bf16[2048,256]{1,0:T(8,128)(2,1)}, bf16[2048,256]{1,0:T(8,128)(2,1)S(1)}, u32[]{:S(2)}, u32[]{:S(2)}) collective-permute-start(bf16[2048,256]{1,0:T(8,128)(2,1)} %collective-permute-done.2), channel_id=1, source_target_pairs={{16,0},{24,8},{0,16},{8,24},{17,1},{25,9},{1,17},{9,25},{18,2},{26... | collective-permute-start | bytes 3145736 | tf_op jit(solution)/shard_map/ppermute | solution.py:210
  218.3 36.1 %collective-permute-start.13 = (bf16[528,768]{1,0:T(8,128)(2,1)S(1)}, bf16[528,768]{1,0:T(8,128)(2,1)S(1)}, u32[]{:S(2)}, u32[]{:S(2)}) collective-permute-start(bf16[528,768]{1,0:T(8,128)(2,1)S(1)} %get-tuple-element.125), channel_id=1, source_target_pairs={{16,0},{24,8},{0,16},{8,24},{17,1},{25,9},{1,17},{9,25},{18,2},{26... | collective-permute-start | bytes 2433032 | tf_op jit(solution)/shard_map/ppermute | solution.py:210
  226.6 41.1 %collective-permute-start.14 = (bf16[512,768]{1,0:T(8,128)(2,1)S(1)}, bf16[512,768]{1,0:T(8,128)(2,1)S(1)}, u32[]{:S(2)}, u32[]{:S(2)}) collective-permute-start(bf16[512,768]{1,0:T(8,128)(2,1)S(1)} %get-tuple-element.128), channel_id=1, source_target_pairs={{16,0},{24,8},{0,16},{8,24},{17,1},{25,9},{1,17},{9,25},{18,2},{26... | collective-permute-start | bytes 2359304 | tf_op jit(solution)/shard_map/ppermute | solution.py:210
  281.6 123.8 %all-gather.16.cloned.1.call-start = ((), (), s32[]{:S(2)}) async-start(), calls=%async_computation.4 | async-start | bytes 4718592 | tf_op jit(solution)/shard_map/all_gather | solution.py:288
  281.8 67.2 %collective-permute-start.19 = (bf16[3,2048,256]{2,1,0:T(8,128)(2,1)S(1)}, bf16[3,2048,256]{2,1,0:T(8,128)(2,1)S(1)}, u32[]{:S(2)}, u32[]{:S(2)}) collective-permute-start(bf16[3,2048,256]{2,1,0:T(8,128)(2,1)S(1)} %copy-done), channel_id=1, source_target_pairs={{8,0},{0,8},{24,16},{16,24},{9,1},{1,9},{25,17},{17,25},{10,2},{2,... | collective-permute-start | bytes 9437192 | tf_op jit(solution)/shard_map/ppermute | solution.py:206
  283.4 67.3 %collective-permute-start.20 = (bf16[2048,256]{1,0:T(8,128)(2,1)}, bf16[2048,256]{1,0:T(8,128)(2,1)S(1)}, u32[]{:S(2)}, u32[]{:S(2)}) collective-permute-start(bf16[2048,256]{1,0:T(8,128)(2,1)} %collective-permute-done.12), channel_id=1, source_target_pairs={{16,0},{24,8},{0,16},{8,24},{17,1},{25,9},{1,17},{9,25},{18,2},{26... | collective-permute-start | bytes 3145736 | tf_op jit(solution)/shard_map/ppermute | solution.py:210
  292.9 34.1 %collective-permute-start.17 = (bf16[528,768]{1,0:T(8,128)(2,1)S(1)}, bf16[528,768]{1,0:T(8,128)(2,1)S(1)}, u32[]{:S(2)}, u32[]{:S(2)}) collective-permute-start(bf16[528,768]{1,0:T(8,128)(2,1)S(1)} %get-tuple-element.140), channel_id=1, source_target_pairs={{16,0},{24,8},{0,16},{8,24},{17,1},{25,9},{1,17},{9,25},{18,2},{26... | collective-permute-start | bytes 2433032 | tf_op jit(solution)/shard_map/ppermute | solution.py:210
  301.1 38.3 %collective-permute-start.18 = (bf16[512,768]{1,0:T(8,128)(2,1)S(1)}, bf16[512,768]{1,0:T(8,128)(2,1)S(1)}, u32[]{:S(2)}, u32[]{:S(2)}) collective-permute-start(bf16[512,768]{1,0:T(8,128)(2,1)S(1)} %get-tuple-element.143), channel_id=1, source_target_pairs={{16,0},{24,8},{0,16},{8,24},{17,1},{25,9},{1,17},{9,25},{18,2},{26... | collective-permute-start | bytes 2359304 | tf_op jit(solution)/shard_map/ppermute | solution.py:210
  354.3 108.3 %all-gather.18.cloned.1.call-start = ((), (), s32[]{:S(2)}) async-start(), calls=%async_computation.5 | async-start | bytes 4718592 | tf_op jit(solution)/shard_map/all_gather | solution.py:288
  354.6 48.4 %collective-permute-start.23 = (bf16[2048,256]{1,0:T(8,128)(2,1)}, bf16[2048,256]{1,0:T(8,128)(2,1)}, u32[]{:S(2)}, u32[]{:S(2)}) collective-permute-start(bf16[2048,256]{1,0:T(8,128)(2,1)} %get-tuple-element.106), channel_id=1, source_target_pairs={{8,0},{0,8},{24,16},{16,24},{9,1},{1,9},{25,17},{17,25},{10,2},{2,... | collective-permute-start | bytes 3145736 | tf_op jit(solution)/shard_map/ppermute | solution.py:206
  355.8 47.1 %collective-permute-start.24 = (bf16[2048,256]{1,0:T(8,128)(2,1)}, bf16[2048,256]{1,0:T(8,128)(2,1)}, u32[]{:S(2)}, u32[]{:S(2)}) collective-permute-start(bf16[2048,256]{1,0:T(8,128)(2,1)} %get-tuple-element.107), channel_id=1, source_target_pairs={{8,0},{0,8},{24,16},{16,24},{9,1},{1,9},{25,17},{17,25},{10,2},{2,... | collective-permute-start | bytes 3145736 | tf_op jit(solution)/shard_map/ppermute | solution.py:206
  364.6 21.1 %collective-permute-start.21 = (bf16[528,768]{1,0:T(8,128)(2,1)S(1)}, bf16[528,768]{1,0:T(8,128)(2,1)S(1)}, u32[]{:S(2)}, u32[]{:S(2)}) collective-permute-start(bf16[528,768]{1,0:T(8,128)(2,1)S(1)} %get-tuple-element.155), channel_id=1, source_target_pairs={{16,0},{24,8},{0,16},{8,24},{17,1},{25,9},{1,17},{9,25},{18,2},{26... | collective-permute-start | bytes 2433032 | tf_op jit(solution)/shard_map/ppermute | solution.py:210
  372.2 25.0 %collective-permute-start.22 = (bf16[512,768]{1,0:T(8,128)(2,1)S(1)}, bf16[512,768]{1,0:T(8,128)(2,1)S(1)}, u32[]{:S(2)}, u32[]{:S(2)}) collective-permute-start(bf16[512,768]{1,0:T(8,128)(2,1)S(1)} %get-tuple-element.158), channel_id=1, source_target_pairs={{16,0},{24,8},{0,16},{8,24},{17,1},{25,9},{1,17},{9,25},{18,2},{26... | collective-permute-start | bytes 2359304 | tf_op jit(solution)/shard_map/ppermute | solution.py:210
  405.4 26.5 %collective-permute-start.25 = (bf16[2048,256]{1,0:T(8,128)(2,1)}, bf16[2048,256]{1,0:T(8,128)(2,1)}, u32[]{:S(2)}, u32[]{:S(2)}) collective-permute-start(bf16[2048,256]{1,0:T(8,128)(2,1)} %collective-permute-done.23), channel_id=1, source_target_pairs={{16,0},{24,8},{0,16},{8,24},{17,1},{25,9},{1,17},{9,25},{18,2},{26... | collective-permute-start | bytes 3145736 | tf_op jit(solution)/shard_map/ppermute | solution.py:210
  407.1 42.9 %collective-permute-start.26 = (bf16[2048,256]{1,0:T(8,128)(2,1)}, bf16[2048,256]{1,0:T(8,128)(2,1)}, u32[]{:S(2)}, u32[]{:S(2)}) collective-permute-start(bf16[2048,256]{1,0:T(8,128)(2,1)} %collective-permute-done.24), channel_id=1, source_target_pairs={{16,0},{24,8},{0,16},{8,24},{17,1},{25,9},{1,17},{9,25},{18,2},{26... | collective-permute-start | bytes 3145736 | tf_op jit(solution)/shard_map/ppermute | solution.py:210
  (29 other events, 187.3 us)
Sparse Core Ops, SparseCore 0:
  46.1 83.3 all-gather.9
  208.8 47.6 all-gather.11
  281.7 47.3 all-gather.13
  354.4 47.3 all-gather.15
  405.5 46.8 all-gather.17

commit v6 on v5

--- a/solution.py
+++ b/solution.py
@@ -138,8 +138,11 @@
     per_block, _, wide = weights[0].shape
     for m in range(columns):
         if held:
-            each = columns // len(held)
-            total = held[m // each][:, m % each * wide : (m % each + 1) * wide]
+            place, at = 0, m * wide
+            while at >= held[place].shape[1]:
+                at -= held[place].shape[1]
+                place += 1
+            total = held[place][:, at : at + wide]
         else:
             total = jnp.zeros((out_ref.shape[0], wide), jnp.float32)
         for b in range(blocks):
@@ -246,17 +249,20 @@
     before = normalised(before, norm_gain)
     theirs_before = [from_far(columns_of(before, (e - k) % far), k) for k in range(1, far)]
     taps = jnp.concatenate([feat_filter.reshape(feat * 3, chans_here), inner_filter], axis=0)
+    rows[1:], theirs_before = together((rows[1:], theirs_before))
     across = [[from_far(block, a) for a in range(1, far)] for block in rows]
-    x_rows, across[0] = together((x_rows, across[0]))
-    normed, across[1] = together((normalised(x_rows, norm_gain), across[1]))
-    mine = columns_of(normed, e)
+    normed, across[0] = together((normalised(x_rows, norm_gain), across[0]))
+    mine, across[1] = together((columns_of(normed, e), across[1]))
     mine_before = columns_of(before, e)
-    theirs, theirs_before, weights[0], mine, mine_before, across = together(
-        (theirs, theirs_before, weights[0], mine, mine_before, across)
+    theirs, theirs_before, weights[0], mine, mine_before, across[:3] = together(
+        (theirs, theirs_before, weights[0], mine, mine_before, across[:3])
     )
 
     def beyond(m):
         return [[from_far(block, a) for block in near_rows[m]] for a in range(1, far)]
+
+    def sideways(m):
+        return [[from_near(block, k) for k in range(1, near)] for block in across[m]]
 
     gated, done, diagonal = [], [], []
     for j in range(CHUNKS):
@@ -272,15 +278,18 @@
         second, _ = project(mine, 1, [], weights[j], sums[1], after=[mark])
         projected = [first, second]
         if j == 0:
-            projected, weights[1], near_rows[1] = together((projected, weights[1], near_rows[1]))
-        elif j < CHUNKS - 1:
-            diagonal.append(beyond(j - 1))
-            projected, weights[j + 1], diagonal[-1] = together(
-                (projected, weights[j + 1], diagonal[-1])
+            projected, weights[1], near_rows[1], across[3] = together(
+                (projected, weights[1], near_rows[1], across[3])
             )
+        elif j == 1:
+            diagonal.append(beyond(0))
+            projected, weights[2], diagonal[0] = together((projected, weights[2], diagonal[0]))
+        elif j == 2:
+            diagonal.append(beyond(1))
+            projected, weights[3], diagonal[1] = together((projected, weights[3], diagonal[1]))
         else:
             projected, near_rows[2:] = together((projected, near_rows[2:]))
-            diagonal += [beyond(2), beyond(3)]
+            diagonal += [beyond(2), sideways(3)]
         mixed, mark = short_mix(projected, taps[:, cuts[j]], feat, filt)
         done = [mark]
         if j > 0:
@@ -296,12 +305,13 @@
         for a in range(1, far):
             found += [across[m][a - 1]] + diagonal[m][a - 1]
         blocks.append([block.reshape(-1, chans_here, block.shape[1]) for block in found])
-    half = OUT_CHUNKS // 2
-    first = out_project(order, gated[:-1], 0, blocks[:half], jnp.float32)
-    first, blocks[half:] = together((first, blocks[half:]))
-    second = out_project(order, gated[:-1], 0, blocks[half:], jnp.float32)
-    first, second, last = together((first, second, gated[-1]))
-    out = out_project(order, [last], edges[CHUNKS - 1], blocks, jnp.bfloat16, [first, second])
+    groups, partial = (blocks[:2], blocks[2:]), []
+    for found in groups:
+        if partial:
+            partial[-1], found = together((partial[-1], found))
+        partial.append(out_project(order, gated[:-1], 0, found, jnp.float32))
+    partial, last = together((partial, gated[-1]))
+    out = out_project(order, [last], edges[CHUNKS - 1], blocks, jnp.bfloat16, partial)
     got = lax.all_to_all(
         out.reshape(chans, share, -1), "chan", split_axis=0, concat_axis=0, tiled=True
     )

time: 540 us -> 531 us (0.983)
  waiting for transfers between devices: 210 us -> 204 us
    ppermute x18 -> x17, waiting for transfers between devices: 181 us -> 151 us  [from_far(): return lax.ppermute(block, 'seq', pairs)]
    all_gather x4, waiting for transfers between devices: 0.01 us -> 12.7 us  [per_device(): gated.append(lax.all_gather(mixed, 'chan', axis=0))]
    ppermute x8 -> x9, waiting for transfers between devices: 9.14 us -> 21.1 us  [from_near(): return lax.ppermute(block, 'seq', pairs)]
    ppermute x18 -> x17, starting transfers between devices: 20.5 us -> 15.4 us  [from_far(): return lax.ppermute(block, 'seq', pairs)]
    unnamed x58 -> x62, local copies, waits for them, and re-layouts: 23.5 us -> 21.9 us
    ppermute x8 -> x9, starting transfers between devices: 11.3 us -> 12.6 us  [from_near(): return lax.ppermute(block, 'seq', pairs)]
  transfers between devices with their start and end apart: 32 -> 32, of which waited for: 16 -> 19; matrix products, arithmetic and copies ran while one was open for 9% -> 9% of each run, Pallas kernels for 25% -> 26%
where the time goes in v6:
time: 531 us; the launch traced here: 527 us
  waiting for transfers between devices  204 us (38%)
  Pallas kernels  147 us (28%)
  blocking collectives  52.6 us (10%)
  local copies, waits for them, and re-layouts  40.2 us (8%)
  other arithmetic  36.4 us (7%)
  starting transfers between devices  32.2 us (6%)
  between operations  13.8 us (3%)
    ppermute x17, waiting for transfers between devices, from_far(): return lax.ppermute(block, 'seq', pairs)  151 us
    pallas_call x16, Pallas kernels, project(): pl.pallas_call(functools.partial(project_kernel, len(weights), len(receiv...  108 us
    all_to_all x1, blocking collectives, per_device(): lax.all_to_all(out.reshape(chans, share, -1), 'chan', split_axis=0, conca...  52.6 us
    pallas_call x3, Pallas kernels, out_project(): pl.pallas_call(functools.partial(out_kernel, blocks, columns, len(gated))...  31.8 us
    unnamed x62, local copies, waits for them, and re-layouts  21.9 us
    ppermute x9, waiting for transfers between devices, from_near(): return lax.ppermute(block, 'seq', pairs)  21.1 us
    ppermute x1, waiting for transfers between devices, per_device(): lax.ppermute(x_rows[tokens - HALO:], 'seq', [(a, a + 1) for a in range(se...  19.4 us
    convert_element_type x3, other arithmetic, normalised(): return (values * lax.rsqrt(squares + 1e-06) * gain).astype(jnp.bfloat16)  17.8 us
  transfers between devices with their start and end apart: 32, of which 19 were waited for; matrix products, arithmetic and copies ran while one was open for 9% of the time, Pallas kernels for 26%

profile of v6, /device:TPU:0, one launch (start us, length us, event | category | flops | bytes accessed | tf_op | source)
XLA Modules:
  0.0 526.9 jit_solution(18151326332086001806)
XLA Ops:
  26.6 19.4 %collective-permute-done.1 = bf16[16,8192]{1,0:T(8,128)(2,1)S(1)} collective-permute-done((bf16[16,8192]{1,0:T(8,128)(2,1)S(1)}, bf16[16,8192]{1,0:T(8,128)(2,1)S(1)}, u32[]{:S(2)}, u32[]{:S(2)}) %collective-permute-start.1) | collective-permute-done | bytes 262176 | tf_op jit(solution)/shard_map/ppermute | solution.py:238
  51.2 8.2 %fusion = f32[1024]{0:T(1024)S(1)} fusion(bf16[1024,8192]{1,0:T(8,128)(2,1)} %param.6), kind=kLoop, calls=%fused_computation.2 | loop fusion | flops 25164800 | bytes 16781312 | tf_op jit(solution)/shard_map/reduce_sum | solution.py:193
  66.3 15.3 %fusion.2 = bf16[1024,8192]{1,0:T(8,128)(2,1)} fusion(bf16[1024,8192]{1,0:T(8,128)(2,1)} %param.6, f32[8192]{0:T(1024)S(1)} %copy-done.28, f32[1024]{0:T(1024)S(1)} %add_rsqrt_fusion), kind=kLoop, calls=%fused_computation.4 | loop fusion | flops 33554432 | bytes 33591296 | tf_op jit(solution)/shard_map/convert_element_type | solution.py:194
  81.7 7.1 %collective-permute-done.5 = bf16[2048,256]{1,0:T(8,128)(2,1)S(1)} collective-permute-done((bf16[2048,256]{1,0:T(8,128)(2,1)}, bf16[2048,256]{1,0:T(8,128)(2,1)S(1)}, u32[]{:S(2)}, u32[]{:S(2)}) %collective-permute-start.5) | collective-permute-done | bytes 1048608 | tf_op jit(solution)/shard_map/ppermute | solution.py:213
  88.8 8.9 %constant_dynamic-slice_fusion.3 = (bf16[1024,2048]{1,0:T(8,128)(2,1)}, bf16[1024,2048]{1,0:T(8,128)(2,1)}) fusion(bf16[1024,8192]{1,0:T(8,128)(2,1)} %fusion.2, s32[]{:T(128)S(6)} %select_n.86, s32[]{:T(128)S(6)} %select_n.87), kind=kLoop, calls=%fused_computation.37 | loop fusion | bytes 16777224 | tf_op jit(solution)/shard_map/dynamic_slice | solution.py:218
  97.7 13.5 %collective-permute-done.6 = bf16[2048,256]{1,0:T(8,128)(2,1)S(1)} collective-permute-done((bf16[2048,256]{1,0:T(8,128)(2,1)S(1)}, bf16[2048,256]{1,0:T(8,128)(2,1)S(1)}, u32[]{:S(2)}, u32[]{:S(2)}) %collective-permute-start.6) | collective-permute-done | bytes 1048608 | tf_op jit(solution)/shard_map/ppermute | solution.py:213
  112.2 8.0 %pad_maximum_fusion.refs_0_ = bf16[1024,4096]{1,0:T(8,128)(2,1)} fusion(bf16[1024,2048]{1,0:T(8,128)(2,1)} %get-tuple-element.196, bf16[1024,2048]{1,0:T(8,128)(2,1)} %get-tuple-element.195), kind=kLoop, calls=%fused_computation.5 | loop fusion | flops 16777216 | bytes 16777216 | tf_op jit(solution)/shard_map/concatenate | solution.py:216
  120.2 13.6 %collective-permute-done.7 = bf16[2048,256]{1,0:T(8,128)(2,1)} collective-permute-done((bf16[2048,256]{1,0:T(8,128)(2,1)}, bf16[2048,256]{1,0:T(8,128)(2,1)}, u32[]{:S(2)}, u32[]{:S(2)}) %collective-permute-start.7) | collective-permute-done | bytes 1048608 | tf_op jit(solution)/shard_map/ppermute | solution.py:213
  133.8 7.9 %project.16 = (bf16[528,768]{1,0:T(8,128)(2,1)}, f32[8,128]{1,0:T(8,128)S(1)}) custom-call(bf16[1024,4096]{1,0:T(8,128)(2,1)} %all-gather.10.cloned.1.call-done.refs_0_, bf16[16,4096]{1,0:T(8,128)(2,1)S(1)} %collective-permute-done.3.refs_1_, bf16[3,2048,256]{2,1,0:T(8,128)(2,1)S(1)} %slice_bitcast_fusion.3.refs_2_.refs_1_, ...), custom_call_target="tpu_custom_call" | custom-call | flops 1024 | bytes 1024 | tf_op jit(solution)/shard_map/project/pallas_call | solution.py:64
  141.7 7.0 %project.18 = (bf16[512,768]{1,0:T(8,128)(2,1)}, f32[8,128]{1,0:T(8,128)}) custom-call(bf16[1024,4096]{1,0:T(8,128)(2,1)} %all-gather.10.cloned.1.call-done.refs_0_, bf16[3,2048,256]{2,1,0:T(8,128)(2,1)S(1)} %slice_bitcast_fusion.3.refs_2_.refs_1_, bf16[3,2048,256]{2,1,0:T(8,128)(2,1)} %collective-permute-done.4.refs_3_.refs_2_, ...), custom_call_target="tpu_custom_call" | custom-call | flops 1024 | bytes 1024 | tf_op jit(solution)/shard_map/project/pallas_call | solution.py:64
  150.8 22.8 %collective-permute-done.8.refs_4_.refs_5_ = bf16[528,768]{1,0:T(8,128)(2,1)} collective-permute-done((bf16[528,768]{1,0:T(8,128)(2,1)}, bf16[528,768]{1,0:T(8,128)(2,1)}, u32[]{:S(2)}, u32[]{:S(2)}) %collective-permute-start.8) | collective-permute-done | bytes 811040 | tf_op jit(solution)/shard_map/ppermute | solution.py:213
  173.6 7.2 %project.17 = (bf16[528,768]{1,0:T(8,128)(2,1)S(1)}, f32[8,128]{1,0:T(8,128)S(1)}) custom-call(bf16[1024,4096]{1,0:T(8,128)(2,1)} %pad_maximum_fusion.refs_0_, bf16[16,4096]{1,0:T(8,128)(2,1)S(1)} %pad_maximum_fusion.3.refs_1_, bf16[3,2048,256]{2,1,0:T(8,128)(2,1)S(1)} %slice_bitcast_fusion.3.refs_2_.refs_1_, ...), custom_call_target="tpu_custom_call" | custom-call | flops 1024 | bytes 1024 | tf_op jit(solution)/shard_map/project/pallas_call | solution.py:64
  186.7 6.8 %project.19 = (bf16[512,768]{1,0:T(8,128)(2,1)S(1)}, f32[8,128]{1,0:T(8,128)}) custom-call(bf16[1024,4096]{1,0:T(8,128)(2,1)} %pad_maximum_fusion.refs_0_, bf16[3,2048,256]{2,1,0:T(8,128)(2,1)S(1)} %slice_bitcast_fusion.3.refs_2_.refs_1_, bf16[3,2048,256]{2,1,0:T(8,128)(2,1)} %collective-permute-done.4.refs_3_.refs_2_, ...), custom_call_target="tpu_custom_call" | custom-call | flops 1024 | bytes 1024 | tf_op jit(solution)/shard_map/project/pallas_call | solution.py:64
  193.5 12.5 %collective-permute-done.11 = bf16[2048,256]{1,0:T(8,128)(2,1)} collective-permute-done((bf16[2048,256]{1,0:T(8,128)(2,1)}, bf16[2048,256]{1,0:T(8,128)(2,1)}, u32[]{:S(2)}, u32[]{:S(2)}) %collective-permute-start.11) | collective-permute-done | bytes 1048608 | tf_op jit(solution)/shard_map/ppermute | solution.py:209
  211.2 7.0 %project.20 = (bf16[528,768]{1,0:T(8,128)(2,1)S(1)}, f32[8,128]{1,0:T(8,128)S(1)}) custom-call(bf16[1024,4096]{1,0:T(8,128)(2,1)} %all-gather.10.cloned.1.call-done.refs_0_, bf16[16,4096]{1,0:T(8,128)(2,1)S(1)} %collective-permute-done.3.refs_1_, bf16[3,2048,256]{2,1,0:T(8,128)(2,1)S(1)} %copy-done.1, ...), custom_call_target="tpu_custom_call" | custom-call | flops 1024 | bytes 1024 | tf_op jit(solution)/shard_map/project/pallas_call | solution.py:64
  219.9 6.7 %project.22 = (bf16[512,768]{1,0:T(8,128)(2,1)S(1)}, f32[8,128]{1,0:T(8,128)}) custom-call(bf16[1024,4096]{1,0:T(8,128)(2,1)} %all-gather.10.cloned.1.call-done.refs_0_, bf16[3,2048,256]{2,1,0:T(8,128)(2,1)S(1)} %copy-done.1, bf16[3,2048,256]{2,1,0:T(8,128)(2,1)} %collective-permute-done.10.refs_3_.refs_2_, f32[8,128]{1,0:T(8,128)S(1)} %get-tuple-element.135.refs_3_), custom_call_target="tpu_custom_call" | custom-call | flops 1024 | bytes 1024 | tf_op jit(solution)/shard_map/project/pallas_call | solution.py:64
  227.1 27.4 %collective-permute-done.13.refs_4_.refs_5_ = bf16[528,768]{1,0:T(8,128)(2,1)S(1)} collective-permute-done((bf16[528,768]{1,0:T(8,128)(2,1)S(1)}, bf16[528,768]{1,0:T(8,128)(2,1)S(1)}, u32[]{:S(2)}, u32[]{:S(2)}) %collective-permute-start.13) | collective-permute-done | bytes 811040 | tf_op jit(solution)/shard_map/ppermute | solution.py:213
  254.4 7.1 %project.21 = (bf16[528,768]{1,0:T(8,128)(2,1)S(1)}, f32[8,128]{1,0:T(8,128)S(1)}) custom-call(bf16[1024,4096]{1,0:T(8,128)(2,1)} %pad_maximum_fusion.refs_0_, bf16[16,4096]{1,0:T(8,128)(2,1)S(1)} %pad_maximum_fusion.3.refs_1_, bf16[3,2048,256]{2,1,0:T(8,128)(2,1)S(1)} %copy-done.1, bf16[3,2048,256]{2,1,0:T(8,128)(2,1)} %collective-permute-done.10.refs_3_.refs_2_, ...), custom_call_target="tpu_custom_call" | custom-call | flops 1024 | bytes 1024 | tf_op jit(solution)/shard_map/project/pallas_call | solution.py:64
  261.5 6.2 %collective-permute-done.14.refs_3_ = bf16[512,768]{1,0:T(8,128)(2,1)S(1)} collective-permute-done((bf16[512,768]{1,0:T(8,128)(2,1)S(1)}, bf16[512,768]{1,0:T(8,128)(2,1)S(1)}, u32[]{:S(2)}, u32[]{:S(2)}) %collective-permute-start.14) | collective-permute-done | bytes 786464 | tf_op jit(solution)/shard_map/ppermute | solution.py:213
  267.7 6.7 %project.23 = (bf16[512,768]{1,0:T(8,128)(2,1)S(1)}, f32[8,128]{1,0:T(8,128)}) custom-call(bf16[1024,4096]{1,0:T(8,128)(2,1)} %pad_maximum_fusion.refs_0_, bf16[3,2048,256]{2,1,0:T(8,128)(2,1)S(1)} %copy-done.1, bf16[3,2048,256]{2,1,0:T(8,128)(2,1)} %collective-permute-done.10.refs_3_.refs_2_, bf16[512,768]{1,0:T(8,128)(2,1)S(1)} %collective-permute-done.14.refs_3_, ...), custom_call_target="tpu_custom_call" | custom-call | flops 1024 | bytes 1024 | tf_op jit(solution)/shard_map/project/pallas_call | solution.py:64
  285.8 7.0 %project.24 = (bf16[528,768]{1,0:T(8,128)(2,1)S(1)}, f32[8,128]{1,0:T(8,128)S(1)}) custom-call(bf16[1024,4096]{1,0:T(8,128)(2,1)} %all-gather.10.cloned.1.call-done.refs_0_, bf16[16,4096]{1,0:T(8,128)(2,1)S(1)} %collective-permute-done.3.refs_1_, bf16[3,2048,256]{2,1,0:T(8,128)(2,1)} %get-tuple-element.145.refs_2_.refs_1_, ...), custom_call_target="tpu_custom_call" | custom-call | flops 1024 | bytes 1024 | tf_op jit(solution)/shard_map/project/pallas_call | solution.py:64
  294.4 6.8 %project.26 = (bf16[512,768]{1,0:T(8,128)(2,1)S(1)}, f32[8,128]{1,0:T(8,128)}) custom-call(bf16[1024,4096]{1,0:T(8,128)(2,1)} %all-gather.10.cloned.1.call-done.refs_0_, bf16[3,2048,256]{2,1,0:T(8,128)(2,1)} %get-tuple-element.145.refs_2_.refs_1_, bf16[3,2048,256]{2,1,0:T(8,128)(2,1)S(1)} %copy-done.5, f32[8,128]{1,0:T(8,128)S(1)} %get-tuple-element.150.refs_3_), custom_call_target="tpu_custom_call" | custom-call | flops 1024 | bytes 1024 | tf_op jit(solution)/shard_map/project/pallas_call | solution.py:64
  301.6 25.5 %collective-permute-done.17.refs_4_.refs_5_ = bf16[528,768]{1,0:T(8,128)(2,1)S(1)} collective-permute-done((bf16[528,768]{1,0:T(8,128)(2,1)S(1)}, bf16[528,768]{1,0:T(8,128)(2,1)S(1)}, u32[]{:S(2)}, u32[]{:S(2)}) %collective-permute-start.17) | collective-permute-done | bytes 811040 | tf_op jit(solution)/shard_map/ppermute | solution.py:213
  327.1 7.1 %project.25 = (bf16[528,768]{1,0:T(8,128)(2,1)S(1)}, f32[8,128]{1,0:T(8,128)S(1)}) custom-call(bf16[1024,4096]{1,0:T(8,128)(2,1)} %pad_maximum_fusion.refs_0_, bf16[16,4096]{1,0:T(8,128)(2,1)S(1)} %pad_maximum_fusion.3.refs_1_, bf16[3,2048,256]{2,1,0:T(8,128)(2,1)} %get-tuple-element.145.refs_2_.refs_1_, bf16[3,2048,256]{2,1,0:T(8,128)(2,1)S(1)} %copy-done.5, ...), custom_call_target="tpu_custom_call" | custom-call | flops 1024 | bytes 1024 | tf_op jit(solution)/shard_map/project/pallas_call | solution.py:64
  339.4 6.7 %project.27 = (bf16[512,768]{1,0:T(8,128)(2,1)S(1)}, f32[8,128]{1,0:T(8,128)}) custom-call(bf16[1024,4096]{1,0:T(8,128)(2,1)} %pad_maximum_fusion.refs_0_, bf16[3,2048,256]{2,1,0:T(8,128)(2,1)} %get-tuple-element.145.refs_2_.refs_1_, bf16[3,2048,256]{2,1,0:T(8,128)(2,1)S(1)} %copy-done.5, bf16[512,768]{1,0:T(8,128)(2,1)S(1)} %collective-permute-done.18.refs_3_, ...), custom_call_target="tpu_custom_call" | custom-call | flops 1024 | bytes 1024 | tf_op jit(solution)/shard_map/project/pallas_call | solution.py:64
  372.6 13.2 %collective-permute-done.21.refs_4_.refs_5_ = bf16[528,768]{1,0:T(8,128)(2,1)S(1)} collective-permute-done((bf16[528,768]{1,0:T(8,128)(2,1)S(1)}, bf16[528,768]{1,0:T(8,128)(2,1)S(1)}, u32[]{:S(2)}, u32[]{:S(2)}) %collective-permute-start.21) | collective-permute-done | bytes 811040 | tf_op jit(solution)/shard_map/ppermute | solution.py:213
  385.8 6.1 %project.29 = (bf16[528,768]{1,0:T(8,128)(2,1)S(1)}, f32[8,128]{1,0:T(8,128)S(1)}) custom-call(bf16[1024,4096]{1,0:T(8,128)(2,1)} %pad_maximum_fusion.refs_0_, bf16[16,4096]{1,0:T(8,128)(2,1)S(1)} %pad_maximum_fusion.3.refs_1_, bf16[3,2048,256]{2,1,0:T(8,128)(2,1)S(1)} %copy-done, bf16[3,2048,256]{2,1,0:T(8,128)(2,1)S(1)} %copy-done.3, ...), custom_call_target="tpu_custom_call" | custom-call | flops 1024 | bytes 1024 | tf_op jit(solution)/shard_map/project/pallas_call | solution.py:64
  411.5 10.8 %out_project.3.refs_17_ = f32[1024,512]{1,0:T(8,128)S(1)} custom-call(s32[4]{0:T(128)S(1)} %pad_add_fusion.order, bf16[8,1024,256]{2,1,0:T(8,128)(2,1)} %bitcast.48, bf16[8,1024,256]{2,1,0:T(8,128)(2,1)} %bitcast.50, bf16[8,1024,256]{2,1,0:T(8,128)(2,1)} %bitcast.52, bf16[2,1024,256]{2,1,0:T(8,128)(2,1)} %bitcast.11.refs_3_.refs_1_, ...), custom_call_target="tpu_custom_call" | custom-call | flops 1024 | bytes 1024 | tf_op jit(solution)/shard_map/out_project/pallas_call | solution.py:181
  428.5 11.6 %out_project.4.refs_18_ = f32[1024,512]{1,0:T(8,128)S(1)} custom-call(s32[4]{0:T(128)S(1)} %pad_add_fusion.order, bf16[8,1024,256]{2,1,0:T(8,128)(2,1)} %bitcast.49, bf16[8,1024,256]{2,1,0:T(8,128)(2,1)} %bitcast.51, bf16[8,1024,256]{2,1,0:T(8,128)(2,1)} %bitcast.53, bf16[2,1024,256]{2,1,0:T(8,128)(2,1)} %bitcast.19.refs_3_.refs_9_, ...), custom_call_target="tpu_custom_call" | custom-call | flops 1024 | bytes 1024 | tf_op jit(solution)/shard_map/out_project/pallas_call | solution.py:181
  441.5 12.7 %all-gather.18.cloned.1.call-done = bf16[8192,256]{1,0:T(8,128)(2,1)} async-done(((bf16[1024,256]{1,0:T(8,128)(2,1)}), bf16[8192,256]{1,0:T(8,128)(2,1)}) %all-gather.18.cloned.1.call-update) | async-done | bytes 4194320 | tf_op jit(solution)/shard_map/all_gather | solution.py:297
  456.6 9.4 %out_project.5 = bf16[1024,1024]{1,0:T(8,128)(2,1)} custom-call(s32[4]{0:T(128)S(1)} %pad_add_fusion.order, bf16[8,1024,256]{2,1,0:T(8,128)(2,1)} %bitcast.56, bf16[2,1024,256]{2,1,0:T(8,128)(2,1)} %bitcast.11.refs_3_.refs_1_, bf16[2,1024,256]{2,1,0:T(8,128)(2,1)} %bitcast.12.refs_4_.refs_2_, bf16[2,1024,256]{2,1,0:T(8,128)(2,1)S(1)} %bitcast.39, ...), custom_call_target="tpu_custom_call" | custom-call | flops 1024 | bytes 1024 | tf_op jit(solution)/shard_map/out_project/pallas_call | solution.py:181
  466.1 52.6 %all_to_all.5 = bf16[8,128,1024]{2,1,0:T(8,128)(2,1)S(1)} all-to-all(bf16[8,128,1024]{2,1,0:T(8,128)(2,1)} %bitcast.54), channel_id=1, replica_groups=mesh['seq'=4,'chan'=8] {'chan'}, dimensions={0} | all-to-all | bytes 4194304 | tf_op jit(solution)/shard_map/all_to_all | solution.py:315
  (147 shorter events, 124.4 us)
Async XLA Ops:
  6.5 127.2 %all-gather.10.cloned.1.call-start = ((), (), s32[]{:S(2)}) async-start(), calls=%async_computation.1 | async-start | bytes 9437184 | tf_op jit(solution)/shard_map/all_gather | solution.py:248
  11.2 34.8 %collective-permute-start = (bf16[128,4096]{1,0:T(8,128)(2,1)S(1)}, bf16[128,4096]{1,0:T(8,128)(2,1)}, u32[]{:S(2)}, u32[]{:S(2)}) collective-permute-start(bf16[128,4096]{1,0:T(8,128)(2,1)S(1)} %pad_maximum_fusion.1), channel_id=1, source_target_pairs={{16,0},{24,8},{0,16},{8,24},{17,1},{25,9},{1,17},{9,25},{18,2},{26... | collective-permute-start | bytes 3145736 | tf_op jit(solution)/shard_map/ppermute | solution.py:213
  16.4 29.6 %collective-permute-start.2 = (bf16[2048,256]{1,0:T(8,128)(2,1)}, bf16[2048,256]{1,0:T(8,128)(2,1)}, u32[]{:S(2)}, u32[]{:S(2)}) collective-permute-start(bf16[2048,256]{1,0:T(8,128)(2,1)} %get-tuple-element.108), channel_id=1, source_target_pairs={{8,0},{0,8},{24,16},{16,24},{9,1},{1,9},{25,17},{17,25},{10,2},{2,... | collective-permute-start | bytes 3145736 | tf_op jit(solution)/shard_map/ppermute | solution.py:209
  19.0 27.0 %collective-permute-start.1 = (bf16[16,8192]{1,0:T(8,128)(2,1)S(1)}, bf16[16,8192]{1,0:T(8,128)(2,1)S(1)}, u32[]{:S(2)}, u32[]{:S(2)}) collective-permute-start(bf16[16,8192]{1,0:T(8,128)(2,1)S(1)} %slice.39), channel_id=1, source_target_pairs={{0,8},{8,16},{16,24},{1,9},{9,17},{17,25},{2,10},{10,18},{18,26},{... | collective-permute-start | bytes 786440 | tf_op jit(solution)/shard_map/ppermute | solution.py:238
  46.0 235.5 %all-gather.12.cloned.1.call-start = ((), (), s32[]{:S(2)}) async-start(), calls=%async_computation.2 | async-start | bytes 4718592 | tf_op jit(solution)/shard_map/all_gather | solution.py:297
  46.6 87.2 %collective-permute-start.4 = (bf16[3,2048,256]{2,1,0:T(8,128)(2,1)S(1)}, bf16[3,2048,256]{2,1,0:T(8,128)(2,1)}, u32[]{:S(2)}, u32[]{:S(2)}) collective-permute-start(bf16[3,2048,256]{2,1,0:T(8,128)(2,1)S(1)} %slice_bitcast_fusion.3.refs_2_.refs_1_), channel_id=1, source_target_pairs={{8,0},{0,8},{24,16},{16,24},{9,1},{1,9},{25,17},{17,25},{10,2},{2,... | collective-permute-start | bytes 9437192 | tf_op jit(solution)/shard_map/ppermute | solution.py:209
  49.1 156.9 %collective-permute-start.10 = (bf16[3,2048,256]{2,1,0:T(8,128)(2,1)}, bf16[3,2048,256]{2,1,0:T(8,128)(2,1)}, u32[]{:S(2)}, u32[]{:S(2)}) collective-permute-start(bf16[3,2048,256]{2,1,0:T(8,128)(2,1)} %get-tuple-element.128.refs_2_.refs_1_), channel_id=1, source_target_pairs={{8,0},{0,8},{24,16},{16,24},{9,1},{1,9},{25,17},{17,25},{10,2},{2,... | collective-permute-start | bytes 9437192 | tf_op jit(solution)/shard_map/ppermute | solution.py:209
  49.2 156.8 %collective-permute-start.11 = (bf16[2048,256]{1,0:T(8,128)(2,1)}, bf16[2048,256]{1,0:T(8,128)(2,1)}, u32[]{:S(2)}, u32[]{:S(2)}) collective-permute-start(bf16[2048,256]{1,0:T(8,128)(2,1)} %get-tuple-element.110), channel_id=1, source_target_pairs={{8,0},{0,8},{24,16},{16,24},{9,1},{1,9},{25,17},{17,25},{10,2},{2,... | collective-permute-start | bytes 3145736 | tf_op jit(solution)/shard_map/ppermute | solution.py:209
  59.8 6.5 %collective-permute-start.3 = (bf16[16,4096]{1,0:T(8,128)(2,1)S(1)}, bf16[16,4096]{1,0:T(8,128)(2,1)S(1)}, u32[]{:S(2)}, u32[]{:S(2)}) collective-permute-start(bf16[16,4096]{1,0:T(8,128)(2,1)S(1)} %pad_maximum_fusion.2), channel_id=1, source_target_pairs={{16,0},{24,8},{0,16},{8,24},{17,1},{25,9},{1,17},{9,25},{18,2},{26... | collective-permute-start | bytes 393224 | tf_op jit(solution)/shard_map/ppermute | solution.py:213
  59.9 28.9 %collective-permute-start.5 = (bf16[2048,256]{1,0:T(8,128)(2,1)}, bf16[2048,256]{1,0:T(8,128)(2,1)S(1)}, u32[]{:S(2)}, u32[]{:S(2)}) collective-permute-start(bf16[2048,256]{1,0:T(8,128)(2,1)} %get-tuple-element.108), channel_id=1, source_target_pairs={{16,0},{24,8},{0,16},{8,24},{17,1},{25,9},{1,17},{9,25},{18,2},{26... | collective-permute-start | bytes 3145736 | tf_op jit(solution)/shard_map/ppermute | solution.py:213
  66.3 44.9 %collective-permute-start.6 = (bf16[2048,256]{1,0:T(8,128)(2,1)S(1)}, bf16[2048,256]{1,0:T(8,128)(2,1)S(1)}, u32[]{:S(2)}, u32[]{:S(2)}) collective-permute-start(bf16[2048,256]{1,0:T(8,128)(2,1)S(1)} %copy-done.6), channel_id=1, source_target_pairs={{16,0},{24,8},{0,16},{8,24},{17,1},{25,9},{1,17},{9,25},{18,2},{26... | collective-permute-start | bytes 3145736 | tf_op jit(solution)/shard_map/ppermute | solution.py:213
  88.7 45.0 %collective-permute-start.7 = (bf16[2048,256]{1,0:T(8,128)(2,1)}, bf16[2048,256]{1,0:T(8,128)(2,1)}, u32[]{:S(2)}, u32[]{:S(2)}) collective-permute-start(bf16[2048,256]{1,0:T(8,128)(2,1)} %get-tuple-element.114), channel_id=1, source_target_pairs={{16,0},{24,8},{0,16},{8,24},{17,1},{25,9},{1,17},{9,25},{18,2},{26... | collective-permute-start | bytes 3145736 | tf_op jit(solution)/shard_map/ppermute | solution.py:213
  112.2 93.9 %collective-permute-start.12 = (bf16[2048,256]{1,0:T(8,128)(2,1)}, bf16[2048,256]{1,0:T(8,128)(2,1)}, u32[]{:S(2)}, u32[]{:S(2)}) collective-permute-start(bf16[2048,256]{1,0:T(8,128)(2,1)} %get-tuple-element.127), channel_id=1, source_target_pairs={{16,0},{24,8},{0,16},{8,24},{17,1},{25,9},{1,17},{9,25},{18,2},{26... | collective-permute-start | bytes 3145736 | tf_op jit(solution)/shard_map/ppermute | solution.py:213
  141.7 32.0 %collective-permute-start.8 = (bf16[528,768]{1,0:T(8,128)(2,1)}, bf16[528,768]{1,0:T(8,128)(2,1)}, u32[]{:S(2)}, u32[]{:S(2)}) collective-permute-start(bf16[528,768]{1,0:T(8,128)(2,1)} %get-tuple-element.121), channel_id=1, source_target_pairs={{16,0},{24,8},{0,16},{8,24},{17,1},{25,9},{1,17},{9,25},{18,2},{26... | collective-permute-start | bytes 2433032 | tf_op jit(solution)/shard_map/ppermute | solution.py:213
  148.8 37.9 %collective-permute-start.9 = (bf16[512,768]{1,0:T(8,128)(2,1)}, bf16[512,768]{1,0:T(8,128)(2,1)}, u32[]{:S(2)}, u32[]{:S(2)}) collective-permute-start(bf16[512,768]{1,0:T(8,128)(2,1)} %get-tuple-element.124), channel_id=1, source_target_pairs={{16,0},{24,8},{0,16},{8,24},{17,1},{25,9},{1,17},{9,25},{18,2},{26... | collective-permute-start | bytes 2359304 | tf_op jit(solution)/shard_map/ppermute | solution.py:213
  208.7 145.6 %all-gather.14.cloned.1.call-start = ((), (), s32[]{:S(2)}) async-start(), calls=%async_computation.3 | async-start | bytes 4718592 | tf_op jit(solution)/shard_map/all_gather | solution.py:297
  208.9 68.3 %collective-permute-start.15 = (bf16[3,2048,256]{2,1,0:T(8,128)(2,1)}, bf16[3,2048,256]{2,1,0:T(8,128)(2,1)S(1)}, u32[]{:S(2)}, u32[]{:S(2)}) collective-permute-start(bf16[3,2048,256]{2,1,0:T(8,128)(2,1)} %get-tuple-element.145.refs_2_.refs_1_), channel_id=1, source_target_pairs={{8,0},{0,8},{24,16},{16,24},{9,1},{1,9},{25,17},{17,25},{10,2},{2,... | collective-permute-start | bytes 9437192 | tf_op jit(solution)/shard_map/ppermute | solution.py:209
  210.7 63.7 %collective-permute-start.16 = (bf16[2048,256]{1,0:T(8,128)(2,1)}, bf16[2048,256]{1,0:T(8,128)(2,1)S(1)}, u32[]{:S(2)}, u32[]{:S(2)}) collective-permute-start(bf16[2048,256]{1,0:T(8,128)(2,1)} %collective-permute-done.2), channel_id=1, source_target_pairs={{16,0},{24,8},{0,16},{8,24},{17,1},{25,9},{1,17},{9,25},{18,2},{26... | collective-permute-start | bytes 3145736 | tf_op jit(solution)/shard_map/ppermute | solution.py:213
  218.3 36.1 %collective-permute-start.13 = (bf16[528,768]{1,0:T(8,128)(2,1)S(1)}, bf16[528,768]{1,0:T(8,128)(2,1)S(1)}, u32[]{:S(2)}, u32[]{:S(2)}) collective-permute-start(bf16[528,768]{1,0:T(8,128)(2,1)S(1)} %get-tuple-element.133), channel_id=1, source_target_pairs={{16,0},{24,8},{0,16},{8,24},{17,1},{25,9},{1,17},{9,25},{18,2},{26... | collective-permute-start | bytes 2433032 | tf_op jit(solution)/shard_map/ppermute | solution.py:213
  226.6 41.1 %collective-permute-start.14 = (bf16[512,768]{1,0:T(8,128)(2,1)S(1)}, bf16[512,768]{1,0:T(8,128)(2,1)S(1)}, u32[]{:S(2)}, u32[]{:S(2)}) collective-permute-start(bf16[512,768]{1,0:T(8,128)(2,1)S(1)} %get-tuple-element.136), channel_id=1, source_target_pairs={{16,0},{24,8},{0,16},{8,24},{17,1},{25,9},{1,17},{9,25},{18,2},{26... | collective-permute-start | bytes 2359304 | tf_op jit(solution)/shard_map/ppermute | solution.py:213
  281.6 125.6 %all-gather.16.cloned.1.call-start = ((), (), s32[]{:S(2)}) async-start(), calls=%async_computation.4 | async-start | bytes 4718592 | tf_op jit(solution)/shard_map/all_gather | solution.py:297
  281.8 67.2 %collective-permute-start.19 = (bf16[3,2048,256]{2,1,0:T(8,128)(2,1)S(1)}, bf16[3,2048,256]{2,1,0:T(8,128)(2,1)S(1)}, u32[]{:S(2)}, u32[]{:S(2)}) collective-permute-start(bf16[3,2048,256]{2,1,0:T(8,128)(2,1)S(1)} %copy-done), channel_id=1, source_target_pairs={{8,0},{0,8},{24,16},{16,24},{9,1},{1,9},{25,17},{17,25},{10,2},{2,... | collective-permute-start | bytes 9437192 | tf_op jit(solution)/shard_map/ppermute | solution.py:209
  283.4 67.3 %collective-permute-start.20 = (bf16[2048,256]{1,0:T(8,128)(2,1)}, bf16[2048,256]{1,0:T(8,128)(2,1)S(1)}, u32[]{:S(2)}, u32[]{:S(2)}) collective-permute-start(bf16[2048,256]{1,0:T(8,128)(2,1)} %collective-permute-done.11), channel_id=1, source_target_pairs={{16,0},{24,8},{0,16},{8,24},{17,1},{25,9},{1,17},{9,25},{18,2},{26... | collective-permute-start | bytes 3145736 | tf_op jit(solution)/shard_map/ppermute | solution.py:213
  292.8 34.3 %collective-permute-start.17 = (bf16[528,768]{1,0:T(8,128)(2,1)S(1)}, bf16[528,768]{1,0:T(8,128)(2,1)S(1)}, u32[]{:S(2)}, u32[]{:S(2)}) collective-permute-start(bf16[528,768]{1,0:T(8,128)(2,1)S(1)} %get-tuple-element.148), channel_id=1, source_target_pairs={{16,0},{24,8},{0,16},{8,24},{17,1},{25,9},{1,17},{9,25},{18,2},{26... | collective-permute-start | bytes 2433032 | tf_op jit(solution)/shard_map/ppermute | solution.py:213
  301.1 38.3 %collective-permute-start.18 = (bf16[512,768]{1,0:T(8,128)(2,1)S(1)}, bf16[512,768]{1,0:T(8,128)(2,1)S(1)}, u32[]{:S(2)}, u32[]{:S(2)}) collective-permute-start(bf16[512,768]{1,0:T(8,128)(2,1)S(1)} %get-tuple-element.151), channel_id=1, source_target_pairs={{16,0},{24,8},{0,16},{8,24},{17,1},{25,9},{1,17},{9,25},{18,2},{26... | collective-permute-start | bytes 2359304 | tf_op jit(solution)/shard_map/ppermute | solution.py:213
  354.3 99.9 %all-gather.18.cloned.1.call-start = ((), (), s32[]{:S(2)}) async-start(), calls=%async_computation.5 | async-start | bytes 4718592 | tf_op jit(solution)/shard_map/all_gather | solution.py:297
  354.6 48.4 %collective-permute-start.23 = (bf16[2048,256]{1,0:T(8,128)(2,1)}, bf16[2048,256]{1,0:T(8,128)(2,1)}, u32[]{:S(2)}, u32[]{:S(2)}) collective-permute-start(bf16[2048,256]{1,0:T(8,128)(2,1)} %get-tuple-element.114), channel_id=1, source_target_pairs={{8,0},{0,8},{24,16},{16,24},{9,1},{1,9},{25,17},{17,25},{10,2},{2,... | collective-permute-start | bytes 3145736 | tf_op jit(solution)/shard_map/ppermute | solution.py:209
  355.9 47.1 %collective-permute-start.24 = (bf16[2048,256]{1,0:T(8,128)(2,1)}, bf16[2048,256]{1,0:T(8,128)(2,1)S(1)}, u32[]{:S(2)}, u32[]{:S(2)}) collective-permute-start(bf16[2048,256]{1,0:T(8,128)(2,1)} %get-tuple-element.127), channel_id=1, source_target_pairs={{8,0},{0,8},{24,16},{16,24},{9,1},{1,9},{25,17},{17,25},{10,2},{2,... | collective-permute-start | bytes 3145736 | tf_op jit(solution)/shard_map/ppermute | solution.py:209
  364.7 21.1 %collective-permute-start.21 = (bf16[528,768]{1,0:T(8,128)(2,1)S(1)}, bf16[528,768]{1,0:T(8,128)(2,1)S(1)}, u32[]{:S(2)}, u32[]{:S(2)}) collective-permute-start(bf16[528,768]{1,0:T(8,128)(2,1)S(1)} %get-tuple-element.163), channel_id=1, source_target_pairs={{16,0},{24,8},{0,16},{8,24},{17,1},{25,9},{1,17},{9,25},{18,2},{26... | collective-permute-start | bytes 2433032 | tf_op jit(solution)/shard_map/ppermute | solution.py:213
  372.1 25.1 %collective-permute-start.22 = (bf16[512,768]{1,0:T(8,128)(2,1)S(1)}, bf16[512,768]{1,0:T(8,128)(2,1)S(1)}, u32[]{:S(2)}, u32[]{:S(2)}) collective-permute-start(bf16[512,768]{1,0:T(8,128)(2,1)S(1)} %get-tuple-element.166), channel_id=1, source_target_pairs={{16,0},{24,8},{0,16},{8,24},{17,1},{25,9},{1,17},{9,25},{18,2},{26... | collective-permute-start | bytes 2359304 | tf_op jit(solution)/shard_map/ppermute | solution.py:213
  407.2 20.4 %collective-permute-start.26 = (bf16[2048,256]{1,0:T(8,128)(2,1)}, bf16[2048,256]{1,0:T(8,128)(2,1)}, u32[]{:S(2)}, u32[]{:S(2)}) collective-permute-start(bf16[2048,256]{1,0:T(8,128)(2,1)} %collective-permute-done.12), channel_id=1, source_target_pairs={{8,0},{0,8},{24,16},{16,24},{9,1},{1,9},{25,17},{17,25},{10,2},{2,... | collective-permute-start | bytes 3145736 | tf_op jit(solution)/shard_map/ppermute | solution.py:209
  408.1 20.4 %collective-permute-start.25 = (bf16[2048,256]{1,0:T(8,128)(2,1)}, bf16[2048,256]{1,0:T(8,128)(2,1)}, u32[]{:S(2)}, u32[]{:S(2)}) collective-permute-start(bf16[2048,256]{1,0:T(8,128)(2,1)} %collective-permute-done.23), channel_id=1, source_target_pairs={{16,0},{24,8},{0,16},{8,24},{17,1},{25,9},{1,17},{9,25},{18,2},{26... | collective-permute-start | bytes 3145736 | tf_op jit(solution)/shard_map/ppermute | solution.py:213
  (31 other events, 149.3 us)
Sparse Core Ops, SparseCore 0:
  46.1 83.3 all-gather.9
  208.8 47.6 all-gather.11
  281.7 47.4 all-gather.13
  354.4 47.3 all-gather.15
  407.3 46.8 all-gather.17

commit v7 on v6

--- a/solution.py
+++ b/solution.py
@@ -250,6 +250,7 @@
     theirs_before = [from_far(columns_of(before, (e - k) % far), k) for k in range(1, far)]
     taps = jnp.concatenate([feat_filter.reshape(feat * 3, chans_here), inner_filter], axis=0)
     rows[1:], theirs_before = together((rows[1:], theirs_before))
+    x_rows, theirs_before = together((x_rows, theirs_before))
     across = [[from_far(block, a) for a in range(1, far)] for block in rows]
     normed, across[0] = together((normalised(x_rows, norm_gain), across[0]))
     mine, across[1] = together((columns_of(normed, e), across[1]))
@@ -278,18 +279,15 @@
         second, _ = project(mine, 1, [], weights[j], sums[1], after=[mark])
         projected = [first, second]
         if j == 0:
-            projected, weights[1], near_rows[1], across[3] = together(
-                (projected, weights[1], near_rows[1], across[3])
-            )
+            projected, weights[1], across[3] = together((projected, weights[1], across[3]))
         elif j == 1:
             diagonal.append(beyond(0))
             projected, weights[2], diagonal[0] = together((projected, weights[2], diagonal[0]))
         elif j == 2:
-            diagonal.append(beyond(1))
-            projected, weights[3], diagonal[1] = together((projected, weights[3], diagonal[1]))
+            projected, weights[3] = together((projected, weights[3]))
         else:
-            projected, near_rows[2:] = together((projected, near_rows[2:]))
-            diagonal += [beyond(2), sideways(3)]
+            projected, near_rows[1:3] = together((projected, near_rows[1:3]))
+            diagonal += [beyond(1), beyond(2), sideways(3)]
         mixed, mark = short_mix(projected, taps[:, cuts[j]], feat, filt)
         done = [mark]
         if j > 0:
@@ -305,7 +303,7 @@
         for a in range(1, far):
             found += [across[m][a - 1]] + diagonal[m][a - 1]
         blocks.append([block.reshape(-1, chans_here, block.shape[1]) for block in found])
-    groups, partial = (blocks[:2], blocks[2:]), []
+    groups, partial = (blocks[:1], blocks[1:2], blocks[2:]), []
     for found in groups:
         if partial:
             partial[-1], found = together((partial[-1], found))

time: 531 us -> 513 us (0.966)
  waiting for transfers between devices: 204 us -> 182 us
    ppermute x17, waiting for transfers between devices: 151 us -> 131 us  [from_far(): return lax.ppermute(block, 'seq', pairs)]
    all_gather x4, waiting for transfers between devices: 12.7 us -> 0.01 us  [per_device(): gated.append(lax.all_gather(mixed, 'chan', axis=0))]
    ppermute x9, waiting for transfers between devices: 21.1 us -> 30 us  [from_near(): return lax.ppermute(block, 'seq', pairs)]
    pallas_call x3 -> x4, Pallas kernels: 31.8 us -> 35.5 us  [out_project(): pl.pallas_call(functools.partial(out_kernel, blocks, columns, len(gated))...]
    unnamed x62 -> x46, local copies, waits for them, and re-layouts: 21.9 us -> 19.7 us
  transfers between devices with their start and end apart: 32 -> 32, of which waited for: 19 -> 17; matrix products, arithmetic and copies ran while one was open for 9% -> 9% of each run, Pallas kernels for 26% -> 27%
where the time goes in v7:
time: 513 us; the launch traced here: 509 us
  waiting for transfers between devices  182 us (35%)
  Pallas kernels  151 us (29%)
  blocking collectives  52.6 us (10%)
  local copies, waits for them, and re-layouts  37.8 us (7%)
  other arithmetic  36.2 us (7%)
  starting transfers between devices  35.6 us (7%)
  between operations  13.7 us (3%)
    ppermute x17, waiting for transfers between devices, from_far(): return lax.ppermute(block, 'seq', pairs)  131 us
    pallas_call x16, Pallas kernels, project(): pl.pallas_call(functools.partial(project_kernel, len(weights), len(receiv...  108 us
    all_to_all x1, blocking collectives, per_device(): lax.all_to_all(out.reshape(chans, share, -1), 'chan', split_axis=0, conca...  52.6 us
    pallas_call x4, Pallas kernels, out_project(): pl.pallas_call(functools.partial(out_kernel, blocks, columns, len(gated))...  35.5 us
    ppermute x9, waiting for transfers between devices, from_near(): return lax.ppermute(block, 'seq', pairs)  30 us
    ppermute x17, starting transfers between devices, from_far(): return lax.ppermute(block, 'seq', pairs)  20 us
    unnamed x46, local copies, waits for them, and re-layouts  19.7 us
    ppermute x1, waiting for transfers between devices, per_device(): lax.ppermute(x_rows[tokens - HALO:], 'seq', [(a, a + 1) for a in range(se...  19.3 us
  transfers between devices with their start and end apart: 32, of which 17 were waited for; matrix products, arithmetic and copies ran while one was open for 9% of the time, Pallas kernels for 27%

profile of v7, /device:TPU:0, one launch (start us, length us, event | category | flops | bytes accessed | tf_op | source)
XLA Modules:
  0.0 508.7 jit_solution(11677259238679126212)
XLA Ops:
  26.7 19.3 %collective-permute-done.1 = bf16[16,8192]{1,0:T(8,128)(2,1)S(1)} collective-permute-done((bf16[16,8192]{1,0:T(8,128)(2,1)S(1)}, bf16[16,8192]{1,0:T(8,128)(2,1)S(1)}, u32[]{:S(2)}, u32[]{:S(2)}) %collective-permute-start.1) | collective-permute-done | bytes 262176 | tf_op jit(solution)/shard_map/ppermute | solution.py:238
  55.7 7.9 %fusion = f32[1024]{0:T(1024)S(1)} fusion(bf16[1024,8192]{1,0:T(8,128)(2,1)} %param.6), kind=kLoop, calls=%fused_computation.2 | loop fusion | flops 25164800 | bytes 16781312 | tf_op jit(solution)/shard_map/reduce_sum | solution.py:193
  63.6 15.3 %fusion.2 = bf16[1024,8192]{1,0:T(8,128)(2,1)} fusion(bf16[1024,8192]{1,0:T(8,128)(2,1)} %param.6, f32[8192]{0:T(1024)S(1)} %copy-done.20, f32[1024]{0:T(1024)S(1)} %add_rsqrt_fusion), kind=kLoop, calls=%fused_computation.4 | loop fusion | flops 33554432 | bytes 33591296 | tf_op jit(solution)/shard_map/convert_element_type | solution.py:194
  83.9 8.6 %constant_dynamic-slice_fusion.3 = (bf16[1024,2048]{1,0:T(8,128)(2,1)}, bf16[1024,2048]{1,0:T(8,128)(2,1)}) fusion(bf16[1024,8192]{1,0:T(8,128)(2,1)} %fusion.2, s32[]{:T(128)S(6)} %select_n.86, s32[]{:T(128)S(6)} %select_n.87), kind=kLoop, calls=%fused_computation.37 | loop fusion | bytes 16777224 | tf_op jit(solution)/shard_map/dynamic_slice | solution.py:218
  92.5 8.0 %pad_maximum_fusion.refs_0_ = bf16[1024,4096]{1,0:T(8,128)(2,1)} fusion(bf16[1024,2048]{1,0:T(8,128)(2,1)} %get-tuple-element.208, bf16[1024,2048]{1,0:T(8,128)(2,1)} %get-tuple-element.207), kind=kLoop, calls=%fused_computation.5 | loop fusion | flops 16777216 | bytes 16777216 | tf_op jit(solution)/shard_map/concatenate | solution.py:216
  105.4 22.5 %collective-permute-done.7 = bf16[2048,256]{1,0:T(8,128)(2,1)} collective-permute-done((bf16[2048,256]{1,0:T(8,128)(2,1)}, bf16[2048,256]{1,0:T(8,128)(2,1)}, u32[]{:S(2)}, u32[]{:S(2)}) %collective-permute-start.7) | collective-permute-done | bytes 1048608 | tf_op jit(solution)/shard_map/ppermute | solution.py:213
  129.5 7.9 %project.16 = (bf16[528,768]{1,0:T(8,128)(2,1)}, f32[8,128]{1,0:T(8,128)S(1)}) custom-call(bf16[1024,4096]{1,0:T(8,128)(2,1)} %all-gather.10.cloned.1.call-done.refs_0_, bf16[16,4096]{1,0:T(8,128)(2,1)S(1)} %collective-permute-done.3.refs_1_, bf16[3,2048,256]{2,1,0:T(8,128)(2,1)S(1)} %slice_bitcast_fusion.3.refs_2_.refs_1_, ...), custom_call_target="tpu_custom_call" | custom-call | flops 1024 | bytes 1024 | tf_op jit(solution)/shard_map/project/pallas_call | solution.py:64
  138.9 7.0 %project.18 = (bf16[512,768]{1,0:T(8,128)(2,1)}, f32[8,128]{1,0:T(8,128)}) custom-call(bf16[1024,4096]{1,0:T(8,128)(2,1)} %all-gather.10.cloned.1.call-done.refs_0_, bf16[3,2048,256]{2,1,0:T(8,128)(2,1)S(1)} %slice_bitcast_fusion.3.refs_2_.refs_1_, bf16[3,2048,256]{2,1,0:T(8,128)(2,1)} %collective-permute-done.4.refs_3_.refs_2_, ...), custom_call_target="tpu_custom_call" | custom-call | flops 1024 | bytes 1024 | tf_op jit(solution)/shard_map/project/pallas_call | solution.py:64
  146.5 21.2 %collective-permute-done.8.refs_4_.refs_5_ = bf16[528,768]{1,0:T(8,128)(2,1)} collective-permute-done((bf16[528,768]{1,0:T(8,128)(2,1)}, bf16[528,768]{1,0:T(8,128)(2,1)}, u32[]{:S(2)}, u32[]{:S(2)}) %collective-permute-start.8) | collective-permute-done | bytes 811040 | tf_op jit(solution)/shard_map/ppermute | solution.py:213
  167.7 7.2 %project.17 = (bf16[528,768]{1,0:T(8,128)(2,1)S(1)}, f32[8,128]{1,0:T(8,128)S(1)}) custom-call(bf16[1024,4096]{1,0:T(8,128)(2,1)} %pad_maximum_fusion.refs_0_, bf16[16,4096]{1,0:T(8,128)(2,1)S(1)} %pad_maximum_fusion.3.refs_1_, bf16[3,2048,256]{2,1,0:T(8,128)(2,1)S(1)} %slice_bitcast_fusion.3.refs_2_.refs_1_, ...), custom_call_target="tpu_custom_call" | custom-call | flops 1024 | bytes 1024 | tf_op jit(solution)/shard_map/project/pallas_call | solution.py:64
  179.7 6.8 %project.19 = (bf16[512,768]{1,0:T(8,128)(2,1)S(1)}, f32[8,128]{1,0:T(8,128)}) custom-call(bf16[1024,4096]{1,0:T(8,128)(2,1)} %pad_maximum_fusion.refs_0_, bf16[3,2048,256]{2,1,0:T(8,128)(2,1)S(1)} %slice_bitcast_fusion.3.refs_2_.refs_1_, bf16[3,2048,256]{2,1,0:T(8,128)(2,1)} %collective-permute-done.4.refs_3_.refs_2_, ...), custom_call_target="tpu_custom_call" | custom-call | flops 1024 | bytes 1024 | tf_op jit(solution)/shard_map/project/pallas_call | solution.py:64
  191.7 7.0 %project.20 = (bf16[528,768]{1,0:T(8,128)(2,1)S(1)}, f32[8,128]{1,0:T(8,128)S(1)}) custom-call(bf16[1024,4096]{1,0:T(8,128)(2,1)} %all-gather.10.cloned.1.call-done.refs_0_, bf16[16,4096]{1,0:T(8,128)(2,1)S(1)} %collective-permute-done.3.refs_1_, bf16[3,2048,256]{2,1,0:T(8,128)(2,1)S(1)} %copy-done.1, ...), custom_call_target="tpu_custom_call" | custom-call | flops 1024 | bytes 1024 | tf_op jit(solution)/shard_map/project/pallas_call | solution.py:64
  200.4 6.7 %project.22 = (bf16[512,768]{1,0:T(8,128)(2,1)S(1)}, f32[8,128]{1,0:T(8,128)}) custom-call(bf16[1024,4096]{1,0:T(8,128)(2,1)} %all-gather.10.cloned.1.call-done.refs_0_, bf16[3,2048,256]{2,1,0:T(8,128)(2,1)S(1)} %copy-done.1, bf16[3,2048,256]{2,1,0:T(8,128)(2,1)} %collective-permute-done.10.refs_3_.refs_2_, f32[8,128]{1,0:T(8,128)S(1)} %get-tuple-element.143.refs_3_), custom_call_target="tpu_custom_call" | custom-call | flops 1024 | bytes 1024 | tf_op jit(solution)/shard_map/project/pallas_call | solution.py:64
  207.5 27.4 %collective-permute-done.12.refs_4_.refs_5_ = bf16[528,768]{1,0:T(8,128)(2,1)S(1)} collective-permute-done((bf16[528,768]{1,0:T(8,128)(2,1)S(1)}, bf16[528,768]{1,0:T(8,128)(2,1)S(1)}, u32[]{:S(2)}, u32[]{:S(2)}) %collective-permute-start.12) | collective-permute-done | bytes 811040 | tf_op jit(solution)/shard_map/ppermute | solution.py:213
  234.9 7.1 %project.21 = (bf16[528,768]{1,0:T(8,128)(2,1)S(1)}, f32[8,128]{1,0:T(8,128)S(1)}) custom-call(bf16[1024,4096]{1,0:T(8,128)(2,1)} %pad_maximum_fusion.refs_0_, bf16[16,4096]{1,0:T(8,128)(2,1)S(1)} %pad_maximum_fusion.3.refs_1_, bf16[3,2048,256]{2,1,0:T(8,128)(2,1)S(1)} %copy-done.1, bf16[3,2048,256]{2,1,0:T(8,128)(2,1)} %collective-permute-done.10.refs_3_.refs_2_, ...), custom_call_target="tpu_custom_call" | custom-call | flops 1024 | bytes 1024 | tf_op jit(solution)/shard_map/project/pallas_call | solution.py:64
  245.6 6.7 %project.23 = (bf16[512,768]{1,0:T(8,128)(2,1)S(1)}, f32[8,128]{1,0:T(8,128)}) custom-call(bf16[1024,4096]{1,0:T(8,128)(2,1)} %pad_maximum_fusion.refs_0_, bf16[3,2048,256]{2,1,0:T(8,128)(2,1)S(1)} %copy-done.1, bf16[3,2048,256]{2,1,0:T(8,128)(2,1)} %collective-permute-done.10.refs_3_.refs_2_, bf16[512,768]{1,0:T(8,128)(2,1)S(1)} %collective-permute-done.13.refs_3_, ...), custom_call_target="tpu_custom_call" | custom-call | flops 1024 | bytes 1024 | tf_op jit(solution)/shard_map/project/pallas_call | solution.py:64
  263.3 7.0 %project.24 = (bf16[528,768]{1,0:T(8,128)(2,1)S(1)}, f32[8,128]{1,0:T(8,128)S(1)}) custom-call(bf16[1024,4096]{1,0:T(8,128)(2,1)} %all-gather.10.cloned.1.call-done.refs_0_, bf16[16,4096]{1,0:T(8,128)(2,1)S(1)} %collective-permute-done.3.refs_1_, bf16[3,2048,256]{2,1,0:T(8,128)(2,1)} %get-tuple-element.153.refs_2_.refs_1_, ...), custom_call_target="tpu_custom_call" | custom-call | flops 1024 | bytes 1024 | tf_op jit(solution)/shard_map/project/pallas_call | solution.py:64
  271.9 6.7 %project.26 = (bf16[512,768]{1,0:T(8,128)(2,1)S(1)}, f32[8,128]{1,0:T(8,128)}) custom-call(bf16[1024,4096]{1,0:T(8,128)(2,1)} %all-gather.10.cloned.1.call-done.refs_0_, bf16[3,2048,256]{2,1,0:T(8,128)(2,1)} %get-tuple-element.153.refs_2_.refs_1_, bf16[3,2048,256]{2,1,0:T(8,128)(2,1)S(1)} %copy-done.5, f32[8,128]{1,0:T(8,128)S(1)} %get-tuple-element.158.refs_3_), custom_call_target="tpu_custom_call" | custom-call | flops 1024 | bytes 1024 | tf_op jit(solution)/shard_map/project/pallas_call | solution.py:64
  279.1 12.3 %collective-permute-done.16.refs_4_.refs_5_ = bf16[528,768]{1,0:T(8,128)(2,1)S(1)} collective-permute-done((bf16[528,768]{1,0:T(8,128)(2,1)S(1)}, bf16[528,768]{1,0:T(8,128)(2,1)S(1)}, u32[]{:S(2)}, u32[]{:S(2)}) %collective-permute-start.16) | collective-permute-done | bytes 811040 | tf_op jit(solution)/shard_map/ppermute | solution.py:213
  291.4 7.1 %project.25 = (bf16[528,768]{1,0:T(8,128)(2,1)S(1)}, f32[8,128]{1,0:T(8,128)S(1)}) custom-call(bf16[1024,4096]{1,0:T(8,128)(2,1)} %pad_maximum_fusion.refs_0_, bf16[16,4096]{1,0:T(8,128)(2,1)S(1)} %pad_maximum_fusion.3.refs_1_, bf16[3,2048,256]{2,1,0:T(8,128)(2,1)} %get-tuple-element.153.refs_2_.refs_1_, bf16[3,2048,256]{2,1,0:T(8,128)(2,1)S(1)} %copy-done.5, ...), custom_call_target="tpu_custom_call" | custom-call | flops 1024 | bytes 1024 | tf_op jit(solution)/shard_map/project/pallas_call | solution.py:64
  301.9 6.8 %project.27 = (bf16[512,768]{1,0:T(8,128)(2,1)S(1)}, f32[8,128]{1,0:T(8,128)}) custom-call(bf16[1024,4096]{1,0:T(8,128)(2,1)} %pad_maximum_fusion.refs_0_, bf16[3,2048,256]{2,1,0:T(8,128)(2,1)} %get-tuple-element.153.refs_2_.refs_1_, bf16[3,2048,256]{2,1,0:T(8,128)(2,1)S(1)} %copy-done.5, bf16[512,768]{1,0:T(8,128)(2,1)S(1)} %collective-permute-done.17.refs_3_, ...), custom_call_target="tpu_custom_call" | custom-call | flops 1024 | bytes 1024 | tf_op jit(solution)/shard_map/project/pallas_call | solution.py:64
  308.7 15.7 %collective-permute-done.18.refs_3_.refs_2_ = bf16[3,2048,256]{2,1,0:T(8,128)(2,1)S(1)} collective-permute-done((bf16[3,2048,256]{2,1,0:T(8,128)(2,1)S(1)}, bf16[3,2048,256]{2,1,0:T(8,128)(2,1)S(1)}, u32[]{:S(2)}, u32[]{:S(2)}) %collective-permute-start.18) | collective-permute-done | bytes 3145760 | tf_op jit(solution)/shard_map/ppermute | solution.py:209
  332.9 6.1 %project.28 = (bf16[528,768]{1,0:T(8,128)(2,1)S(1)}, f32[8,128]{1,0:T(8,128)S(1)}) custom-call(bf16[1024,4096]{1,0:T(8,128)(2,1)} %all-gather.10.cloned.1.call-done.refs_0_, bf16[16,4096]{1,0:T(8,128)(2,1)S(1)} %collective-permute-done.3.refs_1_, bf16[3,2048,256]{2,1,0:T(8,128)(2,1)S(1)} %copy-done, bf16[3,2048,256]{2,1,0:T(8,128)(2,1)S(1)} %copy-done.3, ...), custom_call_target="tpu_custom_call" | custom-call | flops 1024 | bytes 1024 | tf_op jit(solution)/shard_map/project/pallas_call | solution.py:64
  346.9 13.2 %collective-permute-done.19.refs_4_.refs_5_ = bf16[528,768]{1,0:T(8,128)(2,1)S(1)} collective-permute-done((bf16[528,768]{1,0:T(8,128)(2,1)S(1)}, bf16[528,768]{1,0:T(8,128)(2,1)S(1)}, u32[]{:S(2)}, u32[]{:S(2)}) %collective-permute-start.19) | collective-permute-done | bytes 811040 | tf_op jit(solution)/shard_map/ppermute | solution.py:213
  360.1 6.1 %project.29 = (bf16[528,768]{1,0:T(8,128)(2,1)S(1)}, f32[8,128]{1,0:T(8,128)S(1)}) custom-call(bf16[1024,4096]{1,0:T(8,128)(2,1)} %pad_maximum_fusion.refs_0_, bf16[16,4096]{1,0:T(8,128)(2,1)S(1)} %pad_maximum_fusion.3.refs_1_, bf16[3,2048,256]{2,1,0:T(8,128)(2,1)S(1)} %copy-done, bf16[3,2048,256]{2,1,0:T(8,128)(2,1)S(1)} %copy-done.3, ...), custom_call_target="tpu_custom_call" | custom-call | flops 1024 | bytes 1024 | tf_op jit(solution)/shard_map/project/pallas_call | solution.py:64
  387.4 7.0 %out_project.4.refs_17_ = f32[1024,256]{1,0:T(8,128)S(1)} custom-call(s32[4]{0:T(128)S(1)} %pad_add_fusion.order, bf16[8,1024,256]{2,1,0:T(8,128)(2,1)S(1)} %bitcast.37, bf16[8,1024,256]{2,1,0:T(8,128)(2,1)S(1)} %bitcast.40, bf16[8,1024,256]{2,1,0:T(8,128)(2,1)} %bitcast.48, bf16[2,1024,256]{2,1,0:T(8,128)(2,1)} %bitcast.11.refs_3_.refs_1_, ...), custom_call_target="tpu_custom_call" | custom-call | flops 1024 | bytes 1024 | tf_op jit(solution)/shard_map/out_project/pallas_call | solution.py:181
  395.4 9.3 %collective-permute-done.23 = bf16[2048,256]{1,0:T(8,128)(2,1)S(1)} collective-permute-done((bf16[2048,256]{1,0:T(8,128)(2,1)}, bf16[2048,256]{1,0:T(8,128)(2,1)S(1)}, u32[]{:S(2)}, u32[]{:S(2)}) %collective-permute-start.23) | collective-permute-done | bytes 1048608 | tf_op jit(solution)/shard_map/ppermute | solution.py:213
  404.7 7.2 %out_project.5.refs_18_ = f32[1024,256]{1,0:T(8,128)S(1)} custom-call(s32[4]{0:T(128)S(1)} %pad_add_fusion.order, bf16[8,1024,256]{2,1,0:T(8,128)(2,1)S(1)} %bitcast.38, bf16[8,1024,256]{2,1,0:T(8,128)(2,1)S(1)} %bitcast.41, bf16[8,1024,256]{2,1,0:T(8,128)(2,1)} %bitcast.49, bf16[2,1024,256]{2,1,0:T(8,128)(2,1)} %bitcast.15.refs_3_.refs_5_, ...), custom_call_target="tpu_custom_call" | custom-call | flops 1024 | bytes 1024 | tf_op jit(solution)/shard_map/out_project/pallas_call | solution.py:181
  412.9 12.4 %collective-permute-done.26 = bf16[2048,256]{1,0:T(8,128)(2,1)} collective-permute-done((bf16[2048,256]{1,0:T(8,128)(2,1)}, bf16[2048,256]{1,0:T(8,128)(2,1)}, u32[]{:S(2)}, u32[]{:S(2)}) %collective-permute-start.26) | collective-permute-done | bytes 1048608 | tf_op jit(solution)/shard_map/ppermute | solution.py:209
  425.3 11.7 %out_project.6.refs_19_ = f32[1024,512]{1,0:T(8,128)S(1)} custom-call(s32[4]{0:T(128)S(1)} %pad_add_fusion.order, bf16[8,1024,256]{2,1,0:T(8,128)(2,1)} %bitcast.36, bf16[8,1024,256]{2,1,0:T(8,128)(2,1)} %bitcast.39, bf16[8,1024,256]{2,1,0:T(8,128)(2,1)} %bitcast.50, bf16[2,1024,256]{2,1,0:T(8,128)(2,1)} %bitcast.19.refs_3_.refs_9_, ...), custom_call_target="tpu_custom_call" | custom-call | flops 1024 | bytes 1024 | tf_op jit(solution)/shard_map/out_project/pallas_call | solution.py:181
  438.4 9.6 %out_project.7 = bf16[1024,1024]{1,0:T(8,128)(2,1)} custom-call(s32[4]{0:T(128)S(1)} %pad_add_fusion.order, bf16[8,1024,256]{2,1,0:T(8,128)(2,1)} %bitcast.53, bf16[2,1024,256]{2,1,0:T(8,128)(2,1)} %bitcast.11.refs_3_.refs_1_, bf16[2,1024,256]{2,1,0:T(8,128)(2,1)} %bitcast.12.refs_4_.refs_2_, bf16[2,1024,256]{2,1,0:T(8,128)(2,1)S(1)} %bitcast.43, ...), custom_call_target="tpu_custom_call" | custom-call | flops 1024 | bytes 1024 | tf_op jit(solution)/shard_map/out_project/pallas_call | solution.py:181
  448.0 52.6 %all_to_all.5 = bf16[8,128,1024]{2,1,0:T(8,128)(2,1)S(1)} all-to-all(bf16[8,128,1024]{2,1,0:T(8,128)(2,1)} %bitcast.51), channel_id=1, replica_groups=mesh['seq'=4,'chan'=8] {'chan'}, dimensions={0} | all-to-all | bytes 4194304 | tf_op jit(solution)/shard_map/all_to_all | solution.py:313
  (132 shorter events, 117.7 us)
Async XLA Ops:
  6.5 123.0 %all-gather.10.cloned.1.call-start = ((), (), s32[]{:S(2)}) async-start(), calls=%async_computation.1 | async-start | bytes 9437184 | tf_op jit(solution)/shard_map/all_gather | solution.py:248
  11.2 34.8 %collective-permute-start = (bf16[128,4096]{1,0:T(8,128)(2,1)S(1)}, bf16[128,4096]{1,0:T(8,128)(2,1)}, u32[]{:S(2)}, u32[]{:S(2)}) collective-permute-start(bf16[128,4096]{1,0:T(8,128)(2,1)S(1)} %pad_maximum_fusion.1), channel_id=1, source_target_pairs={{16,0},{24,8},{0,16},{8,24},{17,1},{25,9},{1,17},{9,25},{18,2},{26... | collective-permute-start | bytes 3145736 | tf_op jit(solution)/shard_map/ppermute | solution.py:213
  16.4 29.6 %collective-permute-start.2 = (bf16[2048,256]{1,0:T(8,128)(2,1)}, bf16[2048,256]{1,0:T(8,128)(2,1)}, u32[]{:S(2)}, u32[]{:S(2)}) collective-permute-start(bf16[2048,256]{1,0:T(8,128)(2,1)} %get-tuple-element.116), channel_id=1, source_target_pairs={{8,0},{0,8},{24,16},{16,24},{9,1},{1,9},{25,17},{17,25},{10,2},{2,... | collective-permute-start | bytes 3145736 | tf_op jit(solution)/shard_map/ppermute | solution.py:209
  19.0 27.0 %collective-permute-start.1 = (bf16[16,8192]{1,0:T(8,128)(2,1)S(1)}, bf16[16,8192]{1,0:T(8,128)(2,1)S(1)}, u32[]{:S(2)}, u32[]{:S(2)}) collective-permute-start(bf16[16,8192]{1,0:T(8,128)(2,1)S(1)} %slice.39), channel_id=1, source_target_pairs={{0,8},{8,16},{16,24},{1,9},{9,17},{17,25},{2,10},{10,18},{18,26},{... | collective-permute-start | bytes 786440 | tf_op jit(solution)/shard_map/ppermute | solution.py:238
  46.0 213.4 %all-gather.12.cloned.1.call-start = ((), (), s32[]{:S(2)}) async-start(), calls=%async_computation.2 | async-start | bytes 4718592 | tf_op jit(solution)/shard_map/all_gather | solution.py:295
  46.2 81.6 %collective-permute-start.4 = (bf16[3,2048,256]{2,1,0:T(8,128)(2,1)S(1)}, bf16[3,2048,256]{2,1,0:T(8,128)(2,1)}, u32[]{:S(2)}, u32[]{:S(2)}) collective-permute-start(bf16[3,2048,256]{2,1,0:T(8,128)(2,1)S(1)} %slice_bitcast_fusion.3.refs_2_.refs_1_), channel_id=1, source_target_pairs={{8,0},{0,8},{24,16},{16,24},{9,1},{1,9},{25,17},{17,25},{10,2},{2,... | collective-permute-start | bytes 9437192 | tf_op jit(solution)/shard_map/ppermute | solution.py:209
  48.8 137.8 %collective-permute-start.10 = (bf16[3,2048,256]{2,1,0:T(8,128)(2,1)}, bf16[3,2048,256]{2,1,0:T(8,128)(2,1)}, u32[]{:S(2)}, u32[]{:S(2)}) collective-permute-start(bf16[3,2048,256]{2,1,0:T(8,128)(2,1)} %get-tuple-element.136.refs_2_.refs_1_), channel_id=1, source_target_pairs={{8,0},{0,8},{24,16},{16,24},{9,1},{1,9},{25,17},{17,25},{10,2},{2,... | collective-permute-start | bytes 9437192 | tf_op jit(solution)/shard_map/ppermute | solution.py:209
  49.3 6.4 %collective-permute-start.3 = (bf16[16,4096]{1,0:T(8,128)(2,1)S(1)}, bf16[16,4096]{1,0:T(8,128)(2,1)S(1)}, u32[]{:S(2)}, u32[]{:S(2)}) collective-permute-start(bf16[16,4096]{1,0:T(8,128)(2,1)S(1)} %pad_maximum_fusion.2), channel_id=1, source_target_pairs={{16,0},{24,8},{0,16},{8,24},{17,1},{25,9},{1,17},{9,25},{18,2},{26... | collective-permute-start | bytes 393224 | tf_op jit(solution)/shard_map/ppermute | solution.py:213
  51.2 29.8 %collective-permute-start.5 = (bf16[2048,256]{1,0:T(8,128)(2,1)}, bf16[2048,256]{1,0:T(8,128)(2,1)S(1)}, u32[]{:S(2)}, u32[]{:S(2)}) collective-permute-start(bf16[2048,256]{1,0:T(8,128)(2,1)} %get-tuple-element.116), channel_id=1, source_target_pairs={{16,0},{24,8},{0,16},{8,24},{17,1},{25,9},{1,17},{9,25},{18,2},{26... | collective-permute-start | bytes 3145736 | tf_op jit(solution)/shard_map/ppermute | solution.py:213
  79.0 26.4 %collective-permute-start.6 = (bf16[2048,256]{1,0:T(8,128)(2,1)}, bf16[2048,256]{1,0:T(8,128)(2,1)}, u32[]{:S(2)}, u32[]{:S(2)}) collective-permute-start(bf16[2048,256]{1,0:T(8,128)(2,1)} %get-tuple-element.118), channel_id=1, source_target_pairs={{16,0},{24,8},{0,16},{8,24},{17,1},{25,9},{1,17},{9,25},{18,2},{26... | collective-permute-start | bytes 3145736 | tf_op jit(solution)/shard_map/ppermute | solution.py:213
  80.9 46.9 %collective-permute-start.7 = (bf16[2048,256]{1,0:T(8,128)(2,1)}, bf16[2048,256]{1,0:T(8,128)(2,1)}, u32[]{:S(2)}, u32[]{:S(2)}) collective-permute-start(bf16[2048,256]{1,0:T(8,128)(2,1)} %get-tuple-element.122), channel_id=1, source_target_pairs={{16,0},{24,8},{0,16},{8,24},{17,1},{25,9},{1,17},{9,25},{18,2},{26... | collective-permute-start | bytes 3145736 | tf_op jit(solution)/shard_map/ppermute | solution.py:213
  82.0 104.6 %collective-permute-start.11 = (bf16[2048,256]{1,0:T(8,128)(2,1)}, bf16[2048,256]{1,0:T(8,128)(2,1)}, u32[]{:S(2)}, u32[]{:S(2)}) collective-permute-start(bf16[2048,256]{1,0:T(8,128)(2,1)} %get-tuple-element.135), channel_id=1, source_target_pairs={{16,0},{24,8},{0,16},{8,24},{17,1},{25,9},{1,17},{9,25},{18,2},{26... | collective-permute-start | bytes 3145736 | tf_op jit(solution)/shard_map/ppermute | solution.py:213
  137.4 30.3 %collective-permute-start.8 = (bf16[528,768]{1,0:T(8,128)(2,1)}, bf16[528,768]{1,0:T(8,128)(2,1)}, u32[]{:S(2)}, u32[]{:S(2)}) collective-permute-start(bf16[528,768]{1,0:T(8,128)(2,1)} %get-tuple-element.129), channel_id=1, source_target_pairs={{16,0},{24,8},{0,16},{8,24},{17,1},{25,9},{1,17},{9,25},{18,2},{26... | collective-permute-start | bytes 2433032 | tf_op jit(solution)/shard_map/ppermute | solution.py:213
  145.9 33.8 %collective-permute-start.9 = (bf16[512,768]{1,0:T(8,128)(2,1)}, bf16[512,768]{1,0:T(8,128)(2,1)}, u32[]{:S(2)}, u32[]{:S(2)}) collective-permute-start(bf16[512,768]{1,0:T(8,128)(2,1)} %get-tuple-element.132), channel_id=1, source_target_pairs={{16,0},{24,8},{0,16},{8,24},{17,1},{25,9},{1,17},{9,25},{18,2},{26... | collective-permute-start | bytes 2359304 | tf_op jit(solution)/shard_map/ppermute | solution.py:213
  189.3 139.4 %all-gather.14.cloned.1.call-start = ((), (), s32[]{:S(2)}) async-start(), calls=%async_computation.3 | async-start | bytes 4718592 | tf_op jit(solution)/shard_map/all_gather | solution.py:295
  189.5 65.6 %collective-permute-start.14 = (bf16[3,2048,256]{2,1,0:T(8,128)(2,1)}, bf16[3,2048,256]{2,1,0:T(8,128)(2,1)S(1)}, u32[]{:S(2)}, u32[]{:S(2)}) collective-permute-start(bf16[3,2048,256]{2,1,0:T(8,128)(2,1)} %get-tuple-element.153.refs_2_.refs_1_), channel_id=1, source_target_pairs={{8,0},{0,8},{24,16},{16,24},{9,1},{1,9},{25,17},{17,25},{10,2},{2,... | collective-permute-start | bytes 9437192 | tf_op jit(solution)/shard_map/ppermute | solution.py:209
  191.2 61.0 %collective-permute-start.15 = (bf16[2048,256]{1,0:T(8,128)(2,1)}, bf16[2048,256]{1,0:T(8,128)(2,1)S(1)}, u32[]{:S(2)}, u32[]{:S(2)}) collective-permute-start(bf16[2048,256]{1,0:T(8,128)(2,1)} %collective-permute-done.2), channel_id=1, source_target_pairs={{16,0},{24,8},{0,16},{8,24},{17,1},{25,9},{1,17},{9,25},{18,2},{26... | collective-permute-start | bytes 3145736 | tf_op jit(solution)/shard_map/ppermute | solution.py:213
  198.8 36.2 %collective-permute-start.12 = (bf16[528,768]{1,0:T(8,128)(2,1)S(1)}, bf16[528,768]{1,0:T(8,128)(2,1)S(1)}, u32[]{:S(2)}, u32[]{:S(2)}) collective-permute-start(bf16[528,768]{1,0:T(8,128)(2,1)S(1)} %get-tuple-element.141), channel_id=1, source_target_pairs={{16,0},{24,8},{0,16},{8,24},{17,1},{25,9},{1,17},{9,25},{18,2},{26... | collective-permute-start | bytes 2433032 | tf_op jit(solution)/shard_map/ppermute | solution.py:213
  207.1 38.5 %collective-permute-start.13 = (bf16[512,768]{1,0:T(8,128)(2,1)S(1)}, bf16[512,768]{1,0:T(8,128)(2,1)S(1)}, u32[]{:S(2)}, u32[]{:S(2)}) collective-permute-start(bf16[512,768]{1,0:T(8,128)(2,1)S(1)} %get-tuple-element.144), channel_id=1, source_target_pairs={{16,0},{24,8},{0,16},{8,24},{17,1},{25,9},{1,17},{9,25},{18,2},{26... | collective-permute-start | bytes 2359304 | tf_op jit(solution)/shard_map/ppermute | solution.py:213
  259.4 118.8 %all-gather.16.cloned.1.call-start = ((), (), s32[]{:S(2)}) async-start(), calls=%async_computation.4 | async-start | bytes 4718592 | tf_op jit(solution)/shard_map/all_gather | solution.py:295
  259.9 64.4 %collective-permute-start.18 = (bf16[3,2048,256]{2,1,0:T(8,128)(2,1)S(1)}, bf16[3,2048,256]{2,1,0:T(8,128)(2,1)S(1)}, u32[]{:S(2)}, u32[]{:S(2)}) collective-permute-start(bf16[3,2048,256]{2,1,0:T(8,128)(2,1)S(1)} %copy-done), channel_id=1, source_target_pairs={{8,0},{0,8},{24,16},{16,24},{9,1},{1,9},{25,17},{17,25},{10,2},{2,... | collective-permute-start | bytes 9437192 | tf_op jit(solution)/shard_map/ppermute | solution.py:209
  270.3 21.1 %collective-permute-start.16 = (bf16[528,768]{1,0:T(8,128)(2,1)S(1)}, bf16[528,768]{1,0:T(8,128)(2,1)S(1)}, u32[]{:S(2)}, u32[]{:S(2)}) collective-permute-start(bf16[528,768]{1,0:T(8,128)(2,1)S(1)} %get-tuple-element.156), channel_id=1, source_target_pairs={{16,0},{24,8},{0,16},{8,24},{17,1},{25,9},{1,17},{9,25},{18,2},{26... | collective-permute-start | bytes 2433032 | tf_op jit(solution)/shard_map/ppermute | solution.py:213
  278.6 23.3 %collective-permute-start.17 = (bf16[512,768]{1,0:T(8,128)(2,1)S(1)}, bf16[512,768]{1,0:T(8,128)(2,1)S(1)}, u32[]{:S(2)}, u32[]{:S(2)}) collective-permute-start(bf16[512,768]{1,0:T(8,128)(2,1)S(1)} %get-tuple-element.159), channel_id=1, source_target_pairs={{16,0},{24,8},{0,16},{8,24},{17,1},{25,9},{1,17},{9,25},{18,2},{26... | collective-permute-start | bytes 2359304 | tf_op jit(solution)/shard_map/ppermute | solution.py:213
  328.7 109.7 %all-gather.18.cloned.1.call-start = ((), (), s32[]{:S(2)}) async-start(), calls=%async_computation.5 | async-start | bytes 4718592 | tf_op jit(solution)/shard_map/all_gather | solution.py:295
  328.9 46.9 %collective-permute-start.21 = (bf16[2048,256]{1,0:T(8,128)(2,1)}, bf16[2048,256]{1,0:T(8,128)(2,1)}, u32[]{:S(2)}, u32[]{:S(2)}) collective-permute-start(bf16[2048,256]{1,0:T(8,128)(2,1)} %get-tuple-element.118), channel_id=1, source_target_pairs={{8,0},{0,8},{24,16},{16,24},{9,1},{1,9},{25,17},{17,25},{10,2},{2,... | collective-permute-start | bytes 3145736 | tf_op jit(solution)/shard_map/ppermute | solution.py:209
  330.2 45.6 %collective-permute-start.22 = (bf16[2048,256]{1,0:T(8,128)(2,1)}, bf16[2048,256]{1,0:T(8,128)(2,1)}, u32[]{:S(2)}, u32[]{:S(2)}) collective-permute-start(bf16[2048,256]{1,0:T(8,128)(2,1)} %get-tuple-element.122), channel_id=1, source_target_pairs={{8,0},{0,8},{24,16},{16,24},{9,1},{1,9},{25,17},{17,25},{10,2},{2,... | collective-permute-start | bytes 3145736 | tf_op jit(solution)/shard_map/ppermute | solution.py:209
  339.0 21.1 %collective-permute-start.19 = (bf16[528,768]{1,0:T(8,128)(2,1)S(1)}, bf16[528,768]{1,0:T(8,128)(2,1)S(1)}, u32[]{:S(2)}, u32[]{:S(2)}) collective-permute-start(bf16[528,768]{1,0:T(8,128)(2,1)S(1)} %get-tuple-element.170), channel_id=1, source_target_pairs={{16,0},{24,8},{0,16},{8,24},{17,1},{25,9},{1,17},{9,25},{18,2},{26... | collective-permute-start | bytes 2433032 | tf_op jit(solution)/shard_map/ppermute | solution.py:213
  346.8 23.1 %collective-permute-start.20 = (bf16[512,768]{1,0:T(8,128)(2,1)S(1)}, bf16[512,768]{1,0:T(8,128)(2,1)S(1)}, u32[]{:S(2)}, u32[]{:S(2)}) collective-permute-start(bf16[512,768]{1,0:T(8,128)(2,1)S(1)} %get-tuple-element.173), channel_id=1, source_target_pairs={{16,0},{24,8},{0,16},{8,24},{17,1},{25,9},{1,17},{9,25},{18,2},{26... | collective-permute-start | bytes 2359304 | tf_op jit(solution)/shard_map/ppermute | solution.py:213
  378.3 26.4 %collective-permute-start.23 = (bf16[2048,256]{1,0:T(8,128)(2,1)}, bf16[2048,256]{1,0:T(8,128)(2,1)S(1)}, u32[]{:S(2)}, u32[]{:S(2)}) collective-permute-start(bf16[2048,256]{1,0:T(8,128)(2,1)} %collective-permute-done.21), channel_id=1, source_target_pairs={{16,0},{24,8},{0,16},{8,24},{17,1},{25,9},{1,17},{9,25},{18,2},{26... | collective-permute-start | bytes 3145736 | tf_op jit(solution)/shard_map/ppermute | solution.py:213
  380.1 32.8 %collective-permute-start.25 = (bf16[2048,256]{1,0:T(8,128)(2,1)}, bf16[2048,256]{1,0:T(8,128)(2,1)}, u32[]{:S(2)}, u32[]{:S(2)}) collective-permute-start(bf16[2048,256]{1,0:T(8,128)(2,1)} %get-tuple-element.135), channel_id=1, source_target_pairs={{8,0},{0,8},{24,16},{16,24},{9,1},{1,9},{25,17},{17,25},{10,2},{2,... | collective-permute-start | bytes 3145736 | tf_op jit(solution)/shard_map/ppermute | solution.py:209
  381.8 43.6 %collective-permute-start.26 = (bf16[2048,256]{1,0:T(8,128)(2,1)}, bf16[2048,256]{1,0:T(8,128)(2,1)}, u32[]{:S(2)}, u32[]{:S(2)}) collective-permute-start(bf16[2048,256]{1,0:T(8,128)(2,1)} %collective-permute-done.11), channel_id=1, source_target_pairs={{8,0},{0,8},{24,16},{16,24},{9,1},{1,9},{25,17},{17,25},{10,2},{2,... | collective-permute-start | bytes 3145736 | tf_op jit(solution)/shard_map/ppermute | solution.py:209
  382.1 43.2 %collective-permute-start.24 = (bf16[2048,256]{1,0:T(8,128)(2,1)}, bf16[2048,256]{1,0:T(8,128)(2,1)}, u32[]{:S(2)}, u32[]{:S(2)}) collective-permute-start(bf16[2048,256]{1,0:T(8,128)(2,1)} %collective-permute-done.22), channel_id=1, source_target_pairs={{16,0},{24,8},{0,16},{8,24},{17,1},{25,9},{1,17},{9,25},{18,2},{26... | collective-permute-start | bytes 3145736 | tf_op jit(solution)/shard_map/ppermute | solution.py:213
  (23 other events, 104.4 us)
Sparse Core Ops, SparseCore 0:
  46.1 83.3 all-gather.9
  189.4 47.6 all-gather.11
  259.6 47.3 all-gather.13
  328.8 47.1 all-gather.15
  378.4 45.7 all-gather.17
